TPU v7x, 32 devices: a whole 2x2x4 slice. The times are simulated.
32 devices in a mesh: groups: 2 (over x), dap: 16 (over z, y, core).
Axes of the slice: x: 2, y: 2, z: 4, core: 2. Of those that a mesh axis runs over, the one named last changes fastest.
Arguments:
- pair: float32 [128, 64, 128], P(('groups', 'dap')), parts along dimension 0, may hold values from -6 to 6
- residue_mask: int32 [128], P('groups'), parts along dimension 0, may hold values from 0 to 1, as said below
- norm_gain: float32 [2, 2, 128], replicated, may hold values from 0.1 to 1.9
- norm_bias: float32 [2, 2, 128], replicated, may hold values from -3 to 3
- edge_w: bfloat16 [2, 128, 640], replicated, may hold values from -0.5 to 0.5
- edge_bias: float32 [2, 640], replicated, may hold values from -3 to 3
- out_w: bfloat16 [2, 128, 128], replicated, may hold values from -0.5 to 0.5
- out_bias: float32 [2, 128], replicated, may hold values from -3 to 3
Outputs:
- updated: float32 [128, 64, 128], P(('groups', 'dap')), parts along dimension 0
There are 2 independent parts, one for each index of `groups`. A program takes and returns all parts, laid end to end along the dimension named above; an argument that names none is the same for every part. Nothing has to cross between parts.
Inputs may be any that keep to these rules, and one draw needn't show every extreme that they name: `residue_mask`: residues 0 to some count of at least 32 are 1 and all later ones 0.
All inputs are finite; a program needn't handle non-finite values.
Results may differ from a plain program's by a relative error of at most 0.0023.
Values may be sent and summed in bfloat16 or wider, within the bound.
No kernel may reach another device: no remote copies, remote signals or barrier semaphores. Data moves between devices by JAX's collectives and lax.ppermute only.
A program may use at most 128 MiB of HBM per device.

v0:
```python
import jax
import jax.numpy as jnp
from jax import lax
from jax.sharding import PartitionSpec as P


def normalize(values, gain, shift):
    mean = jnp.mean(values, axis=-1, keepdims=True)
    centered = values - mean
    spread = jnp.mean(centered * centered, axis=-1, keepdims=True)
    return centered * lax.rsqrt(spread + 1e-05) * gain + shift


def project(
    block, row_mask, col_mask, norm_gain, norm_bias, edge_w, edge_bias, layer, hidden_width
):
    normed = normalize(block, norm_gain[layer, 0], norm_bias[layer, 0]).astype(jnp.bfloat16)
    projected = (
        jnp.einsum("pqc,ce->pqe", normed, edge_w[layer], preferred_element_type=jnp.float32)
        + edge_bias[layer]
    )
    weight = (row_mask[:, None] * col_mask[None, :])[:, :, None]
    left_edge = (
        weight
        * jax.nn.sigmoid(projected[..., :hidden_width])
        * projected[..., hidden_width : 2 * hidden_width]
    ).astype(jnp.bfloat16)
    right_edge = (
        weight
        * jax.nn.sigmoid(projected[..., 2 * hidden_width : 3 * hidden_width])
        * projected[..., 3 * hidden_width : 4 * hidden_width]
    ).astype(jnp.bfloat16)
    gate_value = jax.nn.sigmoid(projected[..., 4 * hidden_width :])
    return (left_edge, right_edge, gate_value)


def finish(block, contracted, gate_value, norm_gain, norm_bias, out_w, out_bias, layer):
    normed_out = normalize(contracted, norm_gain[layer, 1], norm_bias[layer, 1]).astype(
        jnp.bfloat16
    )
    result = (
        jnp.einsum("pqh,hc->pqc", normed_out, out_w[layer], preferred_element_type=jnp.float32)
        + out_bias[layer]
    )
    return block + gate_value * result


def body(pair, residue_mask, norm_gain, norm_bias, edge_w, edge_bias, out_w, out_bias):
    row_count = pair.shape[0]
    hidden_width = out_w.shape[1]
    offset = lax.axis_index("dap") * row_count
    full_mask = residue_mask.astype(jnp.float32)
    own_mask = lax.dynamic_slice_in_dim(full_mask, offset, row_count, 0)
    left_edge, right_edge, gate_value = project(
        pair, own_mask, full_mask, norm_gain, norm_bias, edge_w, edge_bias, 0, hidden_width
    )
    contracted = jnp.einsum(
        "ikc,jkc->ijc",
        left_edge,
        lax.all_gather(right_edge, "dap", axis=0, tiled=True),
        preferred_element_type=jnp.float32,
    )
    first = finish(pair, contracted, gate_value, norm_gain, norm_bias, out_w, out_bias, 0)
    columns = lax.all_to_all(first, "dap", split_axis=1, concat_axis=0, tiled=True)
    left_cols, right_cols, gate_cols = project(
        columns, full_mask, own_mask, norm_gain, norm_bias, edge_w, edge_bias, 1, hidden_width
    )
    gathered = jnp.einsum(
        "kic,kjc->ijc",
        lax.all_gather(left_cols, "dap", axis=1, tiled=True),
        right_cols,
        preferred_element_type=jnp.float32,
    )
    second = finish(columns, gathered, gate_cols, norm_gain, norm_bias, out_w, out_bias, 1)
    return lax.all_to_all(second, "dap", split_axis=0, concat_axis=1, tiled=True)


def solution(mesh):
    in_specs = (P(("groups", "dap"), None, None), P("groups"), P(), P(), P(), P(), P(), P())
    out_specs = P(("groups", "dap"), None, None)
    return jax.shard_map(body, mesh=mesh, in_specs=in_specs, out_specs=out_specs, check_vma=False)
```

profile of v0, /device:TPU:0, one launch (start us, length us, event | category | flops | bytes accessed | tf_op | source)
XLA Modules:
  0.0 134.3 jit_solution(14030357937542194386)
XLA Ops:
  6.5 0.8 slice_reduce_fusion
  7.3 1.0 reduce_sum.72
  8.4 1.1 multiply_reduce_fusion.3
  9.5 0.7 convert_element_type.31
  10.3 0.8 slice_bitcast_fusion.1
  11.1 1.3 convolution_add_fusion.1
  12.4 0.7 fusion.21
  13.3 40.6 %all-gather.3.cloned.1.call-done = bf16[64,64,128]{2,1,0:T(8,128)(2,1)} async-done(((bf16[4,64,128]{2,1,0:T(8,128)(2,1)}), bf16[64,64,128]{2,1,0:T(8,128)(2,1)}) %all-gather.3.cloned.1.call-update) | async-done | bytes 1048592 | tf_op jit(solution)/shard_map/all_gather | solution.py:60
  53.9 3.9 %copy.28 = bf16[64,64,128]{1,0,2:T(8,128)(2,1)S(1)} copy(bf16[64,64,128]{2,1,0:T(8,128)(2,1)} %all-gather.3.cloned.1.call-done) | data formatting | bytes 2097152 | tf_op jit(solution)/shard_map/all_gather | solution.py:60
  57.9 1.2 fusion.50
  59.5 0.3 fusion.3
  59.8 0.7 copy.31
  60.5 3.6 %all-to-all-start = ((f32[4,64,128]{2,0,1:T(4,128)}), f32[4,64,128]{2,0,1:T(4,128)S(1)}, u32[]{:S(2)}, u32[]{:S(2)}) async-start(f32[4,64,128]{2,0,1:T(4,128)} %copy.31), calls=%async_computation | async-start | bytes 262144 | tf_op jit(solution)/shard_map/all_to_all | solution.py:64
  64.3 7.8 %all-to-all-done = f32[4,64,128]{2,0,1:T(4,128)S(1)} async-done(((f32[4,64,128]{2,0,1:T(4,128)}), f32[4,64,128]{2,0,1:T(4,128)S(1)}, u32[]{:S(2)}, u32[]{:S(2)}) %all-to-all-start) | async-done | bytes 131104 | tf_op jit(solution)/shard_map/all_to_all | solution.py:64
  72.3 0.3 multiply_reduce_fusion.1
  72.6 0.2 add_convert_fusion.1
  72.8 0.2 convolution_add_fusion
  73.0 0.7 fusion.8
  74.0 35.6 %all-gather.5.cloned.1.call-done = bf16[64,64,128]{2,0,1:T(8,128)(2,1)} async-done(((bf16[64,4,128]{2,0,1:T(8,128)(2,1)}), bf16[64,64,128]{2,0,1:T(8,128)(2,1)}) %all-gather.5.cloned.1.call-update) | async-done | bytes 1048592 | tf_op jit(solution)/shard_map/all_gather | solution.py:70
  109.5 3.9 %copy.34 = bf16[64,64,128]{0,1,2:T(8,128)(2,1)S(1)} copy(bf16[64,64,128]{2,0,1:T(8,128)(2,1)} %all-gather.5.cloned.1.call-done) | data formatting | bytes 2097152 | tf_op jit(solution)/shard_map/all_gather | solution.py:70
  113.5 1.2 fusion.51
  115.1 0.3 fusion.1
  115.5 11.4 %all_to_all.36 = f32[64,4,128]{2,1,0:T(4,128)S(1)} all-to-all(f32[64,4,128]{2,1,0:T(4,128)S(1)} %copy.36), channel_id=1, replica_groups=mesh['groups'=2,'dap'=16] {'dap'}, dimensions={0} | all-to-all | bytes 262144 | tf_op jit(solution)/shard_map/all_to_all | solution.py:75
  126.8 0.7 copy.37
  (35 shorter events, 1.8 us)
Async XLA Ops:
  6.5 6.7 %copy-start.2 = (f32[2,128]{1,0:T(2,128)S(1)}, f32[2,128]{1,0:T(2,128)}, u32[]{:S(2)}) copy-start(f32[2,128]{1,0:T(2,128)} %param.15) | copy-start | bytes 3076
  6.5 47.4 %all-gather.3.cloned.1.call-start = ((), (), s32[]{:S(2)}) async-start(), calls=%async_computation.2 | async-start | bytes 1114112 | tf_op jit(solution)/shard_map/all_gather | solution.py:60
  57.9 1.7 %copy-start = (f32[4,64,128]{2,1,0:T(8,128)S(1)}, f32[4,64,128]{2,1,0:T(8,128)}, u32[]{:S(2)}) copy-start(f32[4,64,128]{2,1,0:T(8,128)} %param.8) | copy-start | bytes 393220
  57.9 1.7 %copy-start.3 = (bf16[2,128,128]{2,1,0:T(8,128)(2,1)S(1)}, bf16[2,128,128]{2,1,0:T(8,128)(2,1)}, u32[]{:S(2)}) copy-start(bf16[2,128,128]{2,1,0:T(8,128)(2,1)} %param.14) | copy-start | bytes 196612
  59.0 13.7 %copy-start.1 = (bf16[2,128,640]{2,1,0:T(8,128)(2,1)S(1)}, bf16[2,128,640]{2,1,0:T(8,128)(2,1)}, u32[]{:S(2)}) copy-start(bf16[2,128,640]{2,1,0:T(8,128)(2,1)} %param.12) | copy-start | bytes 983044
  60.5 11.6 %all-to-all-start = ((f32[4,64,128]{2,0,1:T(4,128)}), f32[4,64,128]{2,0,1:T(4,128)S(1)}, u32[]{:S(2)}, u32[]{:S(2)}) async-start(f32[4,64,128]{2,0,1:T(4,128)} %copy.31), calls=%async_computation | async-start | bytes 262144 | tf_op jit(solution)/shard_map/all_to_all | solution.py:64
  64.2 45.3 %all-gather.5.cloned.1.call-start = ((), (), s32[]{:S(2)}) async-start(), calls=%async_computation.3 | async-start | bytes 1114112 | tf_op jit(solution)/shard_map/all_gather | solution.py:70
Sparse Core Ops, SparseCore 0:
  13.2 40.6 all-gather.2
  73.9 35.5 all-gather.4
where the time goes:
time: 135 us; the launch traced here: 134 us
  waiting for transfers between devices  84 us (62%)
  between operations  13.7 us (10%)
  local copies, waits for them, and re-layouts  11.6 us (9%)
  blocking collectives  11.4 us (8%)
  other arithmetic  5.63 us (4%)
  matrix products  4.36 us (3%)
  starting transfers between devices  3.67 us (3%)
    all_gather x1, waiting for transfers between devices, body(): lax.all_gather(right_edge, 'dap', axis=0, tiled=True)  40.6 us
    all_gather x1, waiting for transfers between devices, body(): lax.all_gather(left_cols, 'dap', axis=1, tiled=True)  35.6 us
    all_to_all x1, blocking collectives, body(): lax.all_to_all(second, 'dap', split_axis=0, concat_axis=1, tiled=True)  11.4 us
    all_to_all x1, waiting for transfers between devices, body(): lax.all_to_all(first, 'dap', split_axis=1, concat_axis=0, tiled=True)  7.81 us
    all_gather x1, local copies, waits for them, and re-layouts, body(): lax.all_gather(left_cols, 'dap', axis=1, tiled=True)  3.93 us
    all_gather x1, local copies, waits for them, and re-layouts, body(): lax.all_gather(right_edge, 'dap', axis=0, tiled=True)  3.93 us
    all_to_all x1, starting transfers between devices, body(): lax.all_to_all(first, 'dap', split_axis=1, concat_axis=0, tiled=True)  3.63 us
  transfers between devices with their start and end apart: 3, of which 3 were waited for; matrix products, arithmetic and copies ran while one was open for 0% of the time, Pallas kernels for 0%

commit v1 on v0

v1 whole, which is shorter than its diff:
```python
import functools

import jax
import jax.numpy as jnp
from jax import lax
from jax.experimental import pallas as pl
from jax.experimental.pallas import tpu as pltpu
from jax.sharding import PartitionSpec as P

F32 = jnp.float32
BF16 = jnp.bfloat16
VMEM = pl.BlockSpec(memory_space=pltpu.VMEM)
SMEM = pl.BlockSpec(memory_space=pltpu.SMEM)


def normalize(values, gain, shift):
    mean = jnp.mean(values, axis=-1, keepdims=True)
    centered = values - mean
    spread = jnp.mean(centered * centered, axis=-1, keepdims=True)
    return centered * lax.rsqrt(spread + 1e-05) * gain + shift


def sigmoid(values):
    return 0.5 * jnp.tanh(0.5 * values) + 0.5


def edges(block, rows, first_row, mask_ref, gain_ref, shift_ref, edge_w_ref, edge_bias_ref, layer):
    total, width = block.shape
    side = total // rows
    normed = normalize(block, gain_ref[layer, 0:1, :], shift_ref[layer, 0:1, :]).astype(BF16)
    bias = edge_bias_ref[layer : layer + 1, :]
    hidden = (edge_bias_ref.shape[1] - width) // 4

    def part(index, size):
        low = index * hidden
        return (
            jnp.dot(normed, edge_w_ref[layer, :, low : low + size], preferred_element_type=F32)
            + bias[:, low : low + size]
        )

    valid = jnp.sum(mask_ref[...].astype(F32), axis=1, keepdims=True)
    column = lax.broadcasted_iota(jnp.int32, (rows, side, hidden), 1)
    row = lax.broadcasted_iota(jnp.int32, (rows, side, hidden), 0) + first_row
    keep = (jnp.maximum(column, row).astype(F32) < valid.reshape(1, 1, 1)).reshape(total, hidden)
    left = jnp.where(keep, sigmoid(part(0, hidden)) * part(1, hidden), 0.0)
    right = jnp.where(keep, sigmoid(part(2, hidden)) * part(3, hidden), 0.0)
    return left, right, sigmoid(part(4, width))


def finish(block, contracted, gate, gain_ref, shift_ref, out_w_ref, out_bias_ref, layer):
    normed = normalize(contracted, gain_ref[layer, 1:2, :], shift_ref[layer, 1:2, :]).astype(BF16)
    result = jnp.dot(normed, out_w_ref[layer], preferred_element_type=F32)
    return block + gate * (result + out_bias_ref[layer : layer + 1, :])


def first_kernel(
    at_ref, pair_ref, mask_ref, gain_ref, shift_ref, edge_w_ref, edge_bias_ref,
    send_ref, left_ref, gate_ref,
):
    rows, side, width = pair_ref.shape
    block = pair_ref[...].reshape(rows * side, width)
    left, right, gate = edges(
        block, rows, at_ref[0], mask_ref, gain_ref, shift_ref, edge_w_ref, edge_bias_ref, 0
    )
    right = right.astype(BF16)
    for chip in range(send_ref.shape[0]):
        send_ref[chip] = right
    left_ref[...] = left.astype(BF16)
    gate_ref[...] = gate


def fold(parts, sub):
    shift = 1
    while len(parts) > 1:
        low = (sub & shift) == 0
        parts = [
            jnp.where(low, a, b) + pltpu.roll(jnp.where(low, b, a), shift, 0)
            for a, b in zip(parts[0::2], parts[1::2])
        ]
        shift *= 2
    return parts[0]


def second_kernel(
    at_ref, own_ref, other_ref, left_ref, gate_ref, pair_ref, mask_ref, gain_ref, shift_ref,
    out_w_ref, out_bias_ref, edge_w_ref, edge_bias_ref,
    send_ref, gate_out_ref, first_ref,
    left_scr, x_scr,
):
    rows, side, width = pair_ref.shape
    chips = send_ref.shape[0]
    hidden = left_ref.shape[1]
    left_scr[...] = left_ref[...].astype(F32)
    sub = lax.broadcasted_iota(jnp.int32, (8, hidden), 0)
    core = at_ref[1]

    @pl.loop(0, chips)
    def _(chip):
        totals = [[] for _ in range(rows)]
        for half in (own_ref, other_ref):
            for a in range(rows):
                right = half[chip, a * side : (a + 1) * side, :].astype(F32)
                for i in range(rows):
                    product = left_scr[i * side : (i + 1) * side, :] * right
                    totals[i].append(jnp.sum(product.reshape(side // 8, 8, hidden), axis=0))
        for i in range(rows):
            x = fold(totals[i], sub)
            x = jnp.where(core == 0, x, pltpu.roll(x, rows, 0))
            at = pl.multiple_of(chip * 2 * rows, 2 * rows)
            x_scr[i, pl.ds(at, 2 * rows), :] = x

    block = pair_ref[...].reshape(rows * side, width)
    contracted = x_scr[...].reshape(rows * side, hidden)
    first = finish(
        block, contracted, gate_ref[...], gain_ref, shift_ref, out_w_ref, out_bias_ref, 0
    )
    first_ref[...] = first
    left, right, gate = edges(
        first, rows, at_ref[0], mask_ref, gain_ref, shift_ref, edge_w_ref, edge_bias_ref, 1
    )
    gate_out_ref[...] = gate
    right = right.astype(BF16)
    left = left.reshape(rows, chips, 2 * rows, hidden)
    for chip in range(chips):
        send_ref[chip, 0 : rows * side, :] = right
        send_ref[chip, rows * side :, :] = (
            left[:, chip].reshape(2 * rows * rows, hidden).astype(BF16)
        )


def third_kernel(
    at_ref, own_ref, other_ref, first_ref, gate_ref, gain_ref, shift_ref, out_w_ref, out_bias_ref,
    out_ref, left_scr,
):
    rows, side, width = out_ref.shape
    chips = own_ref.shape[0]
    hidden = own_ref.shape[2]
    core = at_ref[1]
    for h, half in enumerate((own_ref, other_ref)):
        left_scr[h] = half[:, rows * side :, :].astype(F32)

    def step(chip, totals):
        totals = list(totals)
        for h, half in enumerate((own_ref, other_ref)):
            for a in range(rows):
                right = half[chip, a * side : (a + 1) * side, :].astype(F32)
                for i in range(rows):
                    left = left_scr[h, chip, pl.ds(a * 2 * rows + core * rows + i, 1), :]
                    totals[i] = totals[i] + left * right
        return tuple(totals)

    zero = jnp.zeros((side, hidden), F32)
    totals = lax.fori_loop(0, chips, step, (zero,) * rows)
    for i in range(rows):
        here = slice(i * side, (i + 1) * side)
        out_ref[i] = finish(
            first_ref[here, :], totals[i], gate_ref[here, :],
            gain_ref, shift_ref, out_w_ref, out_bias_ref, 1,
        )


def body(pair, residue_mask, norm_gain, norm_bias, edge_w, edge_bias, out_w, out_bias):
    rows, side, width = pair.shape
    hidden = out_w.shape[1]
    dap = lax.axis_size("dap")
    chips = dap // 2
    me = lax.axis_index("dap")
    at = jnp.stack([me * rows, me % 2]).astype(jnp.int32)
    mask = residue_mask.reshape(1, side)
    same_core = [[core + 2 * chip for chip in range(chips)] for core in range(2)]
    flip = [(device, device ^ 1) for device in range(dap)]
    params = pltpu.CompilerParams(vmem_limit_bytes=48 * 1024 * 1024)
    count = rows * side
    shape = jax.ShapeDtypeStruct

    def spread(send):
        block = send.shape[1]
        flat = send.reshape(chips * block, hidden)
        own = lax.all_to_all(flat, "dap", 0, 0, axis_index_groups=same_core, tiled=True)
        other = lax.ppermute(own, "dap", flip)
        return own.reshape(chips, block, hidden), other.reshape(chips, block, hidden)

    send, left, gate = pl.pallas_call(
        first_kernel,
        in_specs=[SMEM, VMEM, VMEM, VMEM, VMEM, VMEM, VMEM],
        out_specs=[VMEM, VMEM, VMEM],
        out_shape=[
            shape((chips, count, hidden), BF16),
            shape((count, hidden), BF16),
            shape((count, width), F32),
        ],
        compiler_params=params,
        name="project_first",
    )(at, pair, mask, norm_gain, norm_bias, edge_w, edge_bias)
    own, other = spread(send)

    send, gate, first = pl.pallas_call(
        second_kernel,
        in_specs=[SMEM] + [VMEM] * 12,
        out_specs=[VMEM, VMEM, VMEM],
        out_shape=[
            shape((chips, count + 2 * rows * rows, hidden), BF16),
            shape((count, width), F32),
            shape((count, width), F32),
        ],
        scratch_shapes=[
            pltpu.VMEM((count, hidden), F32),
            pltpu.VMEM((rows, side, hidden), F32),
        ],
        compiler_params=params,
        name="contract_outgoing",
    )(at, own, other, left, gate, pair, mask, norm_gain, norm_bias, out_w, out_bias, edge_w, edge_bias)
    own, other = spread(send)

    return pl.pallas_call(
        third_kernel,
        in_specs=[SMEM] + [VMEM] * 8,
        out_specs=VMEM,
        out_shape=shape((rows, side, width), F32),
        scratch_shapes=[pltpu.VMEM((2, chips, 2 * rows * rows, hidden), F32)],
        compiler_params=params,
        name="contract_incoming",
    )(at, own, other, first, gate, norm_gain, norm_bias, out_w, out_bias)


def solution(mesh):
    in_specs = (P(("groups", "dap"), None, None), P("groups"), P(), P(), P(), P(), P(), P())
    out_specs = P(("groups", "dap"), None, None)
    return jax.shard_map(body, mesh=mesh, in_specs=in_specs, out_specs=out_specs, check_vma=False)
```

time: 135 us -> 54.8 us (0.41)
  waiting for transfers between devices: 84 us -> 3.91 us
  blocking collectives: 11.4 us -> 42 us
  between operations: 13.7 us -> 0.04 us
  local copies, waits for them, and re-layouts: 11.6 us -> 3.22 us
  other arithmetic: 5.63 us -> 0.07 us
  Pallas kernels: 0 us -> 5.27 us
  matrix products: 4.36 us -> 0 us
  starting transfers between devices: 3.67 us -> 0.01 us
    all_gather x2 -> x0, waiting for transfers between devices: 76.2 us -> none  [the longest x1 40.6 us: body(): lax.all_gather(right_edge, 'dap', axis=0, tiled=True)]
    all_to_all x1 -> x2, blocking collectives: 11.4 us -> 42 us  [spread(): lax.all_to_all(flat, 'dap', 0, 0, axis_index_groups=same_core, tiled=True)]
    all_gather x2 -> x0, local copies, waits for them, and re-layouts: 7.87 us -> none  [the longest x1 3.93 us: body(): lax.all_gather(left_cols, 'dap', axis=1, tiled=True)]
    all_to_all x1 -> x0, waiting for transfers between devices: 7.81 us -> none  [body(): lax.all_to_all(first, 'dap', split_axis=1, concat_axis=0, tiled=True)]
    pallas_call x0 -> x3, Pallas kernels: none -> 5.27 us  [the longest x1 2.22 us: body(): pl.pallas_call(third_kernel, in_specs=[SMEM] + [VMEM] * 8, out_specs=VMEM...]
    dot_general x6 -> x0, matrix products: 4.36 us -> none  [the longest x2 1.51 us: project(): jnp.einsum('pqc,ce->pqe', normed, edge_w[layer], preferred_element_type=j...]
    ppermute x0 -> x2, waiting for transfers between devices: none -> 3.91 us  [spread(): other = lax.ppermute(own, 'dap', flip)]
    all_to_all x1 -> x0, starting transfers between devices: 3.63 us -> none  [body(): lax.all_to_all(first, 'dap', split_axis=1, concat_axis=0, tiled=True)]
  transfers between devices with their start and end apart: 3 -> 2, of which waited for: 3 -> 2; matrix products, arithmetic and copies ran while one was open for 0% -> 0% of each run, Pallas kernels for 0% -> 0%
where the time goes in v1:
time: 54.8 us; the launch traced here: 54.5 us
  blocking collectives  42 us (77%)
  Pallas kernels  5.27 us (10%)
  waiting for transfers between devices  3.91 us (7%)
  local copies, waits for them, and re-layouts  3.22 us (6%)
    all_to_all x2, blocking collectives, spread(): lax.all_to_all(flat, 'dap', 0, 0, axis_index_groups=same_core, tiled=True)  42 us
    ppermute x2, waiting for transfers between devices, spread(): other = lax.ppermute(own, 'dap', flip)  3.91 us
    unnamed x16, local copies, waits for them, and re-layouts  3.22 us
    pallas_call x1, Pallas kernels, body(): pl.pallas_call(third_kernel, in_specs=[SMEM] + [VMEM] * 8, out_specs=VMEM...  2.22 us
    pallas_call x1, Pallas kernels, body(): pl.pallas_call(second_kernel, in_specs=[SMEM] + [VMEM] * 12, out_specs=[V...  2.09 us
  transfers between devices with their start and end apart: 2, of which 2 were waited for; matrix products, arithmetic and copies ran while one was open for 0% of the time, Pallas kernels for 0%

profile of v1, /device:TPU:0, one launch (start us, length us, event | category | flops | bytes accessed | tf_op | source)
XLA Modules:
  0.0 54.5 jit_solution(13549897714693761460)
XLA Ops:
  0.0 0.0 copy-start.3
  0.0 0.0 copy-start.5
  0.0 0.0 copy-start.4
  0.0 0.1 pad_add_fusion.at_ref
  0.1 0.0 copy-start.7
  0.1 0.6 %copy-done.3 = f32[2,640]{1,0:T(2,128)S(1)} copy-done((f32[2,640]{1,0:T(2,128)S(1)}, f32[2,640]{1,0:T(2,128)}, u32[]{:S(2)}) %copy-start.3) | copy-done | bytes 5144
  0.7 0.0 copy-done.5
  0.7 0.0 copy-done.4
  0.7 0.0 copy-done.7
  0.7 0.0 copy-start
  0.7 1.0 %copy-done = bf16[2,128,640]{2,1,0:T(8,128)(2,1)S(1)} copy-done((bf16[2,128,640]{2,1,0:T(8,128)(2,1)S(1)}, bf16[2,128,640]{2,1,0:T(8,128)(2,1)}, u32[]{:S(2)}) %copy-start) | copy-done | bytes 327704
  1.7 0.9 %copy-done.1 = f32[4,64,128]{2,1,0:T(8,128)S(1)} copy-done((f32[4,64,128]{2,1,0:T(8,128)S(1)}, f32[4,64,128]{2,1,0:T(8,128)}, u32[]{:S(2)}) %copy-start.1) | copy-done | bytes 131096
  2.6 1.0 %project_first.1 = (bf16[8,256,128]{2,1,0:T(8,128)(2,1)S(1)}, bf16[256,128]{1,0:T(8,128)(2,1)S(1)}, f32[256,128]{1,0:T(8,128)S(1)}) custom-call(s32[2]{0:T(128)S(1)} %pad_add_fusion.at_ref, f32[4,64,128]{2,1,0:T(8,128)S(1)} %copy-done.1, s32[1,64]{1,0:T(1,128)S(1)} %bitcast.11, f32[2,2,128]{2,1,0:T(2,128)S(1)} %copy-done.4, f32[2,2,128]{2,1,0:T(2,128)S(1)} %copy-done.5, ...), custom_call_target="tpu_custom_call" | custom-call | tf_op jit(solution)/shard_map/project_first/pallas_call | solution.py:183
  3.6 0.0 copy-start.2
  3.6 21.7 %all_to_all.18.own_ref = bf16[8,256,128]{2,1,0:T(8,128)(2,1)S(1)} all-to-all(bf16[8,256,128]{2,1,0:T(8,128)(2,1)S(1)} %get-tuple-element.11), channel_id=1, replica_groups={{0,2,4,6,8,10,12,14},{1,3,5,7,9,11,13,15},{16,18,20,22,24,26,28,30},{17..., dimensions={0} | all-to-all | bytes 1048576 | tf_op jit(solution)/shard_map/all_to_all | solution.py:179
  25.3 0.0 collective-permute-start
  25.3 1.9 %collective-permute-done = bf16[2048,128]{1,0:T(8,128)(2,1)S(1)} collective-permute-done((bf16[2048,128]{1,0:T(8,128)(2,1)S(1)}, bf16[2048,128]{1,0:T(8,128)(2,1)S(1)}, u32[]{:S(2)}, u32[]{:S(2)}) %collective-permute-start) | collective-permute-done | bytes 524320 | tf_op jit(solution)/shard_map/ppermute | solution.py:180
  27.3 0.0 copy-done.2
  27.3 0.7 %copy-done.6 = f32[2,128]{1,0:T(2,128)S(1)} copy-done((f32[2,128]{1,0:T(2,128)S(1)}, f32[2,128]{1,0:T(2,128)}, u32[]{:S(2)}) %copy-start.6) | copy-done | bytes 1048
  27.9 2.1 %contract_outgoing.1 = (bf16[8,288,128]{2,1,0:T(8,128)(2,1)S(1)}, f32[256,128]{1,0:T(8,128)S(1)}, f32[256,128]{1,0:T(8,128)S(1)}) custom-call(s32[2]{0:T(128)S(1)} %pad_add_fusion.at_ref, bf16[8,256,128]{2,1,0:T(8,128)(2,1)S(1)} %all_to_all.18.own_ref, bf16[8,256,128]{2,1,0:T(8,128)(2,1)S(1)} %bitcast.10, bf16[256,128]{1,0:T(8,128)(2,1)S(1)} %get-tuple-element.12.left_ref, ...), custom_call_target="tpu_custom_call" | custom-call | tf_op jit(solution)/shard_map/contract_outgoing/pallas_call | solution.py:197
  30.0 20.2 %all_to_all.19.own_ref = bf16[8,288,128]{2,1,0:T(8,128)(2,1)S(1)} all-to-all(bf16[8,288,128]{2,1,0:T(8,128)(2,1)S(1)} %get-tuple-element.14), channel_id=1, replica_groups={{0,2,4,6,8,10,12,14},{1,3,5,7,9,11,13,15},{16,18,20,22,24,26,28,30},{17..., dimensions={0} | all-to-all | bytes 1179648 | tf_op jit(solution)/shard_map/all_to_all | solution.py:179
  50.2 0.0 collective-permute-start.1
  50.3 2.0 %collective-permute-done.1 = bf16[2304,128]{1,0:T(8,128)(2,1)S(1)} collective-permute-done((bf16[2304,128]{1,0:T(8,128)(2,1)S(1)}, bf16[2304,128]{1,0:T(8,128)(2,1)S(1)}, u32[]{:S(2)}, u32[]{:S(2)}) %collective-permute-start.1) | collective-permute-done | bytes 589856 | tf_op jit(solution)/shard_map/ppermute | solution.py:180
  52.3 2.2 %contract_incoming.1 = f32[4,64,128]{2,1,0:T(8,128)} custom-call(s32[2]{0:T(128)S(1)} %pad_add_fusion.at_ref, bf16[8,288,128]{2,1,0:T(8,128)(2,1)S(1)} %all_to_all.19.own_ref, bf16[8,288,128]{2,1,0:T(8,128)(2,1)S(1)} %bitcast.9, f32[256,128]{1,0:T(8,128)S(1)} %get-tuple-element.15.first_ref, f32[256,128]{1,0:T(8,128)S(1)} %get-tuple-element.16.gate_ref, ...), custom_call_target="tpu_custom_call" | custom-call | tf_op jit(solution)/shard_map/contract_incoming/pallas_call | solution.py:215
  (2 shorter events, 0.0 us)
Async XLA Ops:
  0.0 0.7 %copy-start.3 = (f32[2,640]{1,0:T(2,128)S(1)}, f32[2,640]{1,0:T(2,128)}, u32[]{:S(2)}) copy-start(f32[2,640]{1,0:T(2,128)} %edge_bias_ref.3) | copy-start | bytes 15364
  0.0 0.7 %copy-start.5 = (f32[2,2,128]{2,1,0:T(2,128)S(1)}, f32[2,2,128]{2,1,0:T(2,128)}, u32[]{:S(2)}) copy-start(f32[2,2,128]{2,1,0:T(2,128)} %shift_ref.5) | copy-start | bytes 6148
  0.0 0.7 %copy-start.4 = (f32[2,2,128]{2,1,0:T(2,128)S(1)}, f32[2,2,128]{2,1,0:T(2,128)}, u32[]{:S(2)}) copy-start(f32[2,2,128]{2,1,0:T(2,128)} %gain_ref.5) | copy-start | bytes 6148
  0.1 0.7 %copy-start.7 = (s32[64]{0:T(128)S(1)}, s32[64]{0:T(128)}, u32[]{:S(2)}) copy-start(s32[64]{0:T(128)} %param.9) | copy-start | bytes 772
  0.7 1.0 %copy-start = (bf16[2,128,640]{2,1,0:T(8,128)(2,1)S(1)}, bf16[2,128,640]{2,1,0:T(8,128)(2,1)}, u32[]{:S(2)}) copy-start(bf16[2,128,640]{2,1,0:T(8,128)(2,1)} %edge_w_ref.3) | copy-start | bytes 983044
  1.7 0.9 %copy-start.1 = (f32[4,64,128]{2,1,0:T(8,128)S(1)}, f32[4,64,128]{2,1,0:T(8,128)}, u32[]{:S(2)}) copy-start(f32[4,64,128]{2,1,0:T(8,128)} %pair_ref.3) | copy-start | bytes 393220
  3.6 23.7 %copy-start.2 = (bf16[2,128,128]{2,1,0:T(8,128)(2,1)S(1)}, bf16[2,128,128]{2,1,0:T(8,128)(2,1)}, u32[]{:S(2)}) copy-start(bf16[2,128,128]{2,1,0:T(8,128)(2,1)} %out_w_ref.3) | copy-start | bytes 196612
  25.3 1.9 %collective-permute-start = (bf16[2048,128]{1,0:T(8,128)(2,1)S(1)}, bf16[2048,128]{1,0:T(8,128)(2,1)S(1)}, u32[]{:S(2)}, u32[]{:S(2)}) collective-permute-start(bf16[2048,128]{1,0:T(8,128)(2,1)S(1)} %bitcast.8), channel_id=1, source_target_pairs={{0,1},{1,0},{2,3},{3,2},{4,5},{5,4},{6,7},{7,6},{8,9},{9,8},{10,11... | collective-permute-start | bytes 1572872 | tf_op jit(solution)/shard_map/ppermute | solution.py:180
  27.3 0.7 %copy-start.6 = (f32[2,128]{1,0:T(2,128)S(1)}, f32[2,128]{1,0:T(2,128)}, u32[]{:S(2)}) copy-start(f32[2,128]{1,0:T(2,128)} %out_bias_ref.3) | copy-start | bytes 3076
  50.2 2.0 %collective-permute-start.1 = (bf16[2304,128]{1,0:T(8,128)(2,1)S(1)}, bf16[2304,128]{1,0:T(8,128)(2,1)S(1)}, u32[]{:S(2)}, u32[]{:S(2)}) collective-permute-start(bf16[2304,128]{1,0:T(8,128)(2,1)S(1)} %bitcast.7), channel_id=1, source_target_pairs={{0,1},{1,0},{2,3},{3,2},{4,5},{5,4},{6,7},{7,6},{8,9},{9,8},{10,11... | collective-permute-start | bytes 1769480 | tf_op jit(solution)/shard_map/ppermute | solution.py:180

commit v2 on v1

v2 whole, which is shorter than its diff:
```python
import functools

import jax
import jax.numpy as jnp
from jax import lax
from jax.experimental import pallas as pl
from jax.experimental.pallas import tpu as pltpu
from jax.sharding import PartitionSpec as P

F32 = jnp.float32
BF16 = jnp.bfloat16
VMEM = pl.BlockSpec(memory_space=pltpu.VMEM)
SMEM = pl.BlockSpec(memory_space=pltpu.SMEM)
PLANE = 4
CHUNK = 64


def normalize(values, gain, shift):
    mean = jnp.mean(values, axis=-1, keepdims=True)
    centered = values - mean
    spread = jnp.mean(centered * centered, axis=-1, keepdims=True)
    return centered * lax.rsqrt(spread + 1e-05) * gain + shift


def sigmoid(values):
    return 0.5 * jnp.tanh(0.5 * values) + 0.5


def edges(block, rows, first_row, mask_ref, gain_ref, shift_ref, edge_w_ref, edge_bias_ref, layer):
    total, width = block.shape
    side = total // rows
    normed = normalize(block, gain_ref[layer, 0:1, :], shift_ref[layer, 0:1, :]).astype(BF16)
    bias = edge_bias_ref[layer : layer + 1, :]
    hidden = (edge_bias_ref.shape[1] - width) // 4

    def part(index, size):
        low = index * hidden
        return (
            jnp.dot(normed, edge_w_ref[layer, :, low : low + size], preferred_element_type=F32)
            + bias[:, low : low + size]
        )

    valid = jnp.sum(mask_ref[...].astype(F32), axis=1, keepdims=True)
    column = lax.broadcasted_iota(jnp.int32, (rows, side, hidden), 1)
    row = lax.broadcasted_iota(jnp.int32, (rows, side, hidden), 0) + first_row
    keep = (jnp.maximum(column, row).astype(F32) < valid.reshape(1, 1, 1)).reshape(total, hidden)
    left = jnp.where(keep, sigmoid(part(0, hidden)) * part(1, hidden), 0.0)
    right = jnp.where(keep, sigmoid(part(2, hidden)) * part(3, hidden), 0.0)
    return left, right, sigmoid(part(4, width))


def finish(block, contracted, gate, gain_ref, shift_ref, out_w_ref, out_bias_ref, layer):
    normed = normalize(contracted, gain_ref[layer, 1:2, :], shift_ref[layer, 1:2, :]).astype(BF16)
    result = jnp.dot(normed, out_w_ref[layer], preferred_element_type=F32)
    return block + gate * (result + out_bias_ref[layer : layer + 1, :])


def first_kernel(
    at_ref, pair_ref, mask_ref, gain_ref, shift_ref, edge_w_ref, edge_bias_ref,
    right_ref, left_ref, gate_ref,
):
    rows, side, width = pair_ref.shape
    block = pair_ref[...].reshape(rows * side, width)
    left, right, gate = edges(
        block, rows, at_ref[0] * rows, mask_ref, gain_ref, shift_ref, edge_w_ref, edge_bias_ref, 0
    )
    right_ref[...] = right.astype(BF16)
    left_ref[...] = left
    gate_ref[...] = gate


def fold(parts, sub):
    shift = 1
    while len(parts) > 1:
        low = (sub & shift) == 0
        parts = [
            jnp.where(low, a, b) + pltpu.roll(jnp.where(low, b, a), shift, 0)
            for a, b in zip(parts[0::2], parts[1::2])
        ]
        shift *= 2
    return parts[0]


def row_sums(left_ref, piece_ref, a, rows, side):
    hidden = left_ref.shape[1]

    def chunk(at, totals):
        right = piece_ref[pl.ds(a * side + at, CHUNK), :].astype(F32)
        sums = []
        for i in range(rows):
            product = left_ref[pl.ds(i * side + at, CHUNK), :] * right
            sums.append(jnp.sum(product.reshape(CHUNK // 8, 8, hidden), axis=0))
        return [t + s for t, s in zip(totals, sums)] if totals else sums

    totals = chunk(0, None)
    if side > CHUNK:
        totals = lax.fori_loop(
            1, side // CHUNK, lambda n, t: chunk(pl.multiple_of(n * CHUNK, CHUNK), t), totals
        )
    return totals


def second_kernel(pieces, at_ref, *refs):
    piece_refs = refs[:pieces]
    (
        left_ref, gate_ref, pair_ref, mask_ref, gain_ref, shift_ref,
        out_w_ref, out_bias_ref, edge_w_ref, edge_bias_ref,
    ) = refs[pieces : pieces + 10]
    outs = refs[pieces + 10 :]
    send_refs, (gate_out_ref, first_ref, x_scr, left_scr) = outs[:-4], outs[-4:]
    rows, side, width = pair_ref.shape
    hidden = left_ref.shape[1]
    sub = lax.broadcasted_iota(jnp.int32, (8, hidden), 0)
    me = at_ref[0]
    core = me & 1
    for s in range(0, pieces, 2):
        totals = [[] for _ in range(rows)]
        for piece in piece_refs[s : s + 2]:
            for a in range(rows):
                for i, total in enumerate(row_sums(left_ref, piece, a, rows, side)):
                    totals[i].append(total)
        at = pl.multiple_of((me >> 1 ^ s >> 1) * 2 * rows, 2 * rows)
        for i in range(rows):
            x = fold(totals[i], sub)
            x_scr[i, pl.ds(at, 2 * rows), :] = jnp.where(core == 0, x, pltpu.roll(x, rows, 0))

    block = pair_ref[...].reshape(rows * side, width)
    contracted = x_scr[...].reshape(rows * side, hidden)
    first = finish(
        block, contracted, gate_ref[...], gain_ref, shift_ref, out_w_ref, out_bias_ref, 0
    )
    first_ref[...] = first
    left, right, gate = edges(
        first, rows, me * rows, mask_ref, gain_ref, shift_ref, edge_w_ref, edge_bias_ref, 1
    )
    gate_out_ref[...] = gate
    left_scr[...] = left.reshape(rows, side, hidden)
    right = right.astype(BF16)
    near = PLANE * rows
    for k, send_ref in enumerate(send_refs):
        send_ref[0 : rows * side, :] = right
        at = pl.multiple_of((me // PLANE ^ k) * near, near)
        block = left_scr[:, pl.ds(at, near), :].reshape(rows * near, hidden)
        send_ref[rows * side :, :] = block.astype(BF16)


def third_kernel(pieces, at_ref, *refs):
    piece_refs = refs[:pieces]
    (
        first_ref, gate_ref, gain_ref, shift_ref, out_w_ref, out_bias_ref,
        out_ref, left_scr, x_scr,
    ) = refs[pieces:]
    rows, side, width = out_ref.shape
    hidden = gate_ref.shape[1]
    place = (at_ref[0] % PLANE) * rows
    near = PLANE * rows
    for s, piece in enumerate(piece_refs):
        left_scr[s] = piece[rows * side :, :].astype(F32)

    def columns(at):
        totals = [jnp.zeros((CHUNK, hidden), F32)] * rows
        for s, piece in enumerate(piece_refs):
            for a in range(rows):
                right = piece[pl.ds(a * side + at, CHUNK), :].astype(F32)
                for i in range(rows):
                    left = left_scr[s, pl.ds(a * near + place + i, 1), :]
                    totals[i] = totals[i] + left * right
        for i in range(rows):
            x_scr[i, pl.ds(at, CHUNK), :] = totals[i]

    if side == CHUNK:
        columns(0)
    else:
        pl.loop(0, side // CHUNK)(lambda n: columns(pl.multiple_of(n * CHUNK, CHUNK)))
    out_ref[...] = finish(
        first_ref[...], x_scr[...].reshape(rows * side, hidden), gate_ref[...],
        gain_ref, shift_ref, out_w_ref, out_bias_ref, 1,
    ).reshape(rows, side, width)


def body(pair, residue_mask, norm_gain, norm_bias, edge_w, edge_bias, out_w, out_bias):
    rows, side, width = pair.shape
    hidden = out_w.shape[1]
    dap = lax.axis_size("dap")
    planes = dap // PLANE
    at = lax.axis_index("dap").reshape(1)
    mask = residue_mask.reshape(1, side)
    params = pltpu.CompilerParams(vmem_limit_bytes=48 * 1024 * 1024)
    count = rows * side
    shape = jax.ShapeDtypeStruct

    def swap(piece, bits):
        return lax.ppermute(piece, "dap", [(device, device ^ bits) for device in range(dap)])

    def gather(sends):
        pieces = [None] * dap
        pieces[0] = sends[0]
        pieces[2] = swap(sends[0], 2)
        for k in range(planes - 1, 0, -1):
            pieces[PLANE * k] = swap(sends[k], PLANE * k)
        for k in range(planes - 1, 0, -1):
            pieces[PLANE * k + 2] = swap(pieces[PLANE * k], 2)
        for s in range(0, dap, 2):
            pieces[s + 1] = swap(pieces[s], 1)
        return pieces

    right, left, gate = pl.pallas_call(
        first_kernel,
        in_specs=[SMEM] + [VMEM] * 6,
        out_specs=[VMEM] * 3,
        out_shape=[
            shape((count, hidden), BF16),
            shape((count, hidden), F32),
            shape((count, width), F32),
        ],
        compiler_params=params,
        name="project_first",
    )(at, pair, mask, norm_gain, norm_bias, edge_w, edge_bias)
    pieces = gather([right] * planes)

    *sends, gate, first = pl.pallas_call(
        functools.partial(second_kernel, dap),
        in_specs=[SMEM] + [VMEM] * (dap + 10),
        out_specs=[VMEM] * (planes + 2),
        out_shape=[shape((count + PLANE * rows * rows, hidden), BF16)] * planes
        + [shape((count, width), F32)] * 2,
        scratch_shapes=[pltpu.VMEM((rows, side, hidden), F32)] * 2,
        compiler_params=params,
        name="contract_outgoing",
    )(
        at, *pieces, left, gate, pair, mask, norm_gain, norm_bias,
        out_w, out_bias, edge_w, edge_bias,
    )
    pieces = gather(sends)

    return pl.pallas_call(
        functools.partial(third_kernel, dap),
        in_specs=[SMEM] + [VMEM] * (dap + 6),
        out_specs=VMEM,
        out_shape=shape((rows, side, width), F32),
        scratch_shapes=[
            pltpu.VMEM((dap, PLANE * rows * rows, hidden), F32),
            pltpu.VMEM((rows, side, hidden), F32),
        ],
        compiler_params=params,
        name="contract_incoming",
    )(at, *pieces, first, gate, norm_gain, norm_bias, out_w, out_bias)


def solution(mesh):
    in_specs = (P(("groups", "dap"), None, None), P("groups"), P(), P(), P(), P(), P(), P())
    out_specs = P(("groups", "dap"), None, None)
    return jax.shard_map(body, mesh=mesh, in_specs=in_specs, out_specs=out_specs, check_vma=False)
```

time: 54.8 us -> 44.3 us (0.81)
  blocking collectives: 42 us -> 0 us
  starting transfers between devices: 0.01 us -> 22.7 us
  waiting for transfers between devices: 3.91 us -> 13.7 us
  Pallas kernels: 5.27 us -> 3.56 us
  local copies, waits for them, and re-layouts: 3.22 us -> 3.92 us
    all_to_all x2 -> x0, blocking collectives: 42 us -> none  [spread(): lax.all_to_all(flat, 'dap', 0, 0, axis_index_groups=same_core, tiled=True)]
    ppermute x2 -> x30, starting transfers between devices: 0.01 us -> 22.7 us  [swap(): lax.ppermute(piece, 'dap', [(device, device ^ bits) for device in range(d...]
    ppermute x2 -> x30, waiting for transfers between devices: 3.91 us -> 13.7 us  [swap(): lax.ppermute(piece, 'dap', [(device, device ^ bits) for device in range(d...]
    pallas_call x3, Pallas kernels: 5.27 us -> 3.56 us  [the longest x1 1.7 us: body(): pl.pallas_call(functools.partial(third_kernel, dap), in_specs=[SMEM] + [V...]
    unnamed x16, local copies, waits for them, and re-layouts: 3.22 us -> 3.92 us
  transfers between devices with their start and end apart: 2 -> 30, of which waited for: 2 -> 9; matrix products, arithmetic and copies ran while one was open for 0% -> 0% of each run, Pallas kernels for 0% -> 0%
where the time goes in v2:
time: 44.3 us; the launch traced here: 44 us
  starting transfers between devices  22.7 us (51%)
  waiting for transfers between devices  13.7 us (31%)
  local copies, waits for them, and re-layouts  3.92 us (9%)
  Pallas kernels  3.56 us (8%)
    ppermute x30, starting transfers between devices, swap(): lax.ppermute(piece, 'dap', [(device, device ^ bits) for device in range(d...  22.7 us
    ppermute x30, waiting for transfers between devices, swap(): lax.ppermute(piece, 'dap', [(device, device ^ bits) for device in range(d...  13.7 us
    unnamed x16, local copies, waits for them, and re-layouts  3.92 us
    pallas_call x1, Pallas kernels, body(): pl.pallas_call(functools.partial(third_kernel, dap), in_specs=[SMEM] + [V...  1.7 us
    pallas_call x1, Pallas kernels, body(): pl.pallas_call(functools.partial(second_kernel, dap), in_specs=[SMEM] + [...  1.45 us
  transfers between devices with their start and end apart: 30, of which 9 were waited for; matrix products, arithmetic and copies ran while one was open for 0% of the time, Pallas kernels for 0%

profile of v2, /device:TPU:0, one launch (start us, length us, event | category | flops | bytes accessed | tf_op | source)
XLA Modules:
  0.0 44.0 jit_solution(3435909227830837765)
XLA Ops:
  0.0 0.7 %copy-done.3 = f32[2,640]{1,0:T(2,128)S(1)} copy-done((f32[2,640]{1,0:T(2,128)S(1)}, f32[2,640]{1,0:T(2,128)}, u32[]{:S(2)}) %copy-start.3) | copy-done | bytes 5144
  0.7 1.0 %copy-done = bf16[2,128,640]{2,1,0:T(8,128)(2,1)S(1)} copy-done((bf16[2,128,640]{2,1,0:T(8,128)(2,1)S(1)}, bf16[2,128,640]{2,1,0:T(8,128)(2,1)}, u32[]{:S(2)}) %copy-start) | copy-done | bytes 327704
  1.7 0.9 %copy-done.1 = f32[4,64,128]{2,1,0:T(8,128)S(1)} copy-done((f32[4,64,128]{2,1,0:T(8,128)S(1)}, f32[4,64,128]{2,1,0:T(8,128)}, u32[]{:S(2)}) %copy-start.1) | copy-done | bytes 131096
  3.7 5.1 %collective-permute-start.11 = (bf16[256,128]{1,0:T(8,128)(2,1)S(1)}, bf16[256,128]{1,0:T(8,128)(2,1)S(1)}, u32[]{:S(2)}, u32[]{:S(2)}) collective-permute-start(bf16[256,128]{1,0:T(8,128)(2,1)S(1)} %get-tuple-element.14.refs_0_), channel_id=1, source_target_pairs={{0,12},{1,13},{2,14},{3,15},{4,8},{5,9},{6,10},{7,11},{8,4},{9,5},... | collective-permute-start | bytes 196616 | tf_op jit(solution)/shard_map/ppermute | solution.py:193
  9.4 1.7 %collective-permute-start.1 = (bf16[256,128]{1,0:T(8,128)(2,1)S(1)}, bf16[256,128]{1,0:T(8,128)(2,1)S(1)}, u32[]{:S(2)}, u32[]{:S(2)}) collective-permute-start(bf16[256,128]{1,0:T(8,128)(2,1)S(1)} %get-tuple-element.14.refs_0_), channel_id=1, source_target_pairs={{0,2},{1,3},{2,0},{3,1},{4,6},{5,7},{6,4},{7,5},{8,10},{9,11},{10,... | collective-permute-start | bytes 196616 | tf_op jit(solution)/shard_map/ppermute | solution.py:193
  11.4 1.9 %collective-permute-start.13 = (bf16[256,128]{1,0:T(8,128)(2,1)S(1)}, bf16[256,128]{1,0:T(8,128)(2,1)S(1)}, u32[]{:S(2)}, u32[]{:S(2)}) collective-permute-start(bf16[256,128]{1,0:T(8,128)(2,1)S(1)} %collective-permute-done.11.refs_12_), channel_id=1, source_target_pairs={{0,2},{1,3},{2,0},{3,1},{4,6},{5,7},{6,4},{7,5},{8,10},{9,11},{10,... | collective-permute-start | bytes 196616 | tf_op jit(solution)/shard_map/ppermute | solution.py:193
  13.2 1.1 %collective-permute-done.7.refs_8_ = bf16[256,128]{1,0:T(8,128)(2,1)S(1)} collective-permute-done((bf16[256,128]{1,0:T(8,128)(2,1)S(1)}, bf16[256,128]{1,0:T(8,128)(2,1)S(1)}, u32[]{:S(2)}, u32[]{:S(2)}) %collective-permute-start.7) | collective-permute-done | bytes 65568 | tf_op jit(solution)/shard_map/ppermute | solution.py:193
  14.4 1.5 %collective-permute-start.9 = (bf16[256,128]{1,0:T(8,128)(2,1)S(1)}, bf16[256,128]{1,0:T(8,128)(2,1)S(1)}, u32[]{:S(2)}, u32[]{:S(2)}) collective-permute-start(bf16[256,128]{1,0:T(8,128)(2,1)S(1)} %collective-permute-done.7.refs_8_), channel_id=1, source_target_pairs={{0,2},{1,3},{2,0},{3,1},{4,6},{5,7},{6,4},{7,5},{8,10},{9,11},{10,... | collective-permute-start | bytes 196616 | tf_op jit(solution)/shard_map/ppermute | solution.py:193
  17.2 1.7 %collective-permute-done.9.refs_10_ = bf16[256,128]{1,0:T(8,128)(2,1)S(1)} collective-permute-done((bf16[256,128]{1,0:T(8,128)(2,1)S(1)}, bf16[256,128]{1,0:T(8,128)(2,1)S(1)}, u32[]{:S(2)}, u32[]{:S(2)}) %collective-permute-start.9) | collective-permute-done | bytes 65568 | tf_op jit(solution)/shard_map/ppermute | solution.py:193
  19.4 1.0 %collective-permute-done.5.refs_6_ = bf16[256,128]{1,0:T(8,128)(2,1)S(1)} collective-permute-done((bf16[256,128]{1,0:T(8,128)(2,1)S(1)}, bf16[256,128]{1,0:T(8,128)(2,1)S(1)}, u32[]{:S(2)}, u32[]{:S(2)}) %collective-permute-start.5) | collective-permute-done | bytes 65568 | tf_op jit(solution)/shard_map/ppermute | solution.py:193
  20.5 1.2 %collective-permute-done.6.refs_7_ = bf16[256,128]{1,0:T(8,128)(2,1)S(1)} collective-permute-done((bf16[256,128]{1,0:T(8,128)(2,1)S(1)}, bf16[256,128]{1,0:T(8,128)(2,1)S(1)}, u32[]{:S(2)}, u32[]{:S(2)}) %collective-permute-start.6) | collective-permute-done | bytes 65568 | tf_op jit(solution)/shard_map/ppermute | solution.py:193
  22.4 1.4 %contract_outgoing.1 = (bf16[320,128]{1,0:T(8,128)(2,1)S(1)}, bf16[320,128]{1,0:T(8,128)(2,1)S(1)}, bf16[320,128]{1,0:T(8,128)(2,1)S(1)}, bf16[320,128]{1,0:T(8,...) custom-call(s32[1]{0:T(128)} %bitcast.at_ref, bf16[256,128]{1,0:T(8,128)(2,1)S(1)} %get-tuple-element.14.refs_0_, ...), custom_call_target="tpu_custom_call" | custom-call | tf_op jit(solution)/shard_map/contract_outgoing/pallas_call | solution.py:221
  23.8 1.1 %collective-permute-start.18 = (bf16[320,128]{1,0:T(8,128)(2,1)S(1)}, bf16[320,128]{1,0:T(8,128)(2,1)S(1)}, u32[]{:S(2)}, u32[]{:S(2)}) collective-permute-start(bf16[320,128]{1,0:T(8,128)(2,1)S(1)} %get-tuple-element.18), channel_id=1, source_target_pairs={{0,4},{1,5},{2,6},{3,7},{4,0},{5,1},{6,2},{7,3},{8,12},{9,13},{10,... | collective-permute-start | bytes 245768 | tf_op jit(solution)/shard_map/ppermute | solution.py:193
  25.0 2.2 %collective-permute-start.22 = (bf16[320,128]{1,0:T(8,128)(2,1)S(1)}, bf16[320,128]{1,0:T(8,128)(2,1)S(1)}, u32[]{:S(2)}, u32[]{:S(2)}) collective-permute-start(bf16[320,128]{1,0:T(8,128)(2,1)S(1)} %get-tuple-element.19), channel_id=1, source_target_pairs={{0,8},{1,9},{2,10},{3,11},{4,12},{5,13},{6,14},{7,15},{8,0},{9,1},... | collective-permute-start | bytes 245768 | tf_op jit(solution)/shard_map/ppermute | solution.py:193
  27.2 1.1 %collective-permute-start.26 = (bf16[320,128]{1,0:T(8,128)(2,1)S(1)}, bf16[320,128]{1,0:T(8,128)(2,1)S(1)}, u32[]{:S(2)}, u32[]{:S(2)}) collective-permute-start(bf16[320,128]{1,0:T(8,128)(2,1)S(1)} %get-tuple-element.20), channel_id=1, source_target_pairs={{0,12},{1,13},{2,14},{3,15},{4,8},{5,9},{6,10},{7,11},{8,4},{9,5},... | collective-permute-start | bytes 245768 | tf_op jit(solution)/shard_map/ppermute | solution.py:193
  28.3 1.4 %collective-permute-start.16 = (bf16[320,128]{1,0:T(8,128)(2,1)S(1)}, bf16[320,128]{1,0:T(8,128)(2,1)S(1)}, u32[]{:S(2)}, u32[]{:S(2)}) collective-permute-start(bf16[320,128]{1,0:T(8,128)(2,1)S(1)} %get-tuple-element.17.refs_0_), channel_id=1, source_target_pairs={{0,2},{1,3},{2,0},{3,1},{4,6},{5,7},{6,4},{7,5},{8,10},{9,11},{10,... | collective-permute-start | bytes 245768 | tf_op jit(solution)/shard_map/ppermute | solution.py:193
  29.7 1.0 %collective-permute-start.20 = (bf16[320,128]{1,0:T(8,128)(2,1)S(1)}, bf16[320,128]{1,0:T(8,128)(2,1)S(1)}, u32[]{:S(2)}, u32[]{:S(2)}) collective-permute-start(bf16[320,128]{1,0:T(8,128)(2,1)S(1)} %collective-permute-done.18.refs_4_), channel_id=1, source_target_pairs={{0,2},{1,3},{2,0},{3,1},{4,6},{5,7},{6,4},{7,5},{8,10},{9,11},{10,... | collective-permute-start | bytes 245768 | tf_op jit(solution)/shard_map/ppermute | solution.py:193
  30.7 3.7 %collective-permute-done.22.refs_8_ = bf16[320,128]{1,0:T(8,128)(2,1)S(1)} collective-permute-done((bf16[320,128]{1,0:T(8,128)(2,1)S(1)}, bf16[320,128]{1,0:T(8,128)(2,1)S(1)}, u32[]{:S(2)}, u32[]{:S(2)}) %collective-permute-start.22) | collective-permute-done | bytes 81952 | tf_op jit(solution)/shard_map/ppermute | solution.py:193
  34.5 1.1 %collective-permute-start.24 = (bf16[320,128]{1,0:T(8,128)(2,1)S(1)}, bf16[320,128]{1,0:T(8,128)(2,1)S(1)}, u32[]{:S(2)}, u32[]{:S(2)}) collective-permute-start(bf16[320,128]{1,0:T(8,128)(2,1)S(1)} %collective-permute-done.22.refs_8_), channel_id=1, source_target_pairs={{0,2},{1,3},{2,0},{3,1},{4,6},{5,7},{6,4},{7,5},{8,10},{9,11},{10,... | collective-permute-start | bytes 245768 | tf_op jit(solution)/shard_map/ppermute | solution.py:193
  35.8 0.9 %collective-permute-start.28 = (bf16[320,128]{1,0:T(8,128)(2,1)S(1)}, bf16[320,128]{1,0:T(8,128)(2,1)S(1)}, u32[]{:S(2)}, u32[]{:S(2)}) collective-permute-start(bf16[320,128]{1,0:T(8,128)(2,1)S(1)} %collective-permute-done.26.refs_12_), channel_id=1, source_target_pairs={{0,2},{1,3},{2,0},{3,1},{4,6},{5,7},{6,4},{7,5},{8,10},{9,11},{10,... | collective-permute-start | bytes 245768 | tf_op jit(solution)/shard_map/ppermute | solution.py:193
  37.2 2.5 %collective-permute-done.24.refs_10_ = bf16[320,128]{1,0:T(8,128)(2,1)S(1)} collective-permute-done((bf16[320,128]{1,0:T(8,128)(2,1)S(1)}, bf16[320,128]{1,0:T(8,128)(2,1)S(1)}, u32[]{:S(2)}, u32[]{:S(2)}) %collective-permute-start.24) | collective-permute-done | bytes 81952 | tf_op jit(solution)/shard_map/ppermute | solution.py:193
  40.2 0.9 %collective-permute-done.28.refs_14_ = bf16[320,128]{1,0:T(8,128)(2,1)S(1)} collective-permute-done((bf16[320,128]{1,0:T(8,128)(2,1)S(1)}, bf16[320,128]{1,0:T(8,128)(2,1)S(1)}, u32[]{:S(2)}, u32[]{:S(2)}) %collective-permute-start.28) | collective-permute-done | bytes 81952 | tf_op jit(solution)/shard_map/ppermute | solution.py:193
  41.1 1.2 %collective-permute-done.29.refs_15_ = bf16[320,128]{1,0:T(8,128)(2,1)S(1)} collective-permute-done((bf16[320,128]{1,0:T(8,128)(2,1)S(1)}, bf16[320,128]{1,0:T(8,128)(2,1)S(1)}, u32[]{:S(2)}, u32[]{:S(2)}) %collective-permute-start.29) | collective-permute-done | bytes 81952 | tf_op jit(solution)/shard_map/ppermute | solution.py:193
  42.3 1.7 %contract_incoming.1 = f32[4,64,128]{2,1,0:T(8,128)} custom-call(s32[1]{0:T(128)} %bitcast.at_ref, bf16[320,128]{1,0:T(8,128)(2,1)S(1)} %get-tuple-element.17.refs_0_, bf16[320,128]{1,0:T(8,128)(2,1)S(1)} %collective-permute-done.15.refs_1_, bf16[320,128]{1,0:T(8,128)(2,1)S(1)} %collective-permute-done.16.refs_2_, ...), custom_call_target="tpu_custom_call" | custom-call | tf_op jit(solution)/shard_map/contract_incoming/pallas_call | solution.py:236
  (55 shorter events, 5.8 us)
Async XLA Ops:
  3.7 7.7 %collective-permute-start.11 = (bf16[256,128]{1,0:T(8,128)(2,1)S(1)}, bf16[256,128]{1,0:T(8,128)(2,1)S(1)}, u32[]{:S(2)}, u32[]{:S(2)}) collective-permute-start(bf16[256,128]{1,0:T(8,128)(2,1)S(1)} %get-tuple-element.14.refs_0_), channel_id=1, source_target_pairs={{0,12},{1,13},{2,14},{3,15},{4,8},{5,9},{6,10},{7,11},{8,4},{9,5},... | collective-permute-start | bytes 196616 | tf_op jit(solution)/shard_map/ppermute | solution.py:193
  8.8 5.6 %collective-permute-start.7 = (bf16[256,128]{1,0:T(8,128)(2,1)S(1)}, bf16[256,128]{1,0:T(8,128)(2,1)S(1)}, u32[]{:S(2)}, u32[]{:S(2)}) collective-permute-start(bf16[256,128]{1,0:T(8,128)(2,1)S(1)} %get-tuple-element.14.refs_0_), channel_id=1, source_target_pairs={{0,8},{1,9},{2,10},{3,11},{4,12},{5,13},{6,14},{7,15},{8,0},{9,1},... | collective-permute-start | bytes 196616 | tf_op jit(solution)/shard_map/ppermute | solution.py:193
  8.8 5.6 %collective-permute-start.3 = (bf16[256,128]{1,0:T(8,128)(2,1)S(1)}, bf16[256,128]{1,0:T(8,128)(2,1)S(1)}, u32[]{:S(2)}, u32[]{:S(2)}) collective-permute-start(bf16[256,128]{1,0:T(8,128)(2,1)S(1)} %get-tuple-element.14.refs_0_), channel_id=1, source_target_pairs={{0,4},{1,5},{2,6},{3,7},{4,0},{5,1},{6,2},{7,3},{8,12},{9,13},{10,... | collective-permute-start | bytes 196616 | tf_op jit(solution)/shard_map/ppermute | solution.py:193
  9.4 6.5 %collective-permute-start.1 = (bf16[256,128]{1,0:T(8,128)(2,1)S(1)}, bf16[256,128]{1,0:T(8,128)(2,1)S(1)}, u32[]{:S(2)}, u32[]{:S(2)}) collective-permute-start(bf16[256,128]{1,0:T(8,128)(2,1)S(1)} %get-tuple-element.14.refs_0_), channel_id=1, source_target_pairs={{0,2},{1,3},{2,0},{3,1},{4,6},{5,7},{6,4},{7,5},{8,10},{9,11},{10,... | collective-permute-start | bytes 196616 | tf_op jit(solution)/shard_map/ppermute | solution.py:193
  11.1 5.1 %collective-permute-start = (bf16[256,128]{1,0:T(8,128)(2,1)S(1)}, bf16[256,128]{1,0:T(8,128)(2,1)S(1)}, u32[]{:S(2)}, u32[]{:S(2)}) collective-permute-start(bf16[256,128]{1,0:T(8,128)(2,1)S(1)} %get-tuple-element.14.refs_0_), channel_id=1, source_target_pairs={{0,1},{1,0},{2,3},{3,2},{4,5},{5,4},{6,7},{7,6},{8,9},{9,8},{10,11... | collective-permute-start | bytes 196616 | tf_op jit(solution)/shard_map/ppermute | solution.py:193
  11.4 5.3 %collective-permute-start.13 = (bf16[256,128]{1,0:T(8,128)(2,1)S(1)}, bf16[256,128]{1,0:T(8,128)(2,1)S(1)}, u32[]{:S(2)}, u32[]{:S(2)}) collective-permute-start(bf16[256,128]{1,0:T(8,128)(2,1)S(1)} %collective-permute-done.11.refs_12_), channel_id=1, source_target_pairs={{0,2},{1,3},{2,0},{3,1},{4,6},{5,7},{6,4},{7,5},{8,10},{9,11},{10,... | collective-permute-start | bytes 196616 | tf_op jit(solution)/shard_map/ppermute | solution.py:193
  14.4 2.3 %collective-permute-start.12 = (bf16[256,128]{1,0:T(8,128)(2,1)S(1)}, bf16[256,128]{1,0:T(8,128)(2,1)S(1)}, u32[]{:S(2)}, u32[]{:S(2)}) collective-permute-start(bf16[256,128]{1,0:T(8,128)(2,1)S(1)} %collective-permute-done.11.refs_12_), channel_id=1, source_target_pairs={{0,1},{1,0},{2,3},{3,2},{4,5},{5,4},{6,7},{7,6},{8,9},{9,8},{10,11... | collective-permute-start | bytes 196616 | tf_op jit(solution)/shard_map/ppermute | solution.py:193
  14.4 4.5 %collective-permute-start.9 = (bf16[256,128]{1,0:T(8,128)(2,1)S(1)}, bf16[256,128]{1,0:T(8,128)(2,1)S(1)}, u32[]{:S(2)}, u32[]{:S(2)}) collective-permute-start(bf16[256,128]{1,0:T(8,128)(2,1)S(1)} %collective-permute-done.7.refs_8_), channel_id=1, source_target_pairs={{0,2},{1,3},{2,0},{3,1},{4,6},{5,7},{6,4},{7,5},{8,10},{9,11},{10,... | collective-permute-start | bytes 196616 | tf_op jit(solution)/shard_map/ppermute | solution.py:193
  15.9 3.0 %collective-permute-start.8 = (bf16[256,128]{1,0:T(8,128)(2,1)S(1)}, bf16[256,128]{1,0:T(8,128)(2,1)S(1)}, u32[]{:S(2)}, u32[]{:S(2)}) collective-permute-start(bf16[256,128]{1,0:T(8,128)(2,1)S(1)} %collective-permute-done.7.refs_8_), channel_id=1, source_target_pairs={{0,1},{1,0},{2,3},{3,2},{4,5},{5,4},{6,7},{7,6},{8,9},{9,8},{10,11... | collective-permute-start | bytes 196616 | tf_op jit(solution)/shard_map/ppermute | solution.py:193
  16.1 4.3 %collective-permute-start.5 = (bf16[256,128]{1,0:T(8,128)(2,1)S(1)}, bf16[256,128]{1,0:T(8,128)(2,1)S(1)}, u32[]{:S(2)}, u32[]{:S(2)}) collective-permute-start(bf16[256,128]{1,0:T(8,128)(2,1)S(1)} %collective-permute-done.3.refs_4_), channel_id=1, source_target_pairs={{0,2},{1,3},{2,0},{3,1},{4,6},{5,7},{6,4},{7,5},{8,10},{9,11},{10,... | collective-permute-start | bytes 196616 | tf_op jit(solution)/shard_map/ppermute | solution.py:193
  16.7 3.8 %collective-permute-start.4 = (bf16[256,128]{1,0:T(8,128)(2,1)S(1)}, bf16[256,128]{1,0:T(8,128)(2,1)S(1)}, u32[]{:S(2)}, u32[]{:S(2)}) collective-permute-start(bf16[256,128]{1,0:T(8,128)(2,1)S(1)} %collective-permute-done.3.refs_4_), channel_id=1, source_target_pairs={{0,1},{1,0},{2,3},{3,2},{4,5},{5,4},{6,7},{7,6},{8,9},{9,8},{10,11... | collective-permute-start | bytes 196616 | tf_op jit(solution)/shard_map/ppermute | solution.py:193
  16.7 3.8 %collective-permute-start.2 = (bf16[256,128]{1,0:T(8,128)(2,1)S(1)}, bf16[256,128]{1,0:T(8,128)(2,1)S(1)}, u32[]{:S(2)}, u32[]{:S(2)}) collective-permute-start(bf16[256,128]{1,0:T(8,128)(2,1)S(1)} %collective-permute-done.1.refs_2_), channel_id=1, source_target_pairs={{0,1},{1,0},{2,3},{3,2},{4,5},{5,4},{6,7},{7,6},{8,9},{9,8},{10,11... | collective-permute-start | bytes 196616 | tf_op jit(solution)/shard_map/ppermute | solution.py:193
  23.8 5.9 %collective-permute-start.18 = (bf16[320,128]{1,0:T(8,128)(2,1)S(1)}, bf16[320,128]{1,0:T(8,128)(2,1)S(1)}, u32[]{:S(2)}, u32[]{:S(2)}) collective-permute-start(bf16[320,128]{1,0:T(8,128)(2,1)S(1)} %get-tuple-element.18), channel_id=1, source_target_pairs={{0,4},{1,5},{2,6},{3,7},{4,0},{5,1},{6,2},{7,3},{8,12},{9,13},{10,... | collective-permute-start | bytes 245768 | tf_op jit(solution)/shard_map/ppermute | solution.py:193
  25.0 9.5 %collective-permute-start.22 = (bf16[320,128]{1,0:T(8,128)(2,1)S(1)}, bf16[320,128]{1,0:T(8,128)(2,1)S(1)}, u32[]{:S(2)}, u32[]{:S(2)}) collective-permute-start(bf16[320,128]{1,0:T(8,128)(2,1)S(1)} %get-tuple-element.19), channel_id=1, source_target_pairs={{0,8},{1,9},{2,10},{3,11},{4,12},{5,13},{6,14},{7,15},{8,0},{9,1},... | collective-permute-start | bytes 245768 | tf_op jit(solution)/shard_map/ppermute | solution.py:193
  27.2 7.3 %collective-permute-start.26 = (bf16[320,128]{1,0:T(8,128)(2,1)S(1)}, bf16[320,128]{1,0:T(8,128)(2,1)S(1)}, u32[]{:S(2)}, u32[]{:S(2)}) collective-permute-start(bf16[320,128]{1,0:T(8,128)(2,1)S(1)} %get-tuple-element.20), channel_id=1, source_target_pairs={{0,12},{1,13},{2,14},{3,15},{4,8},{5,9},{6,10},{7,11},{8,4},{9,5},... | collective-permute-start | bytes 245768 | tf_op jit(solution)/shard_map/ppermute | solution.py:193
  28.3 7.3 %collective-permute-start.16 = (bf16[320,128]{1,0:T(8,128)(2,1)S(1)}, bf16[320,128]{1,0:T(8,128)(2,1)S(1)}, u32[]{:S(2)}, u32[]{:S(2)}) collective-permute-start(bf16[320,128]{1,0:T(8,128)(2,1)S(1)} %get-tuple-element.17.refs_0_), channel_id=1, source_target_pairs={{0,2},{1,3},{2,0},{3,1},{4,6},{5,7},{6,4},{7,5},{8,10},{9,11},{10,... | collective-permute-start | bytes 245768 | tf_op jit(solution)/shard_map/ppermute | solution.py:193
  29.7 6.2 %collective-permute-start.15 = (bf16[320,128]{1,0:T(8,128)(2,1)S(1)}, bf16[320,128]{1,0:T(8,128)(2,1)S(1)}, u32[]{:S(2)}, u32[]{:S(2)}) collective-permute-start(bf16[320,128]{1,0:T(8,128)(2,1)S(1)} %get-tuple-element.17.refs_0_), channel_id=1, source_target_pairs={{0,1},{1,0},{2,3},{3,2},{4,5},{5,4},{6,7},{7,6},{8,9},{9,8},{10,11... | collective-permute-start | bytes 245768 | tf_op jit(solution)/shard_map/ppermute | solution.py:193
  29.7 7.0 %collective-permute-start.20 = (bf16[320,128]{1,0:T(8,128)(2,1)S(1)}, bf16[320,128]{1,0:T(8,128)(2,1)S(1)}, u32[]{:S(2)}, u32[]{:S(2)}) collective-permute-start(bf16[320,128]{1,0:T(8,128)(2,1)S(1)} %collective-permute-done.18.refs_4_), channel_id=1, source_target_pairs={{0,2},{1,3},{2,0},{3,1},{4,6},{5,7},{6,4},{7,5},{8,10},{9,11},{10,... | collective-permute-start | bytes 245768 | tf_op jit(solution)/shard_map/ppermute | solution.py:193
  34.4 2.3 %collective-permute-start.19 = (bf16[320,128]{1,0:T(8,128)(2,1)S(1)}, bf16[320,128]{1,0:T(8,128)(2,1)S(1)}, u32[]{:S(2)}, u32[]{:S(2)}) collective-permute-start(bf16[320,128]{1,0:T(8,128)(2,1)S(1)} %collective-permute-done.18.refs_4_), channel_id=1, source_target_pairs={{0,1},{1,0},{2,3},{3,2},{4,5},{5,4},{6,7},{7,6},{8,9},{9,8},{10,11... | collective-permute-start | bytes 245768 | tf_op jit(solution)/shard_map/ppermute | solution.py:193
  34.5 5.2 %collective-permute-start.24 = (bf16[320,128]{1,0:T(8,128)(2,1)S(1)}, bf16[320,128]{1,0:T(8,128)(2,1)S(1)}, u32[]{:S(2)}, u32[]{:S(2)}) collective-permute-start(bf16[320,128]{1,0:T(8,128)(2,1)S(1)} %collective-permute-done.22.refs_8_), channel_id=1, source_target_pairs={{0,2},{1,3},{2,0},{3,1},{4,6},{5,7},{6,4},{7,5},{8,10},{9,11},{10,... | collective-permute-start | bytes 245768 | tf_op jit(solution)/shard_map/ppermute | solution.py:193
  35.6 4.1 %collective-permute-start.23 = (bf16[320,128]{1,0:T(8,128)(2,1)S(1)}, bf16[320,128]{1,0:T(8,128)(2,1)S(1)}, u32[]{:S(2)}, u32[]{:S(2)}) collective-permute-start(bf16[320,128]{1,0:T(8,128)(2,1)S(1)} %collective-permute-done.22.refs_8_), channel_id=1, source_target_pairs={{0,1},{1,0},{2,3},{3,2},{4,5},{5,4},{6,7},{7,6},{8,9},{9,8},{10,11... | collective-permute-start | bytes 245768 | tf_op jit(solution)/shard_map/ppermute | solution.py:193
  35.8 5.2 %collective-permute-start.28 = (bf16[320,128]{1,0:T(8,128)(2,1)S(1)}, bf16[320,128]{1,0:T(8,128)(2,1)S(1)}, u32[]{:S(2)}, u32[]{:S(2)}) collective-permute-start(bf16[320,128]{1,0:T(8,128)(2,1)S(1)} %collective-permute-done.26.refs_12_), channel_id=1, source_target_pairs={{0,2},{1,3},{2,0},{3,1},{4,6},{5,7},{6,4},{7,5},{8,10},{9,11},{10,... | collective-permute-start | bytes 245768 | tf_op jit(solution)/shard_map/ppermute | solution.py:193
  36.7 4.4 %collective-permute-start.27 = (bf16[320,128]{1,0:T(8,128)(2,1)S(1)}, bf16[320,128]{1,0:T(8,128)(2,1)S(1)}, u32[]{:S(2)}, u32[]{:S(2)}) collective-permute-start(bf16[320,128]{1,0:T(8,128)(2,1)S(1)} %collective-permute-done.26.refs_12_), channel_id=1, source_target_pairs={{0,1},{1,0},{2,3},{3,2},{4,5},{5,4},{6,7},{7,6},{8,9},{9,8},{10,11... | collective-permute-start | bytes 245768 | tf_op jit(solution)/shard_map/ppermute | solution.py:193
  36.7 4.3 %collective-permute-start.17 = (bf16[320,128]{1,0:T(8,128)(2,1)S(1)}, bf16[320,128]{1,0:T(8,128)(2,1)S(1)}, u32[]{:S(2)}, u32[]{:S(2)}) collective-permute-start(bf16[320,128]{1,0:T(8,128)(2,1)S(1)} %collective-permute-done.16.refs_2_), channel_id=1, source_target_pairs={{0,1},{1,0},{2,3},{3,2},{4,5},{5,4},{6,7},{7,6},{8,9},{9,8},{10,11... | collective-permute-start | bytes 245768 | tf_op jit(solution)/shard_map/ppermute | solution.py:193
  (14 other events, 32.2 us)

commit v3 on v0

v3 whole, which is shorter than its diff:
```python
import functools

import jax
import jax.numpy as jnp
from jax import lax
from jax.experimental import pallas as pl
from jax.experimental.pallas import tpu as pltpu
from jax.sharding import PartitionSpec as P

F32 = jnp.float32
BF16 = jnp.bfloat16
VMEM = pl.BlockSpec(memory_space=pltpu.VMEM)
SMEM = pl.BlockSpec(memory_space=pltpu.SMEM)
PLANE = 4
CHUNK = 64
BLOCK = 256
PARAMS = pltpu.CompilerParams(vmem_limit_bytes=48 * 1024 * 1024)


def normalize(values, gain, shift):
    mean = jnp.mean(values, axis=-1, keepdims=True)
    centered = values - mean
    spread = jnp.mean(centered * centered, axis=-1, keepdims=True)
    return centered * lax.rsqrt(spread + 1e-05) * gain + shift


def sigmoid(values):
    return 0.5 * jnp.tanh(0.5 * values) + 0.5


def gated(normed, edge_w_ref, edge_bias_ref, layer, index, hidden):
    span = slice(index * hidden, (index + 2) * hidden)
    both = jnp.dot(normed, edge_w_ref[layer, :, span], preferred_element_type=F32)
    both = both + edge_bias_ref[layer : layer + 1, span]
    return sigmoid(both[:, :hidden]) * both[:, hidden:]


def masked(values, row, column, mask_ref):
    valid = jnp.sum(mask_ref[...].astype(F32), axis=1, keepdims=True)
    return jnp.where(jnp.maximum(row, column).astype(F32) < valid, values, 0.0)


def edges(normed_ref, out_ref, first_row, side, mask_ref, edge_w_ref, edge_bias_ref, layer, index):
    count, hidden = normed_ref.shape[0], out_ref.shape[1]
    size = min(count, BLOCK)

    def block(at):
        values = gated(
            normed_ref[pl.ds(at, size), :], edge_w_ref, edge_bias_ref, layer, index, hidden
        )
        position = at + lax.broadcasted_iota(jnp.int32, values.shape, 0)
        values = masked(values, first_row + position // side, position % side, mask_ref)
        out_ref[pl.ds(at, size), :] = values.astype(BF16).astype(out_ref.dtype)

    if count == size:
        block(0)
    else:
        pl.loop(0, count // size)(lambda n: block(pl.multiple_of(n * size, size)))


def gate_of(normed_ref, gate_ref, edge_w_ref, edge_bias_ref, layer):
    width = gate_ref.shape[1]
    low = edge_bias_ref.shape[1] - width
    value = jnp.dot(normed_ref[...], edge_w_ref[layer, :, low:], preferred_element_type=F32)
    gate_ref[...] = sigmoid(value + edge_bias_ref[layer : layer + 1, low:])


def finish(block, contracted, gate, gain_ref, shift_ref, out_w_ref, out_bias_ref, layer):
    normed = normalize(contracted, gain_ref[layer, 1:2, :], shift_ref[layer, 1:2, :]).astype(BF16)
    result = jnp.dot(normed, out_w_ref[layer], preferred_element_type=F32)
    return block + gate * (result + out_bias_ref[layer : layer + 1, :])


def norm_kernel(pair_ref, gain_ref, shift_ref, normed_ref):
    block = pair_ref[...].reshape(normed_ref.shape)
    normed_ref[...] = normalize(block, gain_ref[0, 0:1, :], shift_ref[0, 0:1, :]).astype(BF16)


def merge(low, a, b, shift):
    return jnp.where(low, a, b) + pltpu.roll(jnp.where(low, b, a), shift, 0)


def fold(parts, sub):
    low = (sub & 1) == 0
    first, second = merge(low, parts[0], parts[1], 1), merge(low, parts[2], parts[3], 1)
    return merge((sub & 2) == 0, first, second, 2)


def row_sums(left_ref, piece_ref, a, rows, side):
    hidden = left_ref.shape[1]

    def chunk(at, totals):
        right = piece_ref[pl.ds(a * side + at, CHUNK), :].astype(F32)
        sums = []
        for i in range(rows):
            product = left_ref[pl.ds(i * side + at, CHUNK), :] * right
            sums.append(jnp.sum(product.reshape(CHUNK // 8, 8, hidden), axis=0))
        return [t + s for t, s in zip(totals, sums)] if totals else sums

    totals = chunk(0, None)
    if side > CHUNK:
        totals = lax.fori_loop(
            1, side // CHUNK, lambda n, t: chunk(pl.multiple_of(n * CHUNK, CHUNK), t), totals
        )
    return totals


def piece_products(left_ref, piece_ref, rows, side):
    sub = lax.broadcasted_iota(jnp.int32, (8, left_ref.shape[1]), 0)
    totals = [row_sums(left_ref, piece_ref, a, rows, side) for a in range(rows)]
    return [fold([totals[a][i] for a in range(rows)], sub) for i in range(rows)]


def outgoing_edges_kernel(held, rows, at_ref, *refs):
    normed, refs = refs[: len(held)], refs[len(held) :]
    mask_ref, edge_w_ref, edge_bias_ref, *refs = refs
    own = held[0] == 0
    if own:
        right_ref, part_ref, left_ref, gate_ref = refs
    else:
        left_ref, right_ref, part_ref = refs
    side = left_ref.shape[0] // rows
    shared = (side, mask_ref, edge_w_ref, edge_bias_ref, 0)
    if own:
        edges(normed[0], left_ref, at_ref[0] * rows, *shared, 0)
        gate_of(normed[0], gate_ref, edge_w_ref, edge_bias_ref, 0)
    for n, s in enumerate(held):
        edges(normed[n], right_ref.at[n], (at_ref[0] ^ s) * rows, *shared, 2)
        for i, part in enumerate(piece_products(left_ref, right_ref.at[n], rows, side)):
            part_ref[n, i] = part


def outgoing_kernel(left_ref, piece_ref, part_ref):
    rows = part_ref.shape[1]
    side = left_ref.shape[0] // rows
    for n in range(piece_ref.shape[0]):
        for i, part in enumerate(piece_products(left_ref, piece_ref.at[n], rows, side)):
            part_ref[n, i] = part


def outgoing_finish_kernel(last, given, at_ref, piece_ref, *refs):
    parts, refs = refs[: len(given)], refs[len(given) :]
    (
        left_ref, gate_ref, pair_ref, gain_ref, shift_ref, out_w_ref, out_bias_ref,
        first_ref, normed_ref, x_scr,
    ) = refs
    rows, side, width = pair_ref.shape
    hidden = left_ref.shape[1]
    sub = lax.broadcasted_iota(jnp.int32, (8, hidden), 0)
    me = at_ref[0]
    low = (sub & 4) == 0
    known = {s: (ref, n) for ref, held in zip(parts, given) for n, s in enumerate(held)}

    def part_of(s):
        if s in last:
            return piece_products(left_ref, piece_ref.at[last.index(s)], rows, side)
        ref, n = known[s]
        return [ref[n, i] for i in range(rows)]

    for s in range(0, len(known) + len(last), 2):
        at = pl.multiple_of((me >> 1 ^ s >> 1) * 2 * rows, 2 * rows)
        for i, (a, b) in enumerate(zip(part_of(s), part_of(s + 1))):
            x = merge(low, a, b, 4)
            x = jnp.where(me & 1 == 0, x, pltpu.roll(x, rows, 0))
            x_scr[i, pl.ds(at, 2 * rows), :] = x

    block = pair_ref[...].reshape(rows * side, width)
    contracted = x_scr[...].reshape(rows * side, hidden)
    first = finish(
        block, contracted, gate_ref[...], gain_ref, shift_ref, out_w_ref, out_bias_ref, 0
    )
    first_ref[...] = first
    normed_ref[...] = normalize(first, gain_ref[1, 0:1, :], shift_ref[1, 0:1, :]).astype(BF16)


def add_pieces(pieces, left_scr, x_ref, start):
    rows, side, hidden = x_ref.shape
    for n, (piece, came) in enumerate(pieces):
        left_scr[n] = piece[rows * side :, :].astype(F32)

    def columns(at):
        totals = [start(i, at) for i in range(rows)]
        for n, (piece, came) in enumerate(pieces):
            for a in range(rows):
                right = piece[pl.ds(a * side + at, CHUNK), :].astype(F32)
                for i in range(rows):
                    row = a * 2 * rows + came * rows + i
                    totals[i] = totals[i] + left_scr[n, row : row + 1, :] * right
        for i in range(rows):
            x_ref[i, pl.ds(at, CHUNK), :] = totals[i]

    if side == CHUNK:
        columns(0)
    else:
        pl.loop(0, side // CHUNK)(lambda n: columns(pl.multiple_of(n * CHUNK, CHUNK)))


def incoming_edges_kernel(held, at_ref, *refs):
    normed, refs = refs[: len(held)], refs[len(held) :]
    mask_ref, edge_w_ref, edge_bias_ref, *refs = refs
    if held[0] == 0:
        out_ref, x_ref, gate_ref, left_scr = refs
        gate_of(normed[0], gate_ref, edge_w_ref, edge_bias_ref, 1)
    else:
        before_ref, out_ref, x_ref, left_scr = refs
    rows, side, hidden = x_ref.shape
    me = at_ref[0]
    chip = me >> 1
    columns, places = [], []
    for n, s in enumerate(held):
        edges(
            normed[n], out_ref.at[n, pl.ds(0, rows * side)], (me ^ s) * rows, side,
            mask_ref, edge_w_ref, edge_bias_ref, 1, 2,
        )
        for a in range(rows):
            both = normed[n][pl.ds(pl.multiple_of(a * side + (chip >> 1) * 16, 16), 16), :]
            both = both.astype(F32)
            columns.append(jnp.where(chip & 1 == 0, both[:8], both[8:]))
            places.append(jnp.full((8, hidden), (me ^ s) * rows + a, jnp.int32))
    left = gated(
        jnp.concatenate(columns, 0).astype(BF16), edge_w_ref, edge_bias_ref, 1, 0, hidden
    )
    column = chip * 8 + lax.broadcasted_iota(jnp.int32, left.shape, 0) % 8
    left = masked(left, jnp.concatenate(places, 0), column, mask_ref)
    left = left.reshape(len(held) * rows, 8, hidden)
    left = jnp.where(me & 1 == 0, left, pltpu.roll(left, rows, 1))
    left = left.reshape(len(held), rows * 8, hidden).astype(BF16)
    for n in range(len(held)):
        out_ref[n, rows * side :, :] = left[n]

    def start(i, at):
        if held[0] == 0:
            return jnp.zeros((CHUNK, hidden), F32)
        return before_ref[i, pl.ds(at, CHUNK), :]

    add_pieces([(out_ref.at[n], 0) for n in range(len(held))], left_scr, x_ref, start)


def incoming_kernel(before_ref, piece_ref, x_ref, left_scr):
    pieces = [(piece_ref.at[n], 1) for n in range(piece_ref.shape[0])]
    add_pieces(pieces, left_scr, x_ref, lambda i, at: before_ref[i, pl.ds(at, CHUNK), :])


def incoming_finish_kernel(
    before_ref, piece_ref, first_ref, gate_ref, gain_ref, shift_ref, out_w_ref, out_bias_ref,
    out_ref, left_scr, x_scr,
):
    rows, side, width = out_ref.shape
    hidden = gate_ref.shape[1]
    pieces = [(piece_ref.at[n], 1) for n in range(piece_ref.shape[0])]
    add_pieces(pieces, left_scr, x_scr, lambda i, at: before_ref[i, pl.ds(at, CHUNK), :])
    out_ref[...] = finish(
        first_ref[...], x_scr[...].reshape(rows * side, hidden), gate_ref[...],
        gain_ref, shift_ref, out_w_ref, out_bias_ref, 1,
    ).reshape(rows, side, width)


def call(kernel, name, outs, *operands, scalar=None, scratch=(), flops=0):
    given = operands if scalar is None else (scalar, *operands)
    cost = pl.CostEstimate(flops=flops, bytes_accessed=flops // 64, transcendentals=0)
    return pl.pallas_call(
        kernel,
        in_specs=[SMEM] * (scalar is not None) + [VMEM] * len(operands),
        out_specs=[VMEM] * len(outs),
        out_shape=[jax.ShapeDtypeStruct(*out) for out in outs],
        scratch_shapes=[pltpu.VMEM(*one) for one in scratch],
        compiler_params=PARAMS,
        cost_estimate=cost if flops else None,
        name=name,
    )(*given)


def body(pair, residue_mask, norm_gain, norm_bias, edge_w, edge_bias, out_w, out_bias):
    rows, side, width = pair.shape
    hidden = out_w.shape[1]
    dap = lax.axis_size("dap")
    planes = dap // PLANE
    me = lax.axis_index("dap").reshape(1)
    mask = residue_mask.reshape(1, side)
    norms = (norm_gain, norm_bias)
    weights = (mask, edge_w, edge_bias)
    count = rows * side
    span = count + 2 * rows * rows

    def swap(piece, bits):
        return lax.ppermute(piece, "dap", [(device, device ^ bits) for device in range(dap)])

    def gather(own):
        pieces = {0: own, 2: swap(own, 2)}
        for k in range(planes - 1, 0, -1):
            pieces[PLANE * k] = swap(own, PLANE * k)
        for k in range(planes - 1, 0, -1):
            pieces[PLANE * k + 2] = swap(pieces[PLANE * k], 2)
        return pieces

    groups = (
        [PLANE * k for k in range(planes)],
        [2] + [PLANE * k + 2 for k in range(planes - 1, 0, -1)],
    )
    came = [[s ^ 1 for s in group] for group in groups]

    def work(pieces):
        return 2 * pieces * count * rows * hidden

    (normed,) = call(norm_kernel, "norm", [((count, width), BF16)], pair, *norms)
    pieces = gather(normed)
    others, parts = [], []
    for group in groups:
        held = len(group)
        outs = [((held, count, hidden), BF16), ((held, rows, 8, hidden), F32)]
        if group[0] == 0:
            outs += [((count, hidden), F32), ((count, width), F32)]
        right, part, *rest = call(
            functools.partial(outgoing_edges_kernel, group, rows),
            "outgoing_edges", outs, *[pieces[s] for s in group], *weights,
            *([left] if group[0] else []), scalar=me, flops=work(held),
        )
        if rest:
            left, gate = rest
        parts.append(part)
        others.append(swap(right, 1))
    known = [*groups, came[0]]
    (part,) = call(
        outgoing_kernel, "outgoing", [((planes, rows, 8, hidden), F32)],
        left, others[0], flops=work(planes),
    )
    first, normed = call(
        functools.partial(outgoing_finish_kernel, came[1], known), "outgoing_finish",
        [((count, width), F32), ((count, width), BF16)],
        others[1], *parts, part, left, gate, pair, *norms, out_w, out_bias,
        scalar=me, scratch=[((rows, side, hidden), F32)],
    )

    pieces = gather(normed)
    others, x = [], []
    for group in groups:
        held = len(group)
        outs = [((held, span, hidden), BF16), ((rows, side, hidden), F32)]
        if group[0] == 0:
            outs += [((count, width), F32)]
        edge, *x = call(
            functools.partial(incoming_edges_kernel, group),
            "incoming_edges", outs, *[pieces[s] for s in group], *weights, *x,
            scalar=me, scratch=[((held, 2 * rows * rows, hidden), F32)], flops=work(held),
        )
        if group[0] == 0:
            gate = x.pop()
        others.append(swap(edge, 1))
    x = call(
        incoming_kernel, "incoming", [((rows, side, hidden), F32)], *x, others[0],
        scratch=[((planes, 2 * rows * rows, hidden), F32)], flops=work(planes),
    )
    (out,) = call(
        incoming_finish_kernel, "incoming_finish", [(pair.shape, F32)],
        *x, others[1], first, gate, *norms, out_w, out_bias,
        scratch=[((planes, 2 * rows * rows, hidden), F32), ((rows, side, hidden), F32)],
    )
    return out


def solution(mesh):
    in_specs = (P(("groups", "dap"), None, None), P("groups"), P(), P(), P(), P(), P(), P())
    out_specs = P(("groups", "dap"), None, None)
    return jax.shard_map(body, mesh=mesh, in_specs=in_specs, out_specs=out_specs, check_vma=False)
```

time: 135 us -> 40.1 us (0.30)
  waiting for transfers between devices: 84 us -> 10.5 us
  starting transfers between devices: 3.67 us -> 19.8 us
  between operations: 13.7 us -> 0.18 us
  blocking collectives: 11.4 us -> 0 us
  local copies, waits for them, and re-layouts: 11.6 us -> 4.61 us
  other arithmetic: 5.63 us -> 0 us
  Pallas kernels: 0 us -> 4.74 us
  matrix products: 4.36 us -> 0 us
    all_gather x2 -> x0, waiting for transfers between devices: 76.2 us -> none  [the longest x1 40.6 us: body(): lax.all_gather(right_edge, 'dap', axis=0, tiled=True)]
    ppermute x0 -> x18, starting transfers between devices: none -> 19.8 us  [swap(): lax.ppermute(piece, 'dap', [(device, device ^ bits) for device in range(d...]
    all_to_all x1 -> x0, blocking collectives: 11.4 us -> none  [body(): lax.all_to_all(second, 'dap', split_axis=0, concat_axis=1, tiled=True)]
    ppermute x0 -> x18, waiting for transfers between devices: none -> 10.5 us  [swap(): lax.ppermute(piece, 'dap', [(device, device ^ bits) for device in range(d...]
    all_gather x2 -> x0, local copies, waits for them, and re-layouts: 7.87 us -> none  [the longest x1 3.93 us: body(): lax.all_gather(left_cols, 'dap', axis=1, tiled=True)]
    all_to_all x1 -> x0, waiting for transfers between devices: 7.81 us -> none  [body(): lax.all_to_all(first, 'dap', split_axis=1, concat_axis=0, tiled=True)]
    pallas_call x0 -> x9, Pallas kernels: none -> 4.74 us  [call(): pl.pallas_call(kernel, in_specs=[SMEM] * (scalar is not None) + [VMEM] *...]
    unnamed x8 -> x24, local copies, waits for them, and re-layouts: 0.02 us -> 4.61 us
  transfers between devices with their start and end apart: 3 -> 18, of which waited for: 3 -> 9; matrix products, arithmetic and copies ran while one was open for 0% -> 0% of each run, Pallas kernels for 0% -> 7%
where the time goes in v3:
time: 40.1 us; the launch traced here: 39.8 us
  starting transfers between devices  19.8 us (49%)
  waiting for transfers between devices  10.5 us (26%)
  Pallas kernels  4.74 us (12%)
  local copies, waits for them, and re-layouts  4.61 us (11%)
    ppermute x18, starting transfers between devices, swap(): lax.ppermute(piece, 'dap', [(device, device ^ bits) for device in range(d...  19.8 us
    ppermute x18, waiting for transfers between devices, swap(): lax.ppermute(piece, 'dap', [(device, device ^ bits) for device in range(d...  10.5 us
    pallas_call x9, Pallas kernels, call(): pl.pallas_call(kernel, in_specs=[SMEM] * (scalar is not None) + [VMEM] *...  4.74 us
    unnamed x24, local copies, waits for them, and re-layouts  4.61 us
  transfers between devices with their start and end apart: 18, of which 9 were waited for; matrix products, arithmetic and copies ran while one was open for 0% of the time, Pallas kernels for 7%

profile of v3, /device:TPU:0, one launch (start us, length us, event | category | flops | bytes accessed | tf_op | source)
XLA Modules:
  0.0 39.8 jit_solution(580515766669561965)
XLA Ops:
  0.0 0.9 %copy-done.2 = f32[4,64,128]{2,1,0:T(8,128)S(1)} copy-done((f32[4,64,128]{2,1,0:T(8,128)S(1)}, f32[4,64,128]{2,1,0:T(8,128)}, u32[]{:S(2)}) %copy-start.2) | copy-done | bytes 131096
  0.9 0.7 %copy-done.6 = f32[2,2,128]{2,1,0:T(2,128)S(1)} copy-done((f32[2,2,128]{2,1,0:T(2,128)S(1)}, f32[2,2,128]{2,1,0:T(2,128)}, u32[]{:S(2)}) %copy-start.6) | copy-done | bytes 2072
  1.6 0.7 %copy-done.8 = f32[2,2,128]{2,1,0:T(2,128)S(1)} copy-done((f32[2,2,128]{2,1,0:T(2,128)S(1)}, f32[2,2,128]{2,1,0:T(2,128)}, u32[]{:S(2)}) %copy-start.8) | copy-done | bytes 2072
  2.5 3.1 %collective-permute-start.5 = (bf16[256,128]{1,0:T(8,128)(2,1)S(1)}, bf16[256,128]{1,0:T(8,128)(2,1)S(1)}, u32[]{:S(2)}, u32[]{:S(2)}) collective-permute-start(bf16[256,128]{1,0:T(8,128)(2,1)S(1)} %norm.1.refs_0_), channel_id=1, source_target_pairs={{0,4},{1,5},{2,6},{3,7},{4,0},{5,1},{6,2},{7,3},{8,12},{9,13},{10,... | collective-permute-start | bytes 196616 | tf_op jit(solution)/shard_map/ppermute | solution.py:286
  5.6 2.6 %collective-permute-start.3 = (bf16[256,128]{1,0:T(8,128)(2,1)S(1)}, bf16[256,128]{1,0:T(8,128)(2,1)S(1)}, u32[]{:S(2)}, u32[]{:S(2)}) collective-permute-start(bf16[256,128]{1,0:T(8,128)(2,1)S(1)} %norm.1.refs_0_), channel_id=1, source_target_pairs={{0,8},{1,9},{2,10},{3,11},{4,12},{5,13},{6,14},{7,15},{8,0},{9,1},... | collective-permute-start | bytes 196616 | tf_op jit(solution)/shard_map/ppermute | solution.py:286
  8.2 1.7 %collective-permute-start = (bf16[256,128]{1,0:T(8,128)(2,1)S(1)}, bf16[256,128]{1,0:T(8,128)(2,1)S(1)}, u32[]{:S(2)}, u32[]{:S(2)}) collective-permute-start(bf16[256,128]{1,0:T(8,128)(2,1)S(1)} %norm.1.refs_0_), channel_id=1, source_target_pairs={{0,2},{1,3},{2,0},{3,1},{4,6},{5,7},{6,4},{7,5},{8,10},{9,11},{10,... | collective-permute-start | bytes 196616 | tf_op jit(solution)/shard_map/ppermute | solution.py:286
  10.2 2.6 %collective-permute-done.3.refs_2_ = bf16[256,128]{1,0:T(8,128)(2,1)S(1)} collective-permute-done((bf16[256,128]{1,0:T(8,128)(2,1)S(1)}, bf16[256,128]{1,0:T(8,128)(2,1)S(1)}, u32[]{:S(2)}, u32[]{:S(2)}) %collective-permute-start.3) | collective-permute-done | bytes 65568 | tf_op jit(solution)/shard_map/ppermute | solution.py:286
  12.8 1.5 %collective-permute-start.4 = (bf16[256,128]{1,0:T(8,128)(2,1)S(1)}, bf16[256,128]{1,0:T(8,128)(2,1)S(1)}, u32[]{:S(2)}, u32[]{:S(2)}) collective-permute-start(bf16[256,128]{1,0:T(8,128)(2,1)S(1)} %collective-permute-done.3.refs_2_), channel_id=1, source_target_pairs={{0,2},{1,3},{2,0},{3,1},{4,6},{5,7},{6,4},{7,5},{8,10},{9,11},{10,... | collective-permute-start | bytes 196616 | tf_op jit(solution)/shard_map/ppermute | solution.py:286
  14.4 1.4 %collective-permute-start.2 = (bf16[256,128]{1,0:T(8,128)(2,1)S(1)}, bf16[256,128]{1,0:T(8,128)(2,1)S(1)}, u32[]{:S(2)}, u32[]{:S(2)}) collective-permute-start(bf16[256,128]{1,0:T(8,128)(2,1)S(1)} %collective-permute-done.1.refs_3_), channel_id=1, source_target_pairs={{0,2},{1,3},{2,0},{3,1},{4,6},{5,7},{6,4},{7,5},{8,10},{9,11},{10,... | collective-permute-start | bytes 196616 | tf_op jit(solution)/shard_map/ppermute | solution.py:286
  16.4 1.0 %copy-done = bf16[2,128,640]{2,1,0:T(8,128)(2,1)S(1)} copy-done((bf16[2,128,640]{2,1,0:T(8,128)(2,1)S(1)}, bf16[2,128,640]{2,1,0:T(8,128)(2,1)}, u32[]{:S(2)}) %copy-start) | copy-done | bytes 327704
  19.8 1.0 %collective-permute-done.7.piece_ref = bf16[4,256,128]{2,1,0:T(8,128)(2,1)S(1)} collective-permute-done((bf16[4,256,128]{2,1,0:T(8,128)(2,1)S(1)}, bf16[4,256,128]{2,1,0:T(8,128)(2,1)S(1)}, u32[]{:S(2)}, u32[]{:S(2)}) %collective-permute-start.7) | collective-permute-done | bytes 262176 | tf_op jit(solution)/shard_map/ppermute | solution.py:286
  20.8 0.7 %copy-done.9 = f32[2,2,128]{2,1,0:T(2,128)S(1)} copy-done((f32[2,2,128]{2,1,0:T(2,128)S(1)}, f32[2,2,128]{2,1,0:T(2,128)}, u32[]{:S(2)}) %copy-start.9) | copy-done | bytes 2072
  21.5 0.7 %outgoing_finish.1 = (f32[256,128]{1,0:T(8,128)S(1)}, bf16[256,128]{1,0:T(8,128)(2,1)S(1)}) custom-call(s32[1]{0:T(128)} %bitcast.at_ref, bf16[4,256,128]{2,1,0:T(8,128)(2,1)S(1)} %collective-permute-done.7.piece_ref, f32[4,4,8,128]{3,2,1,0:T(8,128)S(1)} %get-tuple-element.20.refs_0_, f32[4,4,8,128]{3,2,1,0:T(8,128)S(1)} %get-tuple-element.21.refs_1_, ...), custom_call_target="tpu_custom_call" | custom-call | tf_op jit(solution)/shard_map/outgoing_finish/pallas_call | solution.py:261
  22.6 3.4 %collective-permute-start.12 = (bf16[256,128]{1,0:T(8,128)(2,1)S(1)}, bf16[256,128]{1,0:T(8,128)(2,1)S(1)}, u32[]{:S(2)}, u32[]{:S(2)}) collective-permute-start(bf16[256,128]{1,0:T(8,128)(2,1)S(1)} %get-tuple-element.24.refs_0_), channel_id=1, source_target_pairs={{0,8},{1,9},{2,10},{3,11},{4,12},{5,13},{6,14},{7,15},{8,0},{9,1},... | collective-permute-start | bytes 196616 | tf_op jit(solution)/shard_map/ppermute | solution.py:286
  26.7 1.4 %collective-permute-start.9 = (bf16[256,128]{1,0:T(8,128)(2,1)S(1)}, bf16[256,128]{1,0:T(8,128)(2,1)S(1)}, u32[]{:S(2)}, u32[]{:S(2)}) collective-permute-start(bf16[256,128]{1,0:T(8,128)(2,1)S(1)} %get-tuple-element.24.refs_0_), channel_id=1, source_target_pairs={{0,2},{1,3},{2,0},{3,1},{4,6},{5,7},{6,4},{7,5},{8,10},{9,11},{10,... | collective-permute-start | bytes 196616 | tf_op jit(solution)/shard_map/ppermute | solution.py:286
  28.1 1.0 %collective-permute-start.15 = (bf16[256,128]{1,0:T(8,128)(2,1)S(1)}, bf16[256,128]{1,0:T(8,128)(2,1)S(1)}, u32[]{:S(2)}, u32[]{:S(2)}) collective-permute-start(bf16[256,128]{1,0:T(8,128)(2,1)S(1)} %collective-permute-done.14.refs_1_), channel_id=1, source_target_pairs={{0,2},{1,3},{2,0},{3,1},{4,6},{5,7},{6,4},{7,5},{8,10},{9,11},{10,... | collective-permute-start | bytes 196616 | tf_op jit(solution)/shard_map/ppermute | solution.py:286
  29.1 1.0 %collective-permute-done.12.refs_2_ = bf16[256,128]{1,0:T(8,128)(2,1)S(1)} collective-permute-done((bf16[256,128]{1,0:T(8,128)(2,1)S(1)}, bf16[256,128]{1,0:T(8,128)(2,1)S(1)}, u32[]{:S(2)}, u32[]{:S(2)}) %collective-permute-start.12) | collective-permute-done | bytes 65568 | tf_op jit(solution)/shard_map/ppermute | solution.py:286
  30.1 1.3 %collective-permute-start.13 = (bf16[256,128]{1,0:T(8,128)(2,1)S(1)}, bf16[256,128]{1,0:T(8,128)(2,1)S(1)}, u32[]{:S(2)}, u32[]{:S(2)}) collective-permute-start(bf16[256,128]{1,0:T(8,128)(2,1)S(1)} %collective-permute-done.12.refs_2_), channel_id=1, source_target_pairs={{0,2},{1,3},{2,0},{3,1},{4,6},{5,7},{6,4},{7,5},{8,10},{9,11},{10,... | collective-permute-start | bytes 196616 | tf_op jit(solution)/shard_map/ppermute | solution.py:286
  31.4 0.8 %collective-permute-done.10.refs_3_ = bf16[256,128]{1,0:T(8,128)(2,1)S(1)} collective-permute-done((bf16[256,128]{1,0:T(8,128)(2,1)S(1)}, bf16[256,128]{1,0:T(8,128)(2,1)S(1)}, u32[]{:S(2)}, u32[]{:S(2)}) %collective-permute-start.10) | collective-permute-done | bytes 65568 | tf_op jit(solution)/shard_map/ppermute | solution.py:286
  32.2 0.7 %collective-permute-start.11 = (bf16[256,128]{1,0:T(8,128)(2,1)S(1)}, bf16[256,128]{1,0:T(8,128)(2,1)S(1)}, u32[]{:S(2)}, u32[]{:S(2)}) collective-permute-start(bf16[256,128]{1,0:T(8,128)(2,1)S(1)} %collective-permute-done.10.refs_3_), channel_id=1, source_target_pairs={{0,2},{1,3},{2,0},{3,1},{4,6},{5,7},{6,4},{7,5},{8,10},{9,11},{10,... | collective-permute-start | bytes 196616 | tf_op jit(solution)/shard_map/ppermute | solution.py:286
  33.6 1.0 %collective-permute-done.13.refs_2_ = bf16[256,128]{1,0:T(8,128)(2,1)S(1)} collective-permute-done((bf16[256,128]{1,0:T(8,128)(2,1)S(1)}, bf16[256,128]{1,0:T(8,128)(2,1)S(1)}, u32[]{:S(2)}, u32[]{:S(2)}) %collective-permute-start.13) | collective-permute-done | bytes 65568 | tf_op jit(solution)/shard_map/ppermute | solution.py:286
  34.6 1.8 %collective-permute-done.11.refs_1_ = bf16[256,128]{1,0:T(8,128)(2,1)S(1)} collective-permute-done((bf16[256,128]{1,0:T(8,128)(2,1)S(1)}, bf16[256,128]{1,0:T(8,128)(2,1)S(1)}, u32[]{:S(2)}, u32[]{:S(2)}) %collective-permute-start.11) | collective-permute-done | bytes 65568 | tf_op jit(solution)/shard_map/ppermute | solution.py:286
  37.3 1.4 %collective-permute-done.17.piece_ref = bf16[4,288,128]{2,1,0:T(8,128)(2,1)S(1)} collective-permute-done((bf16[4,288,128]{2,1,0:T(8,128)(2,1)S(1)}, bf16[4,288,128]{2,1,0:T(8,128)(2,1)S(1)}, u32[]{:S(2)}, u32[]{:S(2)}) %collective-permute-start.17) | collective-permute-done | bytes 294944 | tf_op jit(solution)/shard_map/ppermute | solution.py:286
  38.7 1.1 %incoming_finish.1 = f32[4,64,128]{2,1,0:T(8,128)} custom-call(f32[4,64,128]{2,1,0:T(8,128)S(1)} %incoming.1.before_ref, bf16[4,288,128]{2,1,0:T(8,128)(2,1)S(1)} %collective-permute-done.17.piece_ref, f32[256,128]{1,0:T(8,128)S(1)} %get-tuple-element.29.first_ref, f32[256,128]{1,0:T(8,128)S(1)} %get-tuple-element.30.gate_ref, f32[2,2,128]{2,1,0:T(2,128)S(1)} %copy-done.7, ...), custom_call_target="tpu_custom_call" | custom-call | tf_op jit(solution)/shard_map/incoming_finish/pallas_call | solution.py:261
  (45 shorter events, 6.1 us)
Async XLA Ops:
  0.0 0.9 %copy-start.2 = (f32[4,64,128]{2,1,0:T(8,128)S(1)}, f32[4,64,128]{2,1,0:T(8,128)}, u32[]{:S(2)}) copy-start(f32[4,64,128]{2,1,0:T(8,128)} %refs_5_.7) | copy-start | bytes 393220
  2.5 13.3 %copy-start.5 = (f32[2,640]{1,0:T(2,128)S(1)}, f32[2,640]{1,0:T(2,128)}, u32[]{:S(2)}) copy-start(f32[2,640]{1,0:T(2,128)} %refs_6_.9) | copy-start | bytes 15364
  2.5 7.4 %collective-permute-start.5 = (bf16[256,128]{1,0:T(8,128)(2,1)S(1)}, bf16[256,128]{1,0:T(8,128)(2,1)S(1)}, u32[]{:S(2)}, u32[]{:S(2)}) collective-permute-start(bf16[256,128]{1,0:T(8,128)(2,1)S(1)} %norm.1.refs_0_), channel_id=1, source_target_pairs={{0,4},{1,5},{2,6},{3,7},{4,0},{5,1},{6,2},{7,3},{8,12},{9,13},{10,... | collective-permute-start | bytes 196616 | tf_op jit(solution)/shard_map/ppermute | solution.py:286
  5.6 7.3 %collective-permute-start.3 = (bf16[256,128]{1,0:T(8,128)(2,1)S(1)}, bf16[256,128]{1,0:T(8,128)(2,1)S(1)}, u32[]{:S(2)}, u32[]{:S(2)}) collective-permute-start(bf16[256,128]{1,0:T(8,128)(2,1)S(1)} %norm.1.refs_0_), channel_id=1, source_target_pairs={{0,8},{1,9},{2,10},{3,11},{4,12},{5,13},{6,14},{7,15},{8,0},{9,1},... | collective-permute-start | bytes 196616 | tf_op jit(solution)/shard_map/ppermute | solution.py:286
  8.2 6.2 %collective-permute-start.1 = (bf16[256,128]{1,0:T(8,128)(2,1)S(1)}, bf16[256,128]{1,0:T(8,128)(2,1)S(1)}, u32[]{:S(2)}, u32[]{:S(2)}) collective-permute-start(bf16[256,128]{1,0:T(8,128)(2,1)S(1)} %norm.1.refs_0_), channel_id=1, source_target_pairs={{0,12},{1,13},{2,14},{3,15},{4,8},{5,9},{6,10},{7,11},{8,4},{9,5},... | collective-permute-start | bytes 196616 | tf_op jit(solution)/shard_map/ppermute | solution.py:286
  8.2 9.9 %collective-permute-start = (bf16[256,128]{1,0:T(8,128)(2,1)S(1)}, bf16[256,128]{1,0:T(8,128)(2,1)S(1)}, u32[]{:S(2)}, u32[]{:S(2)}) collective-permute-start(bf16[256,128]{1,0:T(8,128)(2,1)S(1)} %norm.1.refs_0_), channel_id=1, source_target_pairs={{0,2},{1,3},{2,0},{3,1},{4,6},{5,7},{6,4},{7,5},{8,10},{9,11},{10,... | collective-permute-start | bytes 196616 | tf_op jit(solution)/shard_map/ppermute | solution.py:286
  9.9 8.2 %collective-permute-start.6 = (bf16[256,128]{1,0:T(8,128)(2,1)S(1)}, bf16[256,128]{1,0:T(8,128)(2,1)S(1)}, u32[]{:S(2)}, u32[]{:S(2)}) collective-permute-start(bf16[256,128]{1,0:T(8,128)(2,1)S(1)} %collective-permute-done.5.refs_1_), channel_id=1, source_target_pairs={{0,2},{1,3},{2,0},{3,1},{4,6},{5,7},{6,4},{7,5},{8,10},{9,11},{10,... | collective-permute-start | bytes 196616 | tf_op jit(solution)/shard_map/ppermute | solution.py:286
  12.8 5.3 %collective-permute-start.4 = (bf16[256,128]{1,0:T(8,128)(2,1)S(1)}, bf16[256,128]{1,0:T(8,128)(2,1)S(1)}, u32[]{:S(2)}, u32[]{:S(2)}) collective-permute-start(bf16[256,128]{1,0:T(8,128)(2,1)S(1)} %collective-permute-done.3.refs_2_), channel_id=1, source_target_pairs={{0,2},{1,3},{2,0},{3,1},{4,6},{5,7},{6,4},{7,5},{8,10},{9,11},{10,... | collective-permute-start | bytes 196616 | tf_op jit(solution)/shard_map/ppermute | solution.py:286
  14.4 4.3 %collective-permute-start.2 = (bf16[256,128]{1,0:T(8,128)(2,1)S(1)}, bf16[256,128]{1,0:T(8,128)(2,1)S(1)}, u32[]{:S(2)}, u32[]{:S(2)}) collective-permute-start(bf16[256,128]{1,0:T(8,128)(2,1)S(1)} %collective-permute-done.1.refs_3_), channel_id=1, source_target_pairs={{0,2},{1,3},{2,0},{3,1},{4,6},{5,7},{6,4},{7,5},{8,10},{9,11},{10,... | collective-permute-start | bytes 196616 | tf_op jit(solution)/shard_map/ppermute | solution.py:286
  16.4 1.0 %copy-start = (bf16[2,128,640]{2,1,0:T(8,128)(2,1)S(1)}, bf16[2,128,640]{2,1,0:T(8,128)(2,1)}, u32[]{:S(2)}) copy-start(bf16[2,128,640]{2,1,0:T(8,128)(2,1)} %refs_5_.9) | copy-start | bytes 983044
  17.4 1.2 %copy-start.1 = (bf16[2,128,640]{2,1,0:T(8,128)(2,1)S(1)}, bf16[2,128,640]{2,1,0:T(8,128)(2,1)}, u32[]{:S(2)}) copy-start(bf16[2,128,640]{2,1,0:T(8,128)(2,1)} %refs_5_.9) | copy-start | bytes 983044
  18.0 1.6 %collective-permute-start.8 = (bf16[4,256,128]{2,1,0:T(8,128)(2,1)S(1)}, bf16[4,256,128]{2,1,0:T(8,128)(2,1)S(1)}, u32[]{:S(2)}, u32[]{:S(2)}) collective-permute-start(bf16[4,256,128]{2,1,0:T(8,128)(2,1)S(1)} %get-tuple-element.22), channel_id=1, source_target_pairs={{0,1},{1,0},{2,3},{3,2},{4,5},{5,4},{6,7},{7,6},{8,9},{9,8},{10,11... | collective-permute-start | bytes 786440 | tf_op jit(solution)/shard_map/ppermute | solution.py:286
  19.2 1.6 %copy-start.3 = (f32[4,64,128]{2,1,0:T(8,128)S(1)}, f32[4,64,128]{2,1,0:T(8,128)}, u32[]{:S(2)}) copy-start(f32[4,64,128]{2,1,0:T(8,128)} %refs_5_.7) | copy-start | bytes 393220
  19.2 1.6 %copy-start.4 = (bf16[2,128,128]{2,1,0:T(8,128)(2,1)S(1)}, bf16[2,128,128]{2,1,0:T(8,128)(2,1)}, u32[]{:S(2)}) copy-start(bf16[2,128,128]{2,1,0:T(8,128)(2,1)} %out_w_ref.1) | copy-start | bytes 196612
  19.2 1.6 %collective-permute-start.7 = (bf16[4,256,128]{2,1,0:T(8,128)(2,1)S(1)}, bf16[4,256,128]{2,1,0:T(8,128)(2,1)S(1)}, u32[]{:S(2)}, u32[]{:S(2)}) collective-permute-start(bf16[4,256,128]{2,1,0:T(8,128)(2,1)S(1)} %get-tuple-element.19), channel_id=1, source_target_pairs={{0,1},{1,0},{2,3},{3,2},{4,5},{5,4},{6,7},{7,6},{8,9},{9,8},{10,11... | collective-permute-start | bytes 786440 | tf_op jit(solution)/shard_map/ppermute | solution.py:286
  22.2 5.9 %collective-permute-start.14 = (bf16[256,128]{1,0:T(8,128)(2,1)S(1)}, bf16[256,128]{1,0:T(8,128)(2,1)S(1)}, u32[]{:S(2)}, u32[]{:S(2)}) collective-permute-start(bf16[256,128]{1,0:T(8,128)(2,1)S(1)} %get-tuple-element.24.refs_0_), channel_id=1, source_target_pairs={{0,4},{1,5},{2,6},{3,7},{4,0},{5,1},{6,2},{7,3},{8,12},{9,13},{10,... | collective-permute-start | bytes 196616 | tf_op jit(solution)/shard_map/ppermute | solution.py:286
  22.6 7.4 %collective-permute-start.12 = (bf16[256,128]{1,0:T(8,128)(2,1)S(1)}, bf16[256,128]{1,0:T(8,128)(2,1)S(1)}, u32[]{:S(2)}, u32[]{:S(2)}) collective-permute-start(bf16[256,128]{1,0:T(8,128)(2,1)S(1)} %get-tuple-element.24.refs_0_), channel_id=1, source_target_pairs={{0,8},{1,9},{2,10},{3,11},{4,12},{5,13},{6,14},{7,15},{8,0},{9,1},... | collective-permute-start | bytes 196616 | tf_op jit(solution)/shard_map/ppermute | solution.py:286
  26.0 6.2 %collective-permute-start.10 = (bf16[256,128]{1,0:T(8,128)(2,1)S(1)}, bf16[256,128]{1,0:T(8,128)(2,1)S(1)}, u32[]{:S(2)}, u32[]{:S(2)}) collective-permute-start(bf16[256,128]{1,0:T(8,128)(2,1)S(1)} %get-tuple-element.24.refs_0_), channel_id=1, source_target_pairs={{0,12},{1,13},{2,14},{3,15},{4,8},{5,9},{6,10},{7,11},{8,4},{9,5},... | collective-permute-start | bytes 196616 | tf_op jit(solution)/shard_map/ppermute | solution.py:286
  26.7 6.9 %collective-permute-start.9 = (bf16[256,128]{1,0:T(8,128)(2,1)S(1)}, bf16[256,128]{1,0:T(8,128)(2,1)S(1)}, u32[]{:S(2)}, u32[]{:S(2)}) collective-permute-start(bf16[256,128]{1,0:T(8,128)(2,1)S(1)} %get-tuple-element.24.refs_0_), channel_id=1, source_target_pairs={{0,2},{1,3},{2,0},{3,1},{4,6},{5,7},{6,4},{7,5},{8,10},{9,11},{10,... | collective-permute-start | bytes 196616 | tf_op jit(solution)/shard_map/ppermute | solution.py:286
  28.1 5.5 %collective-permute-start.15 = (bf16[256,128]{1,0:T(8,128)(2,1)S(1)}, bf16[256,128]{1,0:T(8,128)(2,1)S(1)}, u32[]{:S(2)}, u32[]{:S(2)}) collective-permute-start(bf16[256,128]{1,0:T(8,128)(2,1)S(1)} %collective-permute-done.14.refs_1_), channel_id=1, source_target_pairs={{0,2},{1,3},{2,0},{3,1},{4,6},{5,7},{6,4},{7,5},{8,10},{9,11},{10,... | collective-permute-start | bytes 196616 | tf_op jit(solution)/shard_map/ppermute | solution.py:286
  30.1 4.5 %collective-permute-start.13 = (bf16[256,128]{1,0:T(8,128)(2,1)S(1)}, bf16[256,128]{1,0:T(8,128)(2,1)S(1)}, u32[]{:S(2)}, u32[]{:S(2)}) collective-permute-start(bf16[256,128]{1,0:T(8,128)(2,1)S(1)} %collective-permute-done.12.refs_2_), channel_id=1, source_target_pairs={{0,2},{1,3},{2,0},{3,1},{4,6},{5,7},{6,4},{7,5},{8,10},{9,11},{10,... | collective-permute-start | bytes 196616 | tf_op jit(solution)/shard_map/ppermute | solution.py:286
  32.2 4.3 %collective-permute-start.11 = (bf16[256,128]{1,0:T(8,128)(2,1)S(1)}, bf16[256,128]{1,0:T(8,128)(2,1)S(1)}, u32[]{:S(2)}, u32[]{:S(2)}) collective-permute-start(bf16[256,128]{1,0:T(8,128)(2,1)S(1)} %collective-permute-done.10.refs_3_), channel_id=1, source_target_pairs={{0,2},{1,3},{2,0},{3,1},{4,6},{5,7},{6,4},{7,5},{8,10},{9,11},{10,... | collective-permute-start | bytes 196616 | tf_op jit(solution)/shard_map/ppermute | solution.py:286
  33.5 3.6 %collective-permute-start.16 = (bf16[4,288,128]{2,1,0:T(8,128)(2,1)S(1)}, bf16[4,288,128]{2,1,0:T(8,128)(2,1)S(1)}, u32[]{:S(2)}, u32[]{:S(2)}) collective-permute-start(bf16[4,288,128]{2,1,0:T(8,128)(2,1)S(1)} %get-tuple-element.27), channel_id=1, source_target_pairs={{0,1},{1,0},{2,3},{3,2},{4,5},{5,4},{6,7},{7,6},{8,9},{9,8},{10,11... | collective-permute-start | bytes 884744 | tf_op jit(solution)/shard_map/ppermute | solution.py:286
  37.1 1.6 %collective-permute-start.17 = (bf16[4,288,128]{2,1,0:T(8,128)(2,1)S(1)}, bf16[4,288,128]{2,1,0:T(8,128)(2,1)S(1)}, u32[]{:S(2)}, u32[]{:S(2)}) collective-permute-start(bf16[4,288,128]{2,1,0:T(8,128)(2,1)S(1)} %get-tuple-element.28), channel_id=1, source_target_pairs={{0,1},{1,0},{2,3},{3,2},{4,5},{5,4},{6,7},{7,6},{8,9},{9,8},{10,11... | collective-permute-start | bytes 884744 | tf_op jit(solution)/shard_map/ppermute | solution.py:286
  (6 other events, 4.1 us)

commit v4 on v3

--- a/solution.py
+++ b/solution.py
@@ -71,9 +71,22 @@
     return block + gate * (result + out_bias_ref[layer : layer + 1, :])
 
 
-def norm_kernel(pair_ref, gain_ref, shift_ref, normed_ref):
+def norm_kernel(*refs):
+    count = len(refs) // 2 - 1
+    given, kept, (normed_ref, sems) = refs[:count], refs[count : 2 * count], refs[2 * count :]
+    copies = [
+        pltpu.make_async_copy(source, target, sems.at[n])
+        for n, (source, target) in enumerate(zip(given, kept))
+    ]
+    for copy in copies:
+        copy.start()
+    for copy in copies[:3]:
+        copy.wait()
+    pair_ref, gain_ref, shift_ref = kept[:3]
     block = pair_ref[...].reshape(normed_ref.shape)
     normed_ref[...] = normalize(block, gain_ref[0, 0:1, :], shift_ref[0, 0:1, :]).astype(BF16)
+    for copy in copies[3:]:
+        copy.wait()
 
 
 def merge(low, a, b, shift):
@@ -277,9 +290,21 @@
     planes = dap // PLANE
     me = lax.axis_index("dap").reshape(1)
     mask = residue_mask.reshape(1, side)
+    count = rows * side
+    arguments = (pair, norm_gain, norm_bias, mask, edge_w, edge_bias, out_w, out_bias)
+    *kept, normed = pl.pallas_call(
+        norm_kernel,
+        in_specs=[pl.BlockSpec(memory_space=pltpu.HBM)] * len(arguments),
+        out_specs=[VMEM] * (len(arguments) + 1),
+        out_shape=[jax.ShapeDtypeStruct(value.shape, value.dtype) for value in arguments]
+        + [jax.ShapeDtypeStruct((count, width), BF16)],
+        scratch_shapes=[pltpu.SemaphoreType.DMA((len(arguments),))],
+        compiler_params=PARAMS,
+        name="norm",
+    )(*[pltpu.with_memory_space_constraint(value, pltpu.HBM) for value in arguments])
+    pair, norm_gain, norm_bias, mask, edge_w, edge_bias, out_w, out_bias = kept
     norms = (norm_gain, norm_bias)
     weights = (mask, edge_w, edge_bias)
-    count = rows * side
     span = count + 2 * rows * rows
 
     def swap(piece, bits):
@@ -302,7 +327,6 @@
     def work(pieces):
         return 2 * pieces * count * rows * hidden
 
-    (normed,) = call(norm_kernel, "norm", [((count, width), BF16)], pair, *norms)
     pieces = gather(normed)
     others, parts = [], []
     for group in groups:

time: 40.1 us -> 37.9 us (0.945)
  local copies, waits for them, and re-layouts: 4.61 us -> 0 us
  waiting for transfers between devices: 10.5 us -> 12.8 us
  Pallas kernels: 4.74 us -> 5.72 us
  starting transfers between devices: 19.8 us -> 19.1 us
    unnamed x24 -> x0, local copies, waits for them, and re-layouts: 4.61 us -> none
    ppermute x18, waiting for transfers between devices: 10.5 us -> 12.8 us  [swap(): lax.ppermute(piece, 'dap', [(device, device ^ bits) for device in range(d...]
    pallas_call x0 -> x1, Pallas kernels: none -> 1.18 us  [body(): pl.pallas_call(norm_kernel, in_specs=[pl.BlockSpec(memory_space=pltpu.HBM...]
    ppermute x18, starting transfers between devices: 19.8 us -> 19.1 us  [swap(): lax.ppermute(piece, 'dap', [(device, device ^ bits) for device in range(d...]
    pallas_call x9 -> x8, Pallas kernels: 4.74 us -> 4.53 us  [call(): pl.pallas_call(kernel, in_specs=[SMEM] * (scalar is not None) + [VMEM] *...]
where the time goes in v4:
time: 37.9 us; the launch traced here: 37.8 us
  starting transfers between devices  19.1 us (50%)
  waiting for transfers between devices  12.8 us (34%)
  Pallas kernels  5.72 us (15%)
    ppermute x18, starting transfers between devices, swap(): lax.ppermute(piece, 'dap', [(device, device ^ bits) for device in range(d...  19.1 us
    ppermute x18, waiting for transfers between devices, swap(): lax.ppermute(piece, 'dap', [(device, device ^ bits) for device in range(d...  12.8 us
    pallas_call x8, Pallas kernels, call(): pl.pallas_call(kernel, in_specs=[SMEM] * (scalar is not None) + [VMEM] *...  4.53 us
    pallas_call x1, Pallas kernels, body(): pl.pallas_call(norm_kernel, in_specs=[pl.BlockSpec(memory_space=pltpu.HBM...  1.18 us
  transfers between devices with their start and end apart: 18, of which 9 were waited for; matrix products, arithmetic and copies ran while one was open for 0% of the time, Pallas kernels for 7%

profile of v4, /device:TPU:0, one launch (start us, length us, event | category | flops | bytes accessed | tf_op | source)
XLA Modules:
  0.0 37.8 jit_solution(1021449768184293063)
XLA Ops:
  0.0 1.2 %norm.1 = (f32[4,64,128]{2,1,0:T(8,128)S(1)}, f32[2,2,128]{2,1,0:T(2,128)S(1)}, f32[2,2,128]{2,1,0:T(2,128)S(1)}, s32[1,64]{1,0:T(1,128)S(1)}, bf16[2,128,640]{2...) custom-call(f32[4,64,128]{2,1,0:T(8,128)} %refs_0_.1, ...), custom_call_target="tpu_custom_call" | custom-call | tf_op jit(solution)/shard_map/norm/pallas_call | solution.py:295
  1.2 3.1 %collective-permute-start.5 = (bf16[256,128]{1,0:T(8,128)(2,1)S(1)}, bf16[256,128]{1,0:T(8,128)(2,1)S(1)}, u32[]{:S(2)}, u32[]{:S(2)}) collective-permute-start(bf16[256,128]{1,0:T(8,128)(2,1)S(1)} %get-tuple-element.27.refs_0_), channel_id=1, source_target_pairs={{0,4},{1,5},{2,6},{3,7},{4,0},{5,1},{6,2},{7,3},{8,12},{9,13},{10,... | collective-permute-start | bytes 196616 | tf_op jit(solution)/shard_map/ppermute | solution.py:311
  4.3 2.6 %collective-permute-start.3 = (bf16[256,128]{1,0:T(8,128)(2,1)S(1)}, bf16[256,128]{1,0:T(8,128)(2,1)S(1)}, u32[]{:S(2)}, u32[]{:S(2)}) collective-permute-start(bf16[256,128]{1,0:T(8,128)(2,1)S(1)} %get-tuple-element.27.refs_0_), channel_id=1, source_target_pairs={{0,8},{1,9},{2,10},{3,11},{4,12},{5,13},{6,14},{7,15},{8,0},{9,1},... | collective-permute-start | bytes 196616 | tf_op jit(solution)/shard_map/ppermute | solution.py:311
  6.9 1.7 %collective-permute-start = (bf16[256,128]{1,0:T(8,128)(2,1)S(1)}, bf16[256,128]{1,0:T(8,128)(2,1)S(1)}, u32[]{:S(2)}, u32[]{:S(2)}) collective-permute-start(bf16[256,128]{1,0:T(8,128)(2,1)S(1)} %get-tuple-element.27.refs_0_), channel_id=1, source_target_pairs={{0,2},{1,3},{2,0},{3,1},{4,6},{5,7},{6,4},{7,5},{8,10},{9,11},{10,... | collective-permute-start | bytes 196616 | tf_op jit(solution)/shard_map/ppermute | solution.py:311
  8.9 2.6 %collective-permute-done.3.refs_2_ = bf16[256,128]{1,0:T(8,128)(2,1)S(1)} collective-permute-done((bf16[256,128]{1,0:T(8,128)(2,1)S(1)}, bf16[256,128]{1,0:T(8,128)(2,1)S(1)}, u32[]{:S(2)}, u32[]{:S(2)}) %collective-permute-start.3) | collective-permute-done | bytes 65568 | tf_op jit(solution)/shard_map/ppermute | solution.py:311
  11.5 1.5 %collective-permute-start.4 = (bf16[256,128]{1,0:T(8,128)(2,1)S(1)}, bf16[256,128]{1,0:T(8,128)(2,1)S(1)}, u32[]{:S(2)}, u32[]{:S(2)}) collective-permute-start(bf16[256,128]{1,0:T(8,128)(2,1)S(1)} %collective-permute-done.3.refs_2_), channel_id=1, source_target_pairs={{0,2},{1,3},{2,0},{3,1},{4,6},{5,7},{6,4},{7,5},{8,10},{9,11},{10,... | collective-permute-start | bytes 196616 | tf_op jit(solution)/shard_map/ppermute | solution.py:311
  13.1 1.4 %collective-permute-start.2 = (bf16[256,128]{1,0:T(8,128)(2,1)S(1)}, bf16[256,128]{1,0:T(8,128)(2,1)S(1)}, u32[]{:S(2)}, u32[]{:S(2)}) collective-permute-start(bf16[256,128]{1,0:T(8,128)(2,1)S(1)} %collective-permute-done.1.refs_3_), channel_id=1, source_target_pairs={{0,2},{1,3},{2,0},{3,1},{4,6},{5,7},{6,4},{7,5},{8,10},{9,11},{10,... | collective-permute-start | bytes 196616 | tf_op jit(solution)/shard_map/ppermute | solution.py:311
  14.5 0.6 %outgoing_edges.2 = (bf16[4,256,128]{2,1,0:T(8,128)(2,1)S(1)}, f32[4,4,8,128]{3,2,1,0:T(8,128)S(1)}, f32[256,128]{1,0:T(8,128)S(1)}, f32[256,128]{1,0:T(8,128)S(1)}) custom-call(s32[1]{0:T(128)} %bitcast.at_ref, bf16[256,128]{1,0:T(8,128)(2,1)S(1)} %get-tuple-element.27.refs_0_, bf16[256,128]{1,0:T(8,128)(2,1)S(1)} %collective-permute-done.5.refs_1_, ...), custom_call_target="tpu_custom_call" | custom-call | flops 1048576 | bytes 16384 | tf_op jit(solution)/shard_map/outgoing_edges/pallas_call | solution.py:274
  15.2 0.6 %collective-permute-done.4.refs_2_ = bf16[256,128]{1,0:T(8,128)(2,1)S(1)} collective-permute-done((bf16[256,128]{1,0:T(8,128)(2,1)S(1)}, bf16[256,128]{1,0:T(8,128)(2,1)S(1)}, u32[]{:S(2)}, u32[]{:S(2)}) %collective-permute-start.4) | collective-permute-done | bytes 65568 | tf_op jit(solution)/shard_map/ppermute | solution.py:311
  15.8 1.5 %collective-permute-done.2.refs_1_ = bf16[256,128]{1,0:T(8,128)(2,1)S(1)} collective-permute-done((bf16[256,128]{1,0:T(8,128)(2,1)S(1)}, bf16[256,128]{1,0:T(8,128)(2,1)S(1)}, u32[]{:S(2)}, u32[]{:S(2)}) %collective-permute-start.2) | collective-permute-done | bytes 65568 | tf_op jit(solution)/shard_map/ppermute | solution.py:311
  18.2 1.3 %collective-permute-done.7.piece_ref = bf16[4,256,128]{2,1,0:T(8,128)(2,1)S(1)} collective-permute-done((bf16[4,256,128]{2,1,0:T(8,128)(2,1)S(1)}, bf16[4,256,128]{2,1,0:T(8,128)(2,1)S(1)}, u32[]{:S(2)}, u32[]{:S(2)}) %collective-permute-start.7) | collective-permute-done | bytes 262176 | tf_op jit(solution)/shard_map/ppermute | solution.py:311
  19.5 0.7 %outgoing_finish.1 = (f32[256,128]{1,0:T(8,128)S(1)}, bf16[256,128]{1,0:T(8,128)(2,1)S(1)}) custom-call(s32[1]{0:T(128)} %bitcast.at_ref, bf16[4,256,128]{2,1,0:T(8,128)(2,1)S(1)} %collective-permute-done.7.piece_ref, f32[4,4,8,128]{3,2,1,0:T(8,128)S(1)} %get-tuple-element.33.refs_0_, f32[4,4,8,128]{3,2,1,0:T(8,128)S(1)} %get-tuple-element.34.refs_1_, ...), custom_call_target="tpu_custom_call" | custom-call | tf_op jit(solution)/shard_map/outgoing_finish/pallas_call | solution.py:274
  20.6 3.4 %collective-permute-start.12 = (bf16[256,128]{1,0:T(8,128)(2,1)S(1)}, bf16[256,128]{1,0:T(8,128)(2,1)S(1)}, u32[]{:S(2)}, u32[]{:S(2)}) collective-permute-start(bf16[256,128]{1,0:T(8,128)(2,1)S(1)} %get-tuple-element.42.refs_0_), channel_id=1, source_target_pairs={{0,8},{1,9},{2,10},{3,11},{4,12},{5,13},{6,14},{7,15},{8,0},{9,1},... | collective-permute-start | bytes 196616 | tf_op jit(solution)/shard_map/ppermute | solution.py:311
  24.0 0.6 %collective-permute-start.10 = (bf16[256,128]{1,0:T(8,128)(2,1)S(1)}, bf16[256,128]{1,0:T(8,128)(2,1)S(1)}, u32[]{:S(2)}, u32[]{:S(2)}) collective-permute-start(bf16[256,128]{1,0:T(8,128)(2,1)S(1)} %get-tuple-element.42.refs_0_), channel_id=1, source_target_pairs={{0,12},{1,13},{2,14},{3,15},{4,8},{5,9},{6,10},{7,11},{8,4},{9,5},... | collective-permute-start | bytes 196616 | tf_op jit(solution)/shard_map/ppermute | solution.py:311
  24.6 1.4 %collective-permute-start.9 = (bf16[256,128]{1,0:T(8,128)(2,1)S(1)}, bf16[256,128]{1,0:T(8,128)(2,1)S(1)}, u32[]{:S(2)}, u32[]{:S(2)}) collective-permute-start(bf16[256,128]{1,0:T(8,128)(2,1)S(1)} %get-tuple-element.42.refs_0_), channel_id=1, source_target_pairs={{0,2},{1,3},{2,0},{3,1},{4,6},{5,7},{6,4},{7,5},{8,10},{9,11},{10,... | collective-permute-start | bytes 196616 | tf_op jit(solution)/shard_map/ppermute | solution.py:311
  26.1 1.0 %collective-permute-start.15 = (bf16[256,128]{1,0:T(8,128)(2,1)S(1)}, bf16[256,128]{1,0:T(8,128)(2,1)S(1)}, u32[]{:S(2)}, u32[]{:S(2)}) collective-permute-start(bf16[256,128]{1,0:T(8,128)(2,1)S(1)} %collective-permute-done.14.refs_1_), channel_id=1, source_target_pairs={{0,2},{1,3},{2,0},{3,1},{4,6},{5,7},{6,4},{7,5},{8,10},{9,11},{10,... | collective-permute-start | bytes 196616 | tf_op jit(solution)/shard_map/ppermute | solution.py:311
  27.1 1.0 %collective-permute-done.12.refs_2_ = bf16[256,128]{1,0:T(8,128)(2,1)S(1)} collective-permute-done((bf16[256,128]{1,0:T(8,128)(2,1)S(1)}, bf16[256,128]{1,0:T(8,128)(2,1)S(1)}, u32[]{:S(2)}, u32[]{:S(2)}) %collective-permute-start.12) | collective-permute-done | bytes 65568 | tf_op jit(solution)/shard_map/ppermute | solution.py:311
  28.0 0.6 %collective-permute-start.13 = (bf16[256,128]{1,0:T(8,128)(2,1)S(1)}, bf16[256,128]{1,0:T(8,128)(2,1)S(1)}, u32[]{:S(2)}, u32[]{:S(2)}) collective-permute-start(bf16[256,128]{1,0:T(8,128)(2,1)S(1)} %collective-permute-done.12.refs_2_), channel_id=1, source_target_pairs={{0,2},{1,3},{2,0},{3,1},{4,6},{5,7},{6,4},{7,5},{8,10},{9,11},{10,... | collective-permute-start | bytes 196616 | tf_op jit(solution)/shard_map/ppermute | solution.py:311
  28.7 1.5 %collective-permute-done.10.refs_3_ = bf16[256,128]{1,0:T(8,128)(2,1)S(1)} collective-permute-done((bf16[256,128]{1,0:T(8,128)(2,1)S(1)}, bf16[256,128]{1,0:T(8,128)(2,1)S(1)}, u32[]{:S(2)}, u32[]{:S(2)}) %collective-permute-start.10) | collective-permute-done | bytes 65568 | tf_op jit(solution)/shard_map/ppermute | solution.py:311
  30.2 0.7 %collective-permute-start.11 = (bf16[256,128]{1,0:T(8,128)(2,1)S(1)}, bf16[256,128]{1,0:T(8,128)(2,1)S(1)}, u32[]{:S(2)}, u32[]{:S(2)}) collective-permute-start(bf16[256,128]{1,0:T(8,128)(2,1)S(1)} %collective-permute-done.10.refs_3_), channel_id=1, source_target_pairs={{0,2},{1,3},{2,0},{3,1},{4,6},{5,7},{6,4},{7,5},{8,10},{9,11},{10,... | collective-permute-start | bytes 196616 | tf_op jit(solution)/shard_map/ppermute | solution.py:311
  31.6 1.0 %collective-permute-done.13.refs_2_ = bf16[256,128]{1,0:T(8,128)(2,1)S(1)} collective-permute-done((bf16[256,128]{1,0:T(8,128)(2,1)S(1)}, bf16[256,128]{1,0:T(8,128)(2,1)S(1)}, u32[]{:S(2)}, u32[]{:S(2)}) %collective-permute-start.13) | collective-permute-done | bytes 65568 | tf_op jit(solution)/shard_map/ppermute | solution.py:311
  32.6 1.8 %collective-permute-done.11.refs_1_ = bf16[256,128]{1,0:T(8,128)(2,1)S(1)} collective-permute-done((bf16[256,128]{1,0:T(8,128)(2,1)S(1)}, bf16[256,128]{1,0:T(8,128)(2,1)S(1)}, u32[]{:S(2)}, u32[]{:S(2)}) %collective-permute-start.11) | collective-permute-done | bytes 65568 | tf_op jit(solution)/shard_map/ppermute | solution.py:311
  35.3 1.4 %collective-permute-done.17.piece_ref = bf16[4,288,128]{2,1,0:T(8,128)(2,1)S(1)} collective-permute-done((bf16[4,288,128]{2,1,0:T(8,128)(2,1)S(1)}, bf16[4,288,128]{2,1,0:T(8,128)(2,1)S(1)}, u32[]{:S(2)}, u32[]{:S(2)}) %collective-permute-start.17) | collective-permute-done | bytes 294944 | tf_op jit(solution)/shard_map/ppermute | solution.py:311
  36.7 1.1 %incoming_finish.1 = f32[4,64,128]{2,1,0:T(8,128)} custom-call(f32[4,64,128]{2,1,0:T(8,128)S(1)} %incoming.1.before_ref, bf16[4,288,128]{2,1,0:T(8,128)(2,1)S(1)} %collective-permute-done.17.piece_ref, f32[256,128]{1,0:T(8,128)S(1)} %get-tuple-element.47.first_ref, f32[256,128]{1,0:T(8,128)S(1)} %get-tuple-element.48.gate_ref, ...), custom_call_target="tpu_custom_call" | custom-call | tf_op jit(solution)/shard_map/incoming_finish/pallas_call | solution.py:274
  (21 shorter events, 3.1 us)
Async XLA Ops:
  1.2 7.4 %collective-permute-start.5 = (bf16[256,128]{1,0:T(8,128)(2,1)S(1)}, bf16[256,128]{1,0:T(8,128)(2,1)S(1)}, u32[]{:S(2)}, u32[]{:S(2)}) collective-permute-start(bf16[256,128]{1,0:T(8,128)(2,1)S(1)} %get-tuple-element.27.refs_0_), channel_id=1, source_target_pairs={{0,4},{1,5},{2,6},{3,7},{4,0},{5,1},{6,2},{7,3},{8,12},{9,13},{10,... | collective-permute-start | bytes 196616 | tf_op jit(solution)/shard_map/ppermute | solution.py:311
  4.3 7.3 %collective-permute-start.3 = (bf16[256,128]{1,0:T(8,128)(2,1)S(1)}, bf16[256,128]{1,0:T(8,128)(2,1)S(1)}, u32[]{:S(2)}, u32[]{:S(2)}) collective-permute-start(bf16[256,128]{1,0:T(8,128)(2,1)S(1)} %get-tuple-element.27.refs_0_), channel_id=1, source_target_pairs={{0,8},{1,9},{2,10},{3,11},{4,12},{5,13},{6,14},{7,15},{8,0},{9,1},... | collective-permute-start | bytes 196616 | tf_op jit(solution)/shard_map/ppermute | solution.py:311
  6.9 6.2 %collective-permute-start.1 = (bf16[256,128]{1,0:T(8,128)(2,1)S(1)}, bf16[256,128]{1,0:T(8,128)(2,1)S(1)}, u32[]{:S(2)}, u32[]{:S(2)}) collective-permute-start(bf16[256,128]{1,0:T(8,128)(2,1)S(1)} %get-tuple-element.27.refs_0_), channel_id=1, source_target_pairs={{0,12},{1,13},{2,14},{3,15},{4,8},{5,9},{6,10},{7,11},{8,4},{9,5},... | collective-permute-start | bytes 196616 | tf_op jit(solution)/shard_map/ppermute | solution.py:311
  6.9 8.3 %collective-permute-start = (bf16[256,128]{1,0:T(8,128)(2,1)S(1)}, bf16[256,128]{1,0:T(8,128)(2,1)S(1)}, u32[]{:S(2)}, u32[]{:S(2)}) collective-permute-start(bf16[256,128]{1,0:T(8,128)(2,1)S(1)} %get-tuple-element.27.refs_0_), channel_id=1, source_target_pairs={{0,2},{1,3},{2,0},{3,1},{4,6},{5,7},{6,4},{7,5},{8,10},{9,11},{10,... | collective-permute-start | bytes 196616 | tf_op jit(solution)/shard_map/ppermute | solution.py:311
  8.6 6.6 %collective-permute-start.6 = (bf16[256,128]{1,0:T(8,128)(2,1)S(1)}, bf16[256,128]{1,0:T(8,128)(2,1)S(1)}, u32[]{:S(2)}, u32[]{:S(2)}) collective-permute-start(bf16[256,128]{1,0:T(8,128)(2,1)S(1)} %collective-permute-done.5.refs_1_), channel_id=1, source_target_pairs={{0,2},{1,3},{2,0},{3,1},{4,6},{5,7},{6,4},{7,5},{8,10},{9,11},{10,... | collective-permute-start | bytes 196616 | tf_op jit(solution)/shard_map/ppermute | solution.py:311
  11.5 4.3 %collective-permute-start.4 = (bf16[256,128]{1,0:T(8,128)(2,1)S(1)}, bf16[256,128]{1,0:T(8,128)(2,1)S(1)}, u32[]{:S(2)}, u32[]{:S(2)}) collective-permute-start(bf16[256,128]{1,0:T(8,128)(2,1)S(1)} %collective-permute-done.3.refs_2_), channel_id=1, source_target_pairs={{0,2},{1,3},{2,0},{3,1},{4,6},{5,7},{6,4},{7,5},{8,10},{9,11},{10,... | collective-permute-start | bytes 196616 | tf_op jit(solution)/shard_map/ppermute | solution.py:311
  13.1 4.3 %collective-permute-start.2 = (bf16[256,128]{1,0:T(8,128)(2,1)S(1)}, bf16[256,128]{1,0:T(8,128)(2,1)S(1)}, u32[]{:S(2)}, u32[]{:S(2)}) collective-permute-start(bf16[256,128]{1,0:T(8,128)(2,1)S(1)} %collective-permute-done.1.refs_3_), channel_id=1, source_target_pairs={{0,2},{1,3},{2,0},{3,1},{4,6},{5,7},{6,4},{7,5},{8,10},{9,11},{10,... | collective-permute-start | bytes 196616 | tf_op jit(solution)/shard_map/ppermute | solution.py:311
  15.1 2.9 %collective-permute-start.8 = (bf16[4,256,128]{2,1,0:T(8,128)(2,1)S(1)}, bf16[4,256,128]{2,1,0:T(8,128)(2,1)S(1)}, u32[]{:S(2)}, u32[]{:S(2)}) collective-permute-start(bf16[4,256,128]{2,1,0:T(8,128)(2,1)S(1)} %get-tuple-element.35), channel_id=1, source_target_pairs={{0,1},{1,0},{2,3},{3,2},{4,5},{5,4},{6,7},{7,6},{8,9},{9,8},{10,11... | collective-permute-start | bytes 786440 | tf_op jit(solution)/shard_map/ppermute | solution.py:311
  17.9 1.6 %collective-permute-start.7 = (bf16[4,256,128]{2,1,0:T(8,128)(2,1)S(1)}, bf16[4,256,128]{2,1,0:T(8,128)(2,1)S(1)}, u32[]{:S(2)}, u32[]{:S(2)}) collective-permute-start(bf16[4,256,128]{2,1,0:T(8,128)(2,1)S(1)} %get-tuple-element.32), channel_id=1, source_target_pairs={{0,1},{1,0},{2,3},{3,2},{4,5},{5,4},{6,7},{7,6},{8,9},{9,8},{10,11... | collective-permute-start | bytes 786440 | tf_op jit(solution)/shard_map/ppermute | solution.py:311
  20.2 5.9 %collective-permute-start.14 = (bf16[256,128]{1,0:T(8,128)(2,1)S(1)}, bf16[256,128]{1,0:T(8,128)(2,1)S(1)}, u32[]{:S(2)}, u32[]{:S(2)}) collective-permute-start(bf16[256,128]{1,0:T(8,128)(2,1)S(1)} %get-tuple-element.42.refs_0_), channel_id=1, source_target_pairs={{0,4},{1,5},{2,6},{3,7},{4,0},{5,1},{6,2},{7,3},{8,12},{9,13},{10,... | collective-permute-start | bytes 196616 | tf_op jit(solution)/shard_map/ppermute | solution.py:311
  20.6 7.4 %collective-permute-start.12 = (bf16[256,128]{1,0:T(8,128)(2,1)S(1)}, bf16[256,128]{1,0:T(8,128)(2,1)S(1)}, u32[]{:S(2)}, u32[]{:S(2)}) collective-permute-start(bf16[256,128]{1,0:T(8,128)(2,1)S(1)} %get-tuple-element.42.refs_0_), channel_id=1, source_target_pairs={{0,8},{1,9},{2,10},{3,11},{4,12},{5,13},{6,14},{7,15},{8,0},{9,1},... | collective-permute-start | bytes 196616 | tf_op jit(solution)/shard_map/ppermute | solution.py:311
  24.0 6.2 %collective-permute-start.10 = (bf16[256,128]{1,0:T(8,128)(2,1)S(1)}, bf16[256,128]{1,0:T(8,128)(2,1)S(1)}, u32[]{:S(2)}, u32[]{:S(2)}) collective-permute-start(bf16[256,128]{1,0:T(8,128)(2,1)S(1)} %get-tuple-element.42.refs_0_), channel_id=1, source_target_pairs={{0,12},{1,13},{2,14},{3,15},{4,8},{5,9},{6,10},{7,11},{8,4},{9,5},... | collective-permute-start | bytes 196616 | tf_op jit(solution)/shard_map/ppermute | solution.py:311
  24.6 6.9 %collective-permute-start.9 = (bf16[256,128]{1,0:T(8,128)(2,1)S(1)}, bf16[256,128]{1,0:T(8,128)(2,1)S(1)}, u32[]{:S(2)}, u32[]{:S(2)}) collective-permute-start(bf16[256,128]{1,0:T(8,128)(2,1)S(1)} %get-tuple-element.42.refs_0_), channel_id=1, source_target_pairs={{0,2},{1,3},{2,0},{3,1},{4,6},{5,7},{6,4},{7,5},{8,10},{9,11},{10,... | collective-permute-start | bytes 196616 | tf_op jit(solution)/shard_map/ppermute | solution.py:311
  26.1 5.5 %collective-permute-start.15 = (bf16[256,128]{1,0:T(8,128)(2,1)S(1)}, bf16[256,128]{1,0:T(8,128)(2,1)S(1)}, u32[]{:S(2)}, u32[]{:S(2)}) collective-permute-start(bf16[256,128]{1,0:T(8,128)(2,1)S(1)} %collective-permute-done.14.refs_1_), channel_id=1, source_target_pairs={{0,2},{1,3},{2,0},{3,1},{4,6},{5,7},{6,4},{7,5},{8,10},{9,11},{10,... | collective-permute-start | bytes 196616 | tf_op jit(solution)/shard_map/ppermute | solution.py:311
  28.0 4.5 %collective-permute-start.13 = (bf16[256,128]{1,0:T(8,128)(2,1)S(1)}, bf16[256,128]{1,0:T(8,128)(2,1)S(1)}, u32[]{:S(2)}, u32[]{:S(2)}) collective-permute-start(bf16[256,128]{1,0:T(8,128)(2,1)S(1)} %collective-permute-done.12.refs_2_), channel_id=1, source_target_pairs={{0,2},{1,3},{2,0},{3,1},{4,6},{5,7},{6,4},{7,5},{8,10},{9,11},{10,... | collective-permute-start | bytes 196616 | tf_op jit(solution)/shard_map/ppermute | solution.py:311
  30.2 4.3 %collective-permute-start.11 = (bf16[256,128]{1,0:T(8,128)(2,1)S(1)}, bf16[256,128]{1,0:T(8,128)(2,1)S(1)}, u32[]{:S(2)}, u32[]{:S(2)}) collective-permute-start(bf16[256,128]{1,0:T(8,128)(2,1)S(1)} %collective-permute-done.10.refs_3_), channel_id=1, source_target_pairs={{0,2},{1,3},{2,0},{3,1},{4,6},{5,7},{6,4},{7,5},{8,10},{9,11},{10,... | collective-permute-start | bytes 196616 | tf_op jit(solution)/shard_map/ppermute | solution.py:311
  31.5 3.6 %collective-permute-start.16 = (bf16[4,288,128]{2,1,0:T(8,128)(2,1)S(1)}, bf16[4,288,128]{2,1,0:T(8,128)(2,1)S(1)}, u32[]{:S(2)}, u32[]{:S(2)}) collective-permute-start(bf16[4,288,128]{2,1,0:T(8,128)(2,1)S(1)} %get-tuple-element.45), channel_id=1, source_target_pairs={{0,1},{1,0},{2,3},{3,2},{4,5},{5,4},{6,7},{7,6},{8,9},{9,8},{10,11... | collective-permute-start | bytes 884744 | tf_op jit(solution)/shard_map/ppermute | solution.py:311
  35.0 1.6 %collective-permute-start.17 = (bf16[4,288,128]{2,1,0:T(8,128)(2,1)S(1)}, bf16[4,288,128]{2,1,0:T(8,128)(2,1)S(1)}, u32[]{:S(2)}, u32[]{:S(2)}) collective-permute-start(bf16[4,288,128]{2,1,0:T(8,128)(2,1)S(1)} %get-tuple-element.46), channel_id=1, source_target_pairs={{0,1},{1,0},{2,3},{3,2},{4,5},{5,4},{6,7},{7,6},{8,9},{9,8},{10,11... | collective-permute-start | bytes 884744 | tf_op jit(solution)/shard_map/ppermute | solution.py:311

commit v5 on v4

--- a/solution.py
+++ b/solution.py
@@ -143,11 +143,24 @@
             part_ref[n, i] = part
 
 
-def outgoing_kernel(left_ref, piece_ref, part_ref):
+def outgoing_last_kernel(last, rows, at_ref, normed_ref, mask_ref, edge_w_ref, edge_bias_ref, *refs):
+    before_ref, right_ref = refs
+    count = before_ref.shape[0]
+    side = normed_ref.shape[0] // rows
+    right_ref[:count] = before_ref[...]
+    edges(
+        normed_ref, right_ref.at[count], (at_ref[0] ^ last) * rows, side,
+        mask_ref, edge_w_ref, edge_bias_ref, 0, 2,
+    )
+
+
+def outgoing_kernel(left_ref, piece_ref, last_ref, part_ref):
     rows = part_ref.shape[1]
     side = left_ref.shape[0] // rows
-    for n in range(piece_ref.shape[0]):
-        for i, part in enumerate(piece_products(left_ref, piece_ref.at[n], rows, side)):
+    count = piece_ref.shape[0]
+    pieces = [piece_ref.at[n] for n in range(count)] + [last_ref.at[last_ref.shape[0] - 1]]
+    for n, piece in enumerate(pieces):
+        for i, part in enumerate(piece_products(left_ref, piece, rows, side)):
             part_ref[n, i] = part
 
 
@@ -208,6 +221,32 @@
         pl.loop(0, side // CHUNK)(lambda n: columns(pl.multiple_of(n * CHUNK, CHUNK)))
 
 
+def form_incoming(held, me, normed, out_refs, mask_ref, edge_w_ref, edge_bias_ref, rows, side):
+    chip = me >> 1
+    hidden = out_refs[0].shape[1]
+    columns, places = [], []
+    for s, normed_ref, out_ref in zip(held, normed, out_refs):
+        edges(
+            normed_ref, out_ref.at[pl.ds(0, rows * side)], (me ^ s) * rows, side,
+            mask_ref, edge_w_ref, edge_bias_ref, 1, 2,
+        )
+        for a in range(rows):
+            both = normed_ref[pl.ds(pl.multiple_of(a * side + (chip >> 1) * 16, 16), 16), :]
+            both = both.astype(F32)
+            columns.append(jnp.where(chip & 1 == 0, both[:8], both[8:]))
+            places.append(jnp.full((8, hidden), (me ^ s) * rows + a, jnp.int32))
+    left = gated(
+        jnp.concatenate(columns, 0).astype(BF16), edge_w_ref, edge_bias_ref, 1, 0, hidden
+    )
+    column = chip * 8 + lax.broadcasted_iota(jnp.int32, left.shape, 0) % 8
+    left = masked(left, jnp.concatenate(places, 0), column, mask_ref)
+    left = left.reshape(len(held) * rows, 8, hidden)
+    left = jnp.where(me & 1 == 0, left, pltpu.roll(left, rows, 1))
+    left = left.reshape(len(held), rows * 8, hidden).astype(BF16)
+    for n, out_ref in enumerate(out_refs):
+        out_ref[rows * side :, :] = left[n]
+
+
 def incoming_edges_kernel(held, at_ref, *refs):
     normed, refs = refs[: len(held)], refs[len(held) :]
     mask_ref, edge_w_ref, edge_bias_ref, *refs = refs
@@ -217,40 +256,32 @@
     else:
         before_ref, out_ref, x_ref, left_scr = refs
     rows, side, hidden = x_ref.shape
-    me = at_ref[0]
-    chip = me >> 1
-    columns, places = [], []
-    for n, s in enumerate(held):
-        edges(
-            normed[n], out_ref.at[n, pl.ds(0, rows * side)], (me ^ s) * rows, side,
-            mask_ref, edge_w_ref, edge_bias_ref, 1, 2,
-        )
-        for a in range(rows):
-            both = normed[n][pl.ds(pl.multiple_of(a * side + (chip >> 1) * 16, 16), 16), :]
-            both = both.astype(F32)
-            columns.append(jnp.where(chip & 1 == 0, both[:8], both[8:]))
-            places.append(jnp.full((8, hidden), (me ^ s) * rows + a, jnp.int32))
-    left = gated(
-        jnp.concatenate(columns, 0).astype(BF16), edge_w_ref, edge_bias_ref, 1, 0, hidden
-    )
-    column = chip * 8 + lax.broadcasted_iota(jnp.int32, left.shape, 0) % 8
-    left = masked(left, jnp.concatenate(places, 0), column, mask_ref)
-    left = left.reshape(len(held) * rows, 8, hidden)
-    left = jnp.where(me & 1 == 0, left, pltpu.roll(left, rows, 1))
-    left = left.reshape(len(held), rows * 8, hidden).astype(BF16)
-    for n in range(len(held)):
-        out_ref[n, rows * side :, :] = left[n]
+    outs = [out_ref.at[n] for n in range(len(held))]
+    form_incoming(
+        held, at_ref[0], normed, outs, mask_ref, edge_w_ref, edge_bias_ref, rows, side
+    )
 
     def start(i, at):
         if held[0] == 0:
             return jnp.zeros((CHUNK, hidden), F32)
         return before_ref[i, pl.ds(at, CHUNK), :]
 
-    add_pieces([(out_ref.at[n], 0) for n in range(len(held))], left_scr, x_ref, start)
-
-
-def incoming_kernel(before_ref, piece_ref, x_ref, left_scr):
+    add_pieces([(out, 0) for out in outs], left_scr, x_ref, start)
+
+
+def incoming_last_kernel(last, rows, at_ref, normed_ref, mask_ref, edge_w_ref, edge_bias_ref, *refs):
+    before_ref, out_ref = refs
+    count = before_ref.shape[0]
+    out_ref[:count] = before_ref[...]
+    form_incoming(
+        [last], at_ref[0], [normed_ref], [out_ref.at[count]],
+        mask_ref, edge_w_ref, edge_bias_ref, rows, normed_ref.shape[0] // rows,
+    )
+
+
+def incoming_kernel(before_ref, piece_ref, last_ref, x_ref, left_scr):
     pieces = [(piece_ref.at[n], 1) for n in range(piece_ref.shape[0])]
+    pieces.append((last_ref.at[last_ref.shape[0] - 1], 0))
     add_pieces(pieces, left_scr, x_ref, lambda i, at: before_ref[i, pl.ds(at, CHUNK), :])
 
 
@@ -320,9 +351,10 @@
 
     groups = (
         [PLANE * k for k in range(planes)],
-        [2] + [PLANE * k + 2 for k in range(planes - 1, 0, -1)],
-    )
-    came = [[s ^ 1 for s in group] for group in groups]
+        [2] + [PLANE * k + 2 for k in range(planes - 1, 0, -1) if k != 2],
+    )
+    last = PLANE * min(2, planes - 1) + 2
+    came = [[s ^ 1 for s in groups[0]], [s ^ 1 for s in groups[1] + [last]]]
 
     def work(pieces):
         return 2 * pieces * count * rows * hidden
@@ -342,11 +374,17 @@
         if rest:
             left, gate = rest
         parts.append(part)
-        others.append(swap(right, 1))
-    known = [*groups, came[0]]
+        if group[0] == 0:
+            others.append(swap(right, 1))
+    (right,) = call(
+        functools.partial(outgoing_last_kernel, last, rows), "outgoing_last",
+        [((planes, count, hidden), BF16)], pieces[last], *weights, right, scalar=me,
+    )
+    others.append(swap(right, 1))
+    known = [*groups, came[0] + [last]]
     (part,) = call(
-        outgoing_kernel, "outgoing", [((planes, rows, 8, hidden), F32)],
-        left, others[0], flops=work(planes),
+        outgoing_kernel, "outgoing", [((planes + 1, rows, 8, hidden), F32)],
+        left, others[0], right, flops=work(planes + 1),
     )
     first, normed = call(
         functools.partial(outgoing_finish_kernel, came[1], known), "outgoing_finish",
@@ -369,10 +407,15 @@
         )
         if group[0] == 0:
             gate = x.pop()
-        others.append(swap(edge, 1))
+            others.append(swap(edge, 1))
+    (edge,) = call(
+        functools.partial(incoming_last_kernel, last, rows), "incoming_last",
+        [((planes, span, hidden), BF16)], pieces[last], *weights, edge, scalar=me,
+    )
+    others.append(swap(edge, 1))
     x = call(
-        incoming_kernel, "incoming", [((rows, side, hidden), F32)], *x, others[0],
-        scratch=[((planes, 2 * rows * rows, hidden), F32)], flops=work(planes),
+        incoming_kernel, "incoming", [((rows, side, hidden), F32)], *x, others[0], edge,
+        scratch=[((planes + 1, 2 * rows * rows, hidden), F32)], flops=work(planes + 1),
     )
     (out,) = call(
         incoming_finish_kernel, "incoming_finish", [(pair.shape, F32)],

time: 37.9 us -> 36.4 us (0.960)
  waiting for transfers between devices: 12.8 us -> 10 us
  starting transfers between devices: 19.1 us -> 20.1 us
    ppermute x18, waiting for transfers between devices: 12.8 us -> 10 us  [swap(): lax.ppermute(piece, 'dap', [(device, device ^ bits) for device in range(d...]
    ppermute x18, starting transfers between devices: 19.1 us -> 20.1 us  [swap(): lax.ppermute(piece, 'dap', [(device, device ^ bits) for device in range(d...]
    pallas_call x8 -> x10, Pallas kernels: 4.53 us -> 4.8 us  [call(): pl.pallas_call(kernel, in_specs=[SMEM] * (scalar is not None) + [VMEM] *...]
  transfers between devices with their start and end apart: 18 -> 18, of which waited for: 9 -> 10; matrix products, arithmetic and copies ran while one was open for 0% -> 0% of each run, Pallas kernels for 7% -> 8%
where the time goes in v5:
time: 36.4 us; the launch traced here: 36.2 us
  starting transfers between devices  20.1 us (55%)
  waiting for transfers between devices  10 us (27%)
  Pallas kernels  5.98 us (16%)
    ppermute x18, starting transfers between devices, swap(): lax.ppermute(piece, 'dap', [(device, device ^ bits) for device in range(d...  20.1 us
    ppermute x18, waiting for transfers between devices, swap(): lax.ppermute(piece, 'dap', [(device, device ^ bits) for device in range(d...  10 us
    pallas_call x10, Pallas kernels, call(): pl.pallas_call(kernel, in_specs=[SMEM] * (scalar is not None) + [VMEM] *...  4.8 us
    pallas_call x1, Pallas kernels, body(): pl.pallas_call(norm_kernel, in_specs=[pl.BlockSpec(memory_space=pltpu.HBM...  1.18 us
  transfers between devices with their start and end apart: 18, of which 10 were waited for; matrix products, arithmetic and copies ran while one was open for 0% of the time, Pallas kernels for 8%

profile of v5, /device:TPU:0, one launch (start us, length us, event | category | flops | bytes accessed | tf_op | source)
XLA Modules:
  0.0 36.2 jit_solution(7704232992039607576)
XLA Ops:
  0.0 1.2 %norm.1 = (f32[4,64,128]{2,1,0:T(8,128)S(1)}, f32[2,2,128]{2,1,0:T(2,128)S(1)}, f32[2,2,128]{2,1,0:T(2,128)S(1)}, s32[1,64]{1,0:T(1,128)S(1)}, bf16[2,128,640]{2...) custom-call(f32[4,64,128]{2,1,0:T(8,128)} %refs_0_.1, ...), custom_call_target="tpu_custom_call" | custom-call | tf_op jit(solution)/shard_map/norm/pallas_call | solution.py:326
  1.2 5.1 %collective-permute-start.3 = (bf16[256,128]{1,0:T(8,128)(2,1)S(1)}, bf16[256,128]{1,0:T(8,128)(2,1)S(1)}, u32[]{:S(2)}, u32[]{:S(2)}) collective-permute-start(bf16[256,128]{1,0:T(8,128)(2,1)S(1)} %get-tuple-element.27.refs_0_), channel_id=1, source_target_pairs={{0,12},{1,13},{2,14},{3,15},{4,8},{5,9},{6,10},{7,11},{8,4},{9,5},... | collective-permute-start | bytes 196616 | tf_op jit(solution)/shard_map/ppermute | solution.py:342
  6.3 0.6 %collective-permute-start = (bf16[256,128]{1,0:T(8,128)(2,1)S(1)}, bf16[256,128]{1,0:T(8,128)(2,1)S(1)}, u32[]{:S(2)}, u32[]{:S(2)}) collective-permute-start(bf16[256,128]{1,0:T(8,128)(2,1)S(1)} %get-tuple-element.27.refs_0_), channel_id=1, source_target_pairs={{0,8},{1,9},{2,10},{3,11},{4,12},{5,13},{6,14},{7,15},{8,0},{9,1},... | collective-permute-start | bytes 196616 | tf_op jit(solution)/shard_map/ppermute | solution.py:342
  7.0 1.7 %collective-permute-start.2 = (bf16[256,128]{1,0:T(8,128)(2,1)S(1)}, bf16[256,128]{1,0:T(8,128)(2,1)S(1)}, u32[]{:S(2)}, u32[]{:S(2)}) collective-permute-start(bf16[256,128]{1,0:T(8,128)(2,1)S(1)} %get-tuple-element.27.refs_0_), channel_id=1, source_target_pairs={{0,2},{1,3},{2,0},{3,1},{4,6},{5,7},{6,4},{7,5},{8,10},{9,11},{10,... | collective-permute-start | bytes 196616 | tf_op jit(solution)/shard_map/ppermute | solution.py:342
  8.6 0.6 %collective-permute-done.3.refs_3_ = bf16[256,128]{1,0:T(8,128)(2,1)S(1)} collective-permute-done((bf16[256,128]{1,0:T(8,128)(2,1)S(1)}, bf16[256,128]{1,0:T(8,128)(2,1)S(1)}, u32[]{:S(2)}, u32[]{:S(2)}) %collective-permute-start.3) | collective-permute-done | bytes 65568 | tf_op jit(solution)/shard_map/ppermute | solution.py:342
  9.2 1.5 %collective-permute-start.4 = (bf16[256,128]{1,0:T(8,128)(2,1)S(1)}, bf16[256,128]{1,0:T(8,128)(2,1)S(1)}, u32[]{:S(2)}, u32[]{:S(2)}) collective-permute-start(bf16[256,128]{1,0:T(8,128)(2,1)S(1)} %collective-permute-done.3.refs_3_), channel_id=1, source_target_pairs={{0,2},{1,3},{2,0},{3,1},{4,6},{5,7},{6,4},{7,5},{8,10},{9,11},{10,... | collective-permute-start | bytes 196616 | tf_op jit(solution)/shard_map/ppermute | solution.py:342
  11.0 1.7 %collective-permute-start.6 = (bf16[256,128]{1,0:T(8,128)(2,1)S(1)}, bf16[256,128]{1,0:T(8,128)(2,1)S(1)}, u32[]{:S(2)}, u32[]{:S(2)}) collective-permute-start(bf16[256,128]{1,0:T(8,128)(2,1)S(1)} %collective-permute-done.5.refs_1_), channel_id=1, source_target_pairs={{0,2},{1,3},{2,0},{3,1},{4,6},{5,7},{6,4},{7,5},{8,10},{9,11},{10,... | collective-permute-start | bytes 196616 | tf_op jit(solution)/shard_map/ppermute | solution.py:342
  12.6 0.8 %collective-permute-start.1 = (bf16[256,128]{1,0:T(8,128)(2,1)S(1)}, bf16[256,128]{1,0:T(8,128)(2,1)S(1)}, u32[]{:S(2)}, u32[]{:S(2)}) collective-permute-start(bf16[256,128]{1,0:T(8,128)(2,1)S(1)} %collective-permute-done.refs_2_), channel_id=1, source_target_pairs={{0,2},{1,3},{2,0},{3,1},{4,6},{5,7},{6,4},{7,5},{8,10},{9,11},{10,... | collective-permute-start | bytes 196616 | tf_op jit(solution)/shard_map/ppermute | solution.py:342
  13.5 0.6 %outgoing_edges.2 = (bf16[4,256,128]{2,1,0:T(8,128)(2,1)S(1)}, f32[4,4,8,128]{3,2,1,0:T(8,128)S(1)}, f32[256,128]{1,0:T(8,128)S(1)}, f32[256,128]{1,0:T(8,128)S(1)}) custom-call(s32[1]{0:T(128)} %bitcast.at_ref, bf16[256,128]{1,0:T(8,128)(2,1)S(1)} %get-tuple-element.27.refs_0_, bf16[256,128]{1,0:T(8,128)(2,1)S(1)} %collective-permute-done.5.refs_1_, ...), custom_call_target="tpu_custom_call" | custom-call | flops 1048576 | bytes 16384 | tf_op jit(solution)/shard_map/outgoing_edges/pallas_call | solution.py:305
  14.2 1.7 %collective-permute-done.6.refs_2_ = bf16[256,128]{1,0:T(8,128)(2,1)S(1)} collective-permute-done((bf16[256,128]{1,0:T(8,128)(2,1)S(1)}, bf16[256,128]{1,0:T(8,128)(2,1)S(1)}, u32[]{:S(2)}, u32[]{:S(2)}) %collective-permute-start.6) | collective-permute-done | bytes 65568 | tf_op jit(solution)/shard_map/ppermute | solution.py:342
  16.4 0.5 %collective-permute-done.1.normed_ref = bf16[256,128]{1,0:T(8,128)(2,1)S(1)} collective-permute-done((bf16[256,128]{1,0:T(8,128)(2,1)S(1)}, bf16[256,128]{1,0:T(8,128)(2,1)S(1)}, u32[]{:S(2)}, u32[]{:S(2)}) %collective-permute-start.1) | collective-permute-done | bytes 65568 | tf_op jit(solution)/shard_map/ppermute | solution.py:342
  17.4 1.3 %collective-permute-done.7.piece_ref = bf16[4,256,128]{2,1,0:T(8,128)(2,1)S(1)} collective-permute-done((bf16[4,256,128]{2,1,0:T(8,128)(2,1)S(1)}, bf16[4,256,128]{2,1,0:T(8,128)(2,1)S(1)}, u32[]{:S(2)}, u32[]{:S(2)}) %collective-permute-start.7) | collective-permute-done | bytes 262176 | tf_op jit(solution)/shard_map/ppermute | solution.py:342
  18.7 0.7 %outgoing_finish.1 = (f32[256,128]{1,0:T(8,128)S(1)}, bf16[256,128]{1,0:T(8,128)(2,1)S(1)}) custom-call(s32[1]{0:T(128)} %bitcast.at_ref, bf16[4,256,128]{2,1,0:T(8,128)(2,1)S(1)} %collective-permute-done.7.piece_ref, f32[4,4,8,128]{3,2,1,0:T(8,128)S(1)} %get-tuple-element.33.refs_0_, f32[3,4,8,128]{3,2,1,0:T(8,128)S(1)} %get-tuple-element.34.refs_1_, ...), custom_call_target="tpu_custom_call" | custom-call | tf_op jit(solution)/shard_map/outgoing_finish/pallas_call | solution.py:305
  19.4 2.8 %collective-permute-start.10 = (bf16[256,128]{1,0:T(8,128)(2,1)S(1)}, bf16[256,128]{1,0:T(8,128)(2,1)S(1)}, u32[]{:S(2)}, u32[]{:S(2)}) collective-permute-start(bf16[256,128]{1,0:T(8,128)(2,1)S(1)} %get-tuple-element.42.refs_0_), channel_id=1, source_target_pairs={{0,12},{1,13},{2,14},{3,15},{4,8},{5,9},{6,10},{7,11},{8,4},{9,5},... | collective-permute-start | bytes 196616 | tf_op jit(solution)/shard_map/ppermute | solution.py:342
  22.2 1.7 %collective-permute-start.14 = (bf16[256,128]{1,0:T(8,128)(2,1)S(1)}, bf16[256,128]{1,0:T(8,128)(2,1)S(1)}, u32[]{:S(2)}, u32[]{:S(2)}) collective-permute-start(bf16[256,128]{1,0:T(8,128)(2,1)S(1)} %get-tuple-element.42.refs_0_), channel_id=1, source_target_pairs={{0,8},{1,9},{2,10},{3,11},{4,12},{5,13},{6,14},{7,15},{8,0},{9,1},... | collective-permute-start | bytes 196616 | tf_op jit(solution)/shard_map/ppermute | solution.py:342
  23.8 0.9 %collective-permute-start.9 = (bf16[256,128]{1,0:T(8,128)(2,1)S(1)}, bf16[256,128]{1,0:T(8,128)(2,1)S(1)}, u32[]{:S(2)}, u32[]{:S(2)}) collective-permute-start(bf16[256,128]{1,0:T(8,128)(2,1)S(1)} %get-tuple-element.42.refs_0_), channel_id=1, source_target_pairs={{0,2},{1,3},{2,0},{3,1},{4,6},{5,7},{6,4},{7,5},{8,10},{9,11},{10,... | collective-permute-start | bytes 196616 | tf_op jit(solution)/shard_map/ppermute | solution.py:342
  24.8 1.4 %collective-permute-done.10.refs_3_ = bf16[256,128]{1,0:T(8,128)(2,1)S(1)} collective-permute-done((bf16[256,128]{1,0:T(8,128)(2,1)S(1)}, bf16[256,128]{1,0:T(8,128)(2,1)S(1)}, u32[]{:S(2)}, u32[]{:S(2)}) %collective-permute-start.10) | collective-permute-done | bytes 65568 | tf_op jit(solution)/shard_map/ppermute | solution.py:342
  26.2 1.0 %collective-permute-start.11 = (bf16[256,128]{1,0:T(8,128)(2,1)S(1)}, bf16[256,128]{1,0:T(8,128)(2,1)S(1)}, u32[]{:S(2)}, u32[]{:S(2)}) collective-permute-start(bf16[256,128]{1,0:T(8,128)(2,1)S(1)} %collective-permute-done.10.refs_3_), channel_id=1, source_target_pairs={{0,2},{1,3},{2,0},{3,1},{4,6},{5,7},{6,4},{7,5},{8,10},{9,11},{10,... | collective-permute-start | bytes 196616 | tf_op jit(solution)/shard_map/ppermute | solution.py:342
  27.1 1.2 %collective-permute-done.12.refs_1_ = bf16[256,128]{1,0:T(8,128)(2,1)S(1)} collective-permute-done((bf16[256,128]{1,0:T(8,128)(2,1)S(1)}, bf16[256,128]{1,0:T(8,128)(2,1)S(1)}, u32[]{:S(2)}, u32[]{:S(2)}) %collective-permute-start.12) | collective-permute-done | bytes 65568 | tf_op jit(solution)/shard_map/ppermute | solution.py:342
  28.8 1.5 %collective-permute-start.16 = (bf16[256,128]{1,0:T(8,128)(2,1)S(1)}, bf16[256,128]{1,0:T(8,128)(2,1)S(1)}, u32[]{:S(2)}, u32[]{:S(2)}) collective-permute-start(bf16[256,128]{1,0:T(8,128)(2,1)S(1)} %collective-permute-done.14.refs_2_), channel_id=1, source_target_pairs={{0,2},{1,3},{2,0},{3,1},{4,6},{5,7},{6,4},{7,5},{8,10},{9,11},{10,... | collective-permute-start | bytes 196616 | tf_op jit(solution)/shard_map/ppermute | solution.py:342
  30.3 0.6 %incoming_edges.2 = (bf16[4,288,128]{2,1,0:T(8,128)(2,1)S(1)}, f32[4,64,128]{2,1,0:T(8,128)S(1)}, f32[256,128]{1,0:T(8,128)S(1)}) custom-call(s32[1]{0:T(128)} %bitcast.at_ref, bf16[256,128]{1,0:T(8,128)(2,1)S(1)} %get-tuple-element.42.refs_0_, bf16[256,128]{1,0:T(8,128)(2,1)S(1)} %collective-permute-done.12.refs_1_, ...), custom_call_target="tpu_custom_call" | custom-call | flops 1048576 | bytes 16384 | tf_op jit(solution)/shard_map/incoming_edges/pallas_call | solution.py:305
  31.0 1.5 %collective-permute-done.13.refs_2_ = bf16[256,128]{1,0:T(8,128)(2,1)S(1)} collective-permute-done((bf16[256,128]{1,0:T(8,128)(2,1)S(1)}, bf16[256,128]{1,0:T(8,128)(2,1)S(1)}, u32[]{:S(2)}, u32[]{:S(2)}) %collective-permute-start.13) | collective-permute-done | bytes 65568 | tf_op jit(solution)/shard_map/ppermute | solution.py:342
  33.8 1.4 %collective-permute-done.17.piece_ref = bf16[4,288,128]{2,1,0:T(8,128)(2,1)S(1)} collective-permute-done((bf16[4,288,128]{2,1,0:T(8,128)(2,1)S(1)}, bf16[4,288,128]{2,1,0:T(8,128)(2,1)S(1)}, u32[]{:S(2)}, u32[]{:S(2)}) %collective-permute-start.17) | collective-permute-done | bytes 294944 | tf_op jit(solution)/shard_map/ppermute | solution.py:342
  35.1 1.1 %incoming_finish.1 = f32[4,64,128]{2,1,0:T(8,128)} custom-call(f32[4,64,128]{2,1,0:T(8,128)S(1)} %incoming.1.before_ref, bf16[4,288,128]{2,1,0:T(8,128)(2,1)S(1)} %collective-permute-done.17.piece_ref, f32[256,128]{1,0:T(8,128)S(1)} %get-tuple-element.47.first_ref, f32[256,128]{1,0:T(8,128)S(1)} %get-tuple-element.48.gate_ref, ...), custom_call_target="tpu_custom_call" | custom-call | tf_op jit(solution)/shard_map/incoming_finish/pallas_call | solution.py:305
  (23 shorter events, 3.0 us)
Async XLA Ops:
  1.2 8.0 %collective-permute-start.3 = (bf16[256,128]{1,0:T(8,128)(2,1)S(1)}, bf16[256,128]{1,0:T(8,128)(2,1)S(1)}, u32[]{:S(2)}, u32[]{:S(2)}) collective-permute-start(bf16[256,128]{1,0:T(8,128)(2,1)S(1)} %get-tuple-element.27.refs_0_), channel_id=1, source_target_pairs={{0,12},{1,13},{2,14},{3,15},{4,8},{5,9},{6,10},{7,11},{8,4},{9,5},... | collective-permute-start | bytes 196616 | tf_op jit(solution)/shard_map/ppermute | solution.py:342
  6.3 4.7 %collective-permute-start.5 = (bf16[256,128]{1,0:T(8,128)(2,1)S(1)}, bf16[256,128]{1,0:T(8,128)(2,1)S(1)}, u32[]{:S(2)}, u32[]{:S(2)}) collective-permute-start(bf16[256,128]{1,0:T(8,128)(2,1)S(1)} %get-tuple-element.27.refs_0_), channel_id=1, source_target_pairs={{0,4},{1,5},{2,6},{3,7},{4,0},{5,1},{6,2},{7,3},{8,12},{9,13},{10,... | collective-permute-start | bytes 196616 | tf_op jit(solution)/shard_map/ppermute | solution.py:342
  6.3 6.3 %collective-permute-start = (bf16[256,128]{1,0:T(8,128)(2,1)S(1)}, bf16[256,128]{1,0:T(8,128)(2,1)S(1)}, u32[]{:S(2)}, u32[]{:S(2)}) collective-permute-start(bf16[256,128]{1,0:T(8,128)(2,1)S(1)} %get-tuple-element.27.refs_0_), channel_id=1, source_target_pairs={{0,8},{1,9},{2,10},{3,11},{4,12},{5,13},{6,14},{7,15},{8,0},{9,1},... | collective-permute-start | bytes 196616 | tf_op jit(solution)/shard_map/ppermute | solution.py:342
  7.0 7.2 %collective-permute-start.2 = (bf16[256,128]{1,0:T(8,128)(2,1)S(1)}, bf16[256,128]{1,0:T(8,128)(2,1)S(1)}, u32[]{:S(2)}, u32[]{:S(2)}) collective-permute-start(bf16[256,128]{1,0:T(8,128)(2,1)S(1)} %get-tuple-element.27.refs_0_), channel_id=1, source_target_pairs={{0,2},{1,3},{2,0},{3,1},{4,6},{5,7},{6,4},{7,5},{8,10},{9,11},{10,... | collective-permute-start | bytes 196616 | tf_op jit(solution)/shard_map/ppermute | solution.py:342
  9.2 5.0 %collective-permute-start.4 = (bf16[256,128]{1,0:T(8,128)(2,1)S(1)}, bf16[256,128]{1,0:T(8,128)(2,1)S(1)}, u32[]{:S(2)}, u32[]{:S(2)}) collective-permute-start(bf16[256,128]{1,0:T(8,128)(2,1)S(1)} %collective-permute-done.3.refs_3_), channel_id=1, source_target_pairs={{0,2},{1,3},{2,0},{3,1},{4,6},{5,7},{6,4},{7,5},{8,10},{9,11},{10,... | collective-permute-start | bytes 196616 | tf_op jit(solution)/shard_map/ppermute | solution.py:342
  11.0 5.0 %collective-permute-start.6 = (bf16[256,128]{1,0:T(8,128)(2,1)S(1)}, bf16[256,128]{1,0:T(8,128)(2,1)S(1)}, u32[]{:S(2)}, u32[]{:S(2)}) collective-permute-start(bf16[256,128]{1,0:T(8,128)(2,1)S(1)} %collective-permute-done.5.refs_1_), channel_id=1, source_target_pairs={{0,2},{1,3},{2,0},{3,1},{4,6},{5,7},{6,4},{7,5},{8,10},{9,11},{10,... | collective-permute-start | bytes 196616 | tf_op jit(solution)/shard_map/ppermute | solution.py:342
  12.6 4.3 %collective-permute-start.1 = (bf16[256,128]{1,0:T(8,128)(2,1)S(1)}, bf16[256,128]{1,0:T(8,128)(2,1)S(1)}, u32[]{:S(2)}, u32[]{:S(2)}) collective-permute-start(bf16[256,128]{1,0:T(8,128)(2,1)S(1)} %collective-permute-done.refs_2_), channel_id=1, source_target_pairs={{0,2},{1,3},{2,0},{3,1},{4,6},{5,7},{6,4},{7,5},{8,10},{9,11},{10,... | collective-permute-start | bytes 196616 | tf_op jit(solution)/shard_map/ppermute | solution.py:342
  14.1 3.1 %collective-permute-start.8 = (bf16[4,256,128]{2,1,0:T(8,128)(2,1)S(1)}, bf16[4,256,128]{2,1,0:T(8,128)(2,1)S(1)}, u32[]{:S(2)}, u32[]{:S(2)}) collective-permute-start(bf16[4,256,128]{2,1,0:T(8,128)(2,1)S(1)} %get-tuple-element.35), channel_id=1, source_target_pairs={{0,1},{1,0},{2,3},{3,2},{4,5},{5,4},{6,7},{7,6},{8,9},{9,8},{10,11... | collective-permute-start | bytes 786440 | tf_op jit(solution)/shard_map/ppermute | solution.py:342
  17.1 1.6 %collective-permute-start.7 = (bf16[4,256,128]{2,1,0:T(8,128)(2,1)S(1)}, bf16[4,256,128]{2,1,0:T(8,128)(2,1)S(1)}, u32[]{:S(2)}, u32[]{:S(2)}) collective-permute-start(bf16[4,256,128]{2,1,0:T(8,128)(2,1)S(1)} %outgoing_last.1.last_ref), channel_id=1, source_target_pairs={{0,1},{1,0},{2,3},{3,2},{4,5},{5,4},{6,7},{7,6},{8,9},{9,8},{10,11... | collective-permute-start | bytes 786440 | tf_op jit(solution)/shard_map/ppermute | solution.py:342
  19.4 6.8 %collective-permute-start.10 = (bf16[256,128]{1,0:T(8,128)(2,1)S(1)}, bf16[256,128]{1,0:T(8,128)(2,1)S(1)}, u32[]{:S(2)}, u32[]{:S(2)}) collective-permute-start(bf16[256,128]{1,0:T(8,128)(2,1)S(1)} %get-tuple-element.42.refs_0_), channel_id=1, source_target_pairs={{0,12},{1,13},{2,14},{3,15},{4,8},{5,9},{6,10},{7,11},{8,4},{9,5},... | collective-permute-start | bytes 196616 | tf_op jit(solution)/shard_map/ppermute | solution.py:342
  22.2 6.1 %collective-permute-start.12 = (bf16[256,128]{1,0:T(8,128)(2,1)S(1)}, bf16[256,128]{1,0:T(8,128)(2,1)S(1)}, u32[]{:S(2)}, u32[]{:S(2)}) collective-permute-start(bf16[256,128]{1,0:T(8,128)(2,1)S(1)} %get-tuple-element.42.refs_0_), channel_id=1, source_target_pairs={{0,4},{1,5},{2,6},{3,7},{4,0},{5,1},{6,2},{7,3},{8,12},{9,13},{10,... | collective-permute-start | bytes 196616 | tf_op jit(solution)/shard_map/ppermute | solution.py:342
  22.2 6.6 %collective-permute-start.14 = (bf16[256,128]{1,0:T(8,128)(2,1)S(1)}, bf16[256,128]{1,0:T(8,128)(2,1)S(1)}, u32[]{:S(2)}, u32[]{:S(2)}) collective-permute-start(bf16[256,128]{1,0:T(8,128)(2,1)S(1)} %get-tuple-element.42.refs_0_), channel_id=1, source_target_pairs={{0,8},{1,9},{2,10},{3,11},{4,12},{5,13},{6,14},{7,15},{8,0},{9,1},... | collective-permute-start | bytes 196616 | tf_op jit(solution)/shard_map/ppermute | solution.py:342
  23.8 7.2 %collective-permute-start.9 = (bf16[256,128]{1,0:T(8,128)(2,1)S(1)}, bf16[256,128]{1,0:T(8,128)(2,1)S(1)}, u32[]{:S(2)}, u32[]{:S(2)}) collective-permute-start(bf16[256,128]{1,0:T(8,128)(2,1)S(1)} %get-tuple-element.42.refs_0_), channel_id=1, source_target_pairs={{0,2},{1,3},{2,0},{3,1},{4,6},{5,7},{6,4},{7,5},{8,10},{9,11},{10,... | collective-permute-start | bytes 196616 | tf_op jit(solution)/shard_map/ppermute | solution.py:342
  26.2 4.9 %collective-permute-start.11 = (bf16[256,128]{1,0:T(8,128)(2,1)S(1)}, bf16[256,128]{1,0:T(8,128)(2,1)S(1)}, u32[]{:S(2)}, u32[]{:S(2)}) collective-permute-start(bf16[256,128]{1,0:T(8,128)(2,1)S(1)} %collective-permute-done.10.refs_3_), channel_id=1, source_target_pairs={{0,2},{1,3},{2,0},{3,1},{4,6},{5,7},{6,4},{7,5},{8,10},{9,11},{10,... | collective-permute-start | bytes 196616 | tf_op jit(solution)/shard_map/ppermute | solution.py:342
  28.3 4.3 %collective-permute-start.13 = (bf16[256,128]{1,0:T(8,128)(2,1)S(1)}, bf16[256,128]{1,0:T(8,128)(2,1)S(1)}, u32[]{:S(2)}, u32[]{:S(2)}) collective-permute-start(bf16[256,128]{1,0:T(8,128)(2,1)S(1)} %collective-permute-done.12.refs_1_), channel_id=1, source_target_pairs={{0,2},{1,3},{2,0},{3,1},{4,6},{5,7},{6,4},{7,5},{8,10},{9,11},{10,... | collective-permute-start | bytes 196616 | tf_op jit(solution)/shard_map/ppermute | solution.py:342
  28.8 4.5 %collective-permute-start.16 = (bf16[256,128]{1,0:T(8,128)(2,1)S(1)}, bf16[256,128]{1,0:T(8,128)(2,1)S(1)}, u32[]{:S(2)}, u32[]{:S(2)}) collective-permute-start(bf16[256,128]{1,0:T(8,128)(2,1)S(1)} %collective-permute-done.14.refs_2_), channel_id=1, source_target_pairs={{0,2},{1,3},{2,0},{3,1},{4,6},{5,7},{6,4},{7,5},{8,10},{9,11},{10,... | collective-permute-start | bytes 196616 | tf_op jit(solution)/shard_map/ppermute | solution.py:342
  30.9 2.6 %collective-permute-start.15 = (bf16[4,288,128]{2,1,0:T(8,128)(2,1)S(1)}, bf16[4,288,128]{2,1,0:T(8,128)(2,1)S(1)}, u32[]{:S(2)}, u32[]{:S(2)}) collective-permute-start(bf16[4,288,128]{2,1,0:T(8,128)(2,1)S(1)} %get-tuple-element.45), channel_id=1, source_target_pairs={{0,1},{1,0},{2,3},{3,2},{4,5},{5,4},{6,7},{7,6},{8,9},{9,8},{10,11... | collective-permute-start | bytes 884744 | tf_op jit(solution)/shard_map/ppermute | solution.py:342
  33.5 1.6 %collective-permute-start.17 = (bf16[4,288,128]{2,1,0:T(8,128)(2,1)S(1)}, bf16[4,288,128]{2,1,0:T(8,128)(2,1)S(1)}, u32[]{:S(2)}, u32[]{:S(2)}) collective-permute-start(bf16[4,288,128]{2,1,0:T(8,128)(2,1)S(1)} %incoming_last.1.last_ref), channel_id=1, source_target_pairs={{0,1},{1,0},{2,3},{3,2},{4,5},{5,4},{6,7},{7,6},{8,9},{9,8},{10,11... | collective-permute-start | bytes 884744 | tf_op jit(solution)/shard_map/ppermute | solution.py:342

commit v6 on v5

--- a/solution.py
+++ b/solution.py
@@ -15,6 +15,11 @@
 CHUNK = 64
 BLOCK = 256
 PARAMS = pltpu.CompilerParams(vmem_limit_bytes=48 * 1024 * 1024)
+
+
+def source(me, s):
+    turn = PLANE if s >= 2 * PLANE else 0
+    return me ^ s ^ ((me ^ s) & 1) * turn
 
 
 def normalize(values, gain, shift):
@@ -138,7 +143,7 @@
         edges(normed[0], left_ref, at_ref[0] * rows, *shared, 0)
         gate_of(normed[0], gate_ref, edge_w_ref, edge_bias_ref, 0)
     for n, s in enumerate(held):
-        edges(normed[n], right_ref.at[n], (at_ref[0] ^ s) * rows, *shared, 2)
+        edges(normed[n], right_ref.at[n], source(at_ref[0], s) * rows, *shared, 2)
         for i, part in enumerate(piece_products(left_ref, right_ref.at[n], rows, side)):
             part_ref[n, i] = part
 
@@ -149,7 +154,7 @@
     side = normed_ref.shape[0] // rows
     right_ref[:count] = before_ref[...]
     edges(
-        normed_ref, right_ref.at[count], (at_ref[0] ^ last) * rows, side,
+        normed_ref, right_ref.at[count], source(at_ref[0], last) * rows, side,
         mask_ref, edge_w_ref, edge_bias_ref, 0, 2,
     )
 
@@ -184,8 +189,9 @@
         return [ref[n, i] for i in range(rows)]
 
     for s in range(0, len(known) + len(last), 2):
-        at = pl.multiple_of((me >> 1 ^ s >> 1) * 2 * rows, 2 * rows)
-        for i, (a, b) in enumerate(zip(part_of(s), part_of(s + 1))):
+        at = pl.multiple_of((source(me, s) >> 1) * 2 * rows, 2 * rows)
+        other = s + 1 if s < 2 * PLANE else (s ^ PLANE) + 1
+        for i, (a, b) in enumerate(zip(part_of(s), part_of(other))):
             x = merge(low, a, b, 4)
             x = jnp.where(me & 1 == 0, x, pltpu.roll(x, rows, 0))
             x_scr[i, pl.ds(at, 2 * rows), :] = x
@@ -227,14 +233,14 @@
     columns, places = [], []
     for s, normed_ref, out_ref in zip(held, normed, out_refs):
         edges(
-            normed_ref, out_ref.at[pl.ds(0, rows * side)], (me ^ s) * rows, side,
+            normed_ref, out_ref.at[pl.ds(0, rows * side)], source(me, s) * rows, side,
             mask_ref, edge_w_ref, edge_bias_ref, 1, 2,
         )
         for a in range(rows):
             both = normed_ref[pl.ds(pl.multiple_of(a * side + (chip >> 1) * 16, 16), 16), :]
             both = both.astype(F32)
             columns.append(jnp.where(chip & 1 == 0, both[:8], both[8:]))
-            places.append(jnp.full((8, hidden), (me ^ s) * rows + a, jnp.int32))
+            places.append(jnp.full((8, hidden), source(me, s) * rows + a, jnp.int32))
     left = gated(
         jnp.concatenate(columns, 0).astype(BF16), edge_w_ref, edge_bias_ref, 1, 0, hidden
     )
@@ -338,8 +344,8 @@
     weights = (mask, edge_w, edge_bias)
     span = count + 2 * rows * rows
 
-    def swap(piece, bits):
-        return lax.ppermute(piece, "dap", [(device, device ^ bits) for device in range(dap)])
+    def swap(piece, s):
+        return lax.ppermute(piece, "dap", [(source(device, s), device) for device in range(dap)])
 
     def gather(own):
         pieces = {0: own, 2: swap(own, 2)}

time: 36.4 us -> 35.3 us (0.970)
  waiting for transfers between devices: 10 us -> 7.56 us
  starting transfers between devices: 20.1 us -> 21.5 us
    ppermute x18, waiting for transfers between devices: 10 us -> 7.56 us  [swap(): lax.ppermute(piece, 'dap', [(source(device, s), device) for device in ran...]
    ppermute x18, starting transfers between devices: 20.1 us -> 21.5 us  [swap(): lax.ppermute(piece, 'dap', [(source(device, s), device) for device in ran...]
  transfers between devices with their start and end apart: 18 -> 18, of which waited for: 10 -> 9; matrix products, arithmetic and copies ran while one was open for 0% -> 0% of each run, Pallas kernels for 8% -> 8%
where the time goes in v6:
time: 35.3 us; the launch traced here: 35.2 us
  starting transfers between devices  21.5 us (61%)
  waiting for transfers between devices  7.56 us (21%)
  Pallas kernels  5.98 us (17%)
    ppermute x18, starting transfers between devices, swap(): lax.ppermute(piece, 'dap', [(source(device, s), device) for device in ran...  21.5 us
    ppermute x18, waiting for transfers between devices, swap(): lax.ppermute(piece, 'dap', [(source(device, s), device) for device in ran...  7.56 us
    pallas_call x10, Pallas kernels, call(): pl.pallas_call(kernel, in_specs=[SMEM] * (scalar is not None) + [VMEM] *...  4.79 us
    pallas_call x1, Pallas kernels, body(): pl.pallas_call(norm_kernel, in_specs=[pl.BlockSpec(memory_space=pltpu.HBM...  1.18 us
  transfers between devices with their start and end apart: 18, of which 9 were waited for; matrix products, arithmetic and copies ran while one was open for 0% of the time, Pallas kernels for 8%

profile of v6, /device:TPU:0, one launch (start us, length us, event | category | flops | bytes accessed | tf_op | source)
XLA Modules:
  0.0 35.2 jit_solution(11262330259743970918)
XLA Ops:
  0.0 1.2 %norm.1 = (f32[4,64,128]{2,1,0:T(8,128)S(1)}, f32[2,2,128]{2,1,0:T(2,128)S(1)}, f32[2,2,128]{2,1,0:T(2,128)S(1)}, s32[1,64]{1,0:T(1,128)S(1)}, bf16[2,128,640]{2...) custom-call(f32[4,64,128]{2,1,0:T(8,128)} %refs_0_.1, ...), custom_call_target="tpu_custom_call" | custom-call | tf_op jit(solution)/shard_map/norm/pallas_call | solution.py:332
  1.2 5.1 %collective-permute-start.3 = (bf16[256,128]{1,0:T(8,128)(2,1)S(1)}, bf16[256,128]{1,0:T(8,128)(2,1)S(1)}, u32[]{:S(2)}, u32[]{:S(2)}) collective-permute-start(bf16[256,128]{1,0:T(8,128)(2,1)S(1)} %get-tuple-element.27.refs_0_), channel_id=1, source_target_pairs={{12,0},{9,1},{14,2},{11,3},{8,4},{13,5},{10,6},{15,7},{4,8},{1,9},... | collective-permute-start | bytes 196616 | tf_op jit(solution)/shard_map/ppermute | solution.py:348
  6.3 0.6 %collective-permute-start = (bf16[256,128]{1,0:T(8,128)(2,1)S(1)}, bf16[256,128]{1,0:T(8,128)(2,1)S(1)}, u32[]{:S(2)}, u32[]{:S(2)}) collective-permute-start(bf16[256,128]{1,0:T(8,128)(2,1)S(1)} %get-tuple-element.27.refs_0_), channel_id=1, source_target_pairs={{8,0},{13,1},{10,2},{15,3},{12,4},{9,5},{14,6},{11,7},{0,8},{5,9},... | collective-permute-start | bytes 196616 | tf_op jit(solution)/shard_map/ppermute | solution.py:348
  7.0 1.7 %collective-permute-start.2 = (bf16[256,128]{1,0:T(8,128)(2,1)S(1)}, bf16[256,128]{1,0:T(8,128)(2,1)S(1)}, u32[]{:S(2)}, u32[]{:S(2)}) collective-permute-start(bf16[256,128]{1,0:T(8,128)(2,1)S(1)} %get-tuple-element.27.refs_0_), channel_id=1, source_target_pairs={{2,0},{3,1},{0,2},{1,3},{6,4},{7,5},{4,6},{5,7},{10,8},{11,9},{8,1... | collective-permute-start | bytes 196616 | tf_op jit(solution)/shard_map/ppermute | solution.py:348
  8.6 0.5 %collective-permute-done.3.refs_3_ = bf16[256,128]{1,0:T(8,128)(2,1)S(1)} collective-permute-done((bf16[256,128]{1,0:T(8,128)(2,1)S(1)}, bf16[256,128]{1,0:T(8,128)(2,1)S(1)}, u32[]{:S(2)}, u32[]{:S(2)}) %collective-permute-start.3) | collective-permute-done | bytes 65568 | tf_op jit(solution)/shard_map/ppermute | solution.py:348
  9.2 1.5 %collective-permute-start.4 = (bf16[256,128]{1,0:T(8,128)(2,1)S(1)}, bf16[256,128]{1,0:T(8,128)(2,1)S(1)}, u32[]{:S(2)}, u32[]{:S(2)}) collective-permute-start(bf16[256,128]{1,0:T(8,128)(2,1)S(1)} %collective-permute-done.3.refs_3_), channel_id=1, source_target_pairs={{2,0},{3,1},{0,2},{1,3},{6,4},{7,5},{4,6},{5,7},{10,8},{11,9},{8,1... | collective-permute-start | bytes 196616 | tf_op jit(solution)/shard_map/ppermute | solution.py:348
  10.7 1.4 %collective-permute-start.6 = (bf16[256,128]{1,0:T(8,128)(2,1)S(1)}, bf16[256,128]{1,0:T(8,128)(2,1)S(1)}, u32[]{:S(2)}, u32[]{:S(2)}) collective-permute-start(bf16[256,128]{1,0:T(8,128)(2,1)S(1)} %collective-permute-done.5.refs_1_), channel_id=1, source_target_pairs={{2,0},{3,1},{0,2},{1,3},{6,4},{7,5},{4,6},{5,7},{10,8},{11,9},{8,1... | collective-permute-start | bytes 196616 | tf_op jit(solution)/shard_map/ppermute | solution.py:348
  12.1 1.4 %collective-permute-start.1 = (bf16[256,128]{1,0:T(8,128)(2,1)S(1)}, bf16[256,128]{1,0:T(8,128)(2,1)S(1)}, u32[]{:S(2)}, u32[]{:S(2)}) collective-permute-start(bf16[256,128]{1,0:T(8,128)(2,1)S(1)} %collective-permute-done.refs_2_), channel_id=1, source_target_pairs={{2,0},{3,1},{0,2},{1,3},{6,4},{7,5},{4,6},{5,7},{10,8},{11,9},{8,1... | collective-permute-start | bytes 196616 | tf_op jit(solution)/shard_map/ppermute | solution.py:348
  13.5 0.6 %outgoing_edges.2 = (bf16[4,256,128]{2,1,0:T(8,128)(2,1)S(1)}, f32[4,4,8,128]{3,2,1,0:T(8,128)S(1)}, f32[256,128]{1,0:T(8,128)S(1)}, f32[256,128]{1,0:T(8,128)S(1)}) custom-call(s32[1]{0:T(128)} %bitcast.at_ref, bf16[256,128]{1,0:T(8,128)(2,1)S(1)} %get-tuple-element.27.refs_0_, bf16[256,128]{1,0:T(8,128)(2,1)S(1)} %collective-permute-done.5.refs_1_, ...), custom_call_target="tpu_custom_call" | custom-call | flops 1048576 | bytes 16384 | tf_op jit(solution)/shard_map/outgoing_edges/pallas_call | solution.py:311
  14.2 0.9 %collective-permute-done.6.refs_2_ = bf16[256,128]{1,0:T(8,128)(2,1)S(1)} collective-permute-done((bf16[256,128]{1,0:T(8,128)(2,1)S(1)}, bf16[256,128]{1,0:T(8,128)(2,1)S(1)}, u32[]{:S(2)}, u32[]{:S(2)}) %collective-permute-start.6) | collective-permute-done | bytes 65568 | tf_op jit(solution)/shard_map/ppermute | solution.py:348
  15.6 0.8 %collective-permute-done.1.normed_ref = bf16[256,128]{1,0:T(8,128)(2,1)S(1)} collective-permute-done((bf16[256,128]{1,0:T(8,128)(2,1)S(1)}, bf16[256,128]{1,0:T(8,128)(2,1)S(1)}, u32[]{:S(2)}, u32[]{:S(2)}) %collective-permute-start.1) | collective-permute-done | bytes 65568 | tf_op jit(solution)/shard_map/ppermute | solution.py:348
  16.9 1.3 %collective-permute-done.7.piece_ref = bf16[4,256,128]{2,1,0:T(8,128)(2,1)S(1)} collective-permute-done((bf16[4,256,128]{2,1,0:T(8,128)(2,1)S(1)}, bf16[4,256,128]{2,1,0:T(8,128)(2,1)S(1)}, u32[]{:S(2)}, u32[]{:S(2)}) %collective-permute-start.7) | collective-permute-done | bytes 262176 | tf_op jit(solution)/shard_map/ppermute | solution.py:348
  18.2 0.7 %outgoing_finish.1 = (f32[256,128]{1,0:T(8,128)S(1)}, bf16[256,128]{1,0:T(8,128)(2,1)S(1)}) custom-call(s32[1]{0:T(128)} %bitcast.at_ref, bf16[4,256,128]{2,1,0:T(8,128)(2,1)S(1)} %collective-permute-done.7.piece_ref, f32[4,4,8,128]{3,2,1,0:T(8,128)S(1)} %get-tuple-element.33.refs_0_, f32[3,4,8,128]{3,2,1,0:T(8,128)S(1)} %get-tuple-element.34.refs_1_, ...), custom_call_target="tpu_custom_call" | custom-call | tf_op jit(solution)/shard_map/outgoing_finish/pallas_call | solution.py:311
  18.9 3.2 %collective-permute-start.10 = (bf16[256,128]{1,0:T(8,128)(2,1)S(1)}, bf16[256,128]{1,0:T(8,128)(2,1)S(1)}, u32[]{:S(2)}, u32[]{:S(2)}) collective-permute-start(bf16[256,128]{1,0:T(8,128)(2,1)S(1)} %get-tuple-element.42.refs_0_), channel_id=1, source_target_pairs={{12,0},{9,1},{14,2},{11,3},{8,4},{13,5},{10,6},{15,7},{4,8},{1,9},... | collective-permute-start | bytes 196616 | tf_op jit(solution)/shard_map/ppermute | solution.py:348
  22.1 1.2 %collective-permute-start.14 = (bf16[256,128]{1,0:T(8,128)(2,1)S(1)}, bf16[256,128]{1,0:T(8,128)(2,1)S(1)}, u32[]{:S(2)}, u32[]{:S(2)}) collective-permute-start(bf16[256,128]{1,0:T(8,128)(2,1)S(1)} %get-tuple-element.42.refs_0_), channel_id=1, source_target_pairs={{8,0},{13,1},{10,2},{15,3},{12,4},{9,5},{14,6},{11,7},{0,8},{5,9},... | collective-permute-start | bytes 196616 | tf_op jit(solution)/shard_map/ppermute | solution.py:348
  23.3 1.4 %collective-permute-start.9 = (bf16[256,128]{1,0:T(8,128)(2,1)S(1)}, bf16[256,128]{1,0:T(8,128)(2,1)S(1)}, u32[]{:S(2)}, u32[]{:S(2)}) collective-permute-start(bf16[256,128]{1,0:T(8,128)(2,1)S(1)} %get-tuple-element.42.refs_0_), channel_id=1, source_target_pairs={{2,0},{3,1},{0,2},{1,3},{6,4},{7,5},{4,6},{5,7},{10,8},{11,9},{8,1... | collective-permute-start | bytes 196616 | tf_op jit(solution)/shard_map/ppermute | solution.py:348
  24.7 0.8 %collective-permute-done.10.refs_3_ = bf16[256,128]{1,0:T(8,128)(2,1)S(1)} collective-permute-done((bf16[256,128]{1,0:T(8,128)(2,1)S(1)}, bf16[256,128]{1,0:T(8,128)(2,1)S(1)}, u32[]{:S(2)}, u32[]{:S(2)}) %collective-permute-start.10) | collective-permute-done | bytes 65568 | tf_op jit(solution)/shard_map/ppermute | solution.py:348
  25.5 1.5 %collective-permute-start.11 = (bf16[256,128]{1,0:T(8,128)(2,1)S(1)}, bf16[256,128]{1,0:T(8,128)(2,1)S(1)}, u32[]{:S(2)}, u32[]{:S(2)}) collective-permute-start(bf16[256,128]{1,0:T(8,128)(2,1)S(1)} %collective-permute-done.10.refs_3_), channel_id=1, source_target_pairs={{2,0},{3,1},{0,2},{1,3},{6,4},{7,5},{4,6},{5,7},{10,8},{11,9},{8,1... | collective-permute-start | bytes 196616 | tf_op jit(solution)/shard_map/ppermute | solution.py:348
  27.0 0.7 %collective-permute-start.13 = (bf16[256,128]{1,0:T(8,128)(2,1)S(1)}, bf16[256,128]{1,0:T(8,128)(2,1)S(1)}, u32[]{:S(2)}, u32[]{:S(2)}) collective-permute-start(bf16[256,128]{1,0:T(8,128)(2,1)S(1)} %collective-permute-done.12.refs_1_), channel_id=1, source_target_pairs={{2,0},{3,1},{0,2},{1,3},{6,4},{7,5},{4,6},{5,7},{10,8},{11,9},{8,1... | collective-permute-start | bytes 196616 | tf_op jit(solution)/shard_map/ppermute | solution.py:348
  28.0 1.4 %collective-permute-start.16 = (bf16[256,128]{1,0:T(8,128)(2,1)S(1)}, bf16[256,128]{1,0:T(8,128)(2,1)S(1)}, u32[]{:S(2)}, u32[]{:S(2)}) collective-permute-start(bf16[256,128]{1,0:T(8,128)(2,1)S(1)} %collective-permute-done.14.refs_2_), channel_id=1, source_target_pairs={{2,0},{3,1},{0,2},{1,3},{6,4},{7,5},{4,6},{5,7},{10,8},{11,9},{8,1... | collective-permute-start | bytes 196616 | tf_op jit(solution)/shard_map/ppermute | solution.py:348
  29.4 0.6 %incoming_edges.2 = (bf16[4,288,128]{2,1,0:T(8,128)(2,1)S(1)}, f32[4,64,128]{2,1,0:T(8,128)S(1)}, f32[256,128]{1,0:T(8,128)S(1)}) custom-call(s32[1]{0:T(128)} %bitcast.at_ref, bf16[256,128]{1,0:T(8,128)(2,1)S(1)} %get-tuple-element.42.refs_0_, bf16[256,128]{1,0:T(8,128)(2,1)S(1)} %collective-permute-done.12.refs_1_, ...), custom_call_target="tpu_custom_call" | custom-call | flops 1048576 | bytes 16384 | tf_op jit(solution)/shard_map/incoming_edges/pallas_call | solution.py:311
  30.1 1.2 %collective-permute-done.13.refs_2_ = bf16[256,128]{1,0:T(8,128)(2,1)S(1)} collective-permute-done((bf16[256,128]{1,0:T(8,128)(2,1)S(1)}, bf16[256,128]{1,0:T(8,128)(2,1)S(1)}, u32[]{:S(2)}, u32[]{:S(2)}) %collective-permute-start.13) | collective-permute-done | bytes 65568 | tf_op jit(solution)/shard_map/ppermute | solution.py:348
  32.7 1.4 %collective-permute-done.17.piece_ref = bf16[4,288,128]{2,1,0:T(8,128)(2,1)S(1)} collective-permute-done((bf16[4,288,128]{2,1,0:T(8,128)(2,1)S(1)}, bf16[4,288,128]{2,1,0:T(8,128)(2,1)S(1)}, u32[]{:S(2)}, u32[]{:S(2)}) %collective-permute-start.17) | collective-permute-done | bytes 294944 | tf_op jit(solution)/shard_map/ppermute | solution.py:348
  34.1 1.1 %incoming_finish.1 = f32[4,64,128]{2,1,0:T(8,128)} custom-call(f32[4,64,128]{2,1,0:T(8,128)S(1)} %incoming.1.before_ref, bf16[4,288,128]{2,1,0:T(8,128)(2,1)S(1)} %collective-permute-done.17.piece_ref, f32[256,128]{1,0:T(8,128)S(1)} %get-tuple-element.47.first_ref, f32[256,128]{1,0:T(8,128)S(1)} %get-tuple-element.48.gate_ref, ...), custom_call_target="tpu_custom_call" | custom-call | tf_op jit(solution)/shard_map/incoming_finish/pallas_call | solution.py:311
  (23 shorter events, 2.7 us)
Async XLA Ops:
  1.2 8.0 %collective-permute-start.3 = (bf16[256,128]{1,0:T(8,128)(2,1)S(1)}, bf16[256,128]{1,0:T(8,128)(2,1)S(1)}, u32[]{:S(2)}, u32[]{:S(2)}) collective-permute-start(bf16[256,128]{1,0:T(8,128)(2,1)S(1)} %get-tuple-element.27.refs_0_), channel_id=1, source_target_pairs={{12,0},{9,1},{14,2},{11,3},{8,4},{13,5},{10,6},{15,7},{4,8},{1,9},... | collective-permute-start | bytes 196616 | tf_op jit(solution)/shard_map/ppermute | solution.py:348
  6.3 4.4 %collective-permute-start.5 = (bf16[256,128]{1,0:T(8,128)(2,1)S(1)}, bf16[256,128]{1,0:T(8,128)(2,1)S(1)}, u32[]{:S(2)}, u32[]{:S(2)}) collective-permute-start(bf16[256,128]{1,0:T(8,128)(2,1)S(1)} %get-tuple-element.27.refs_0_), channel_id=1, source_target_pairs={{4,0},{5,1},{6,2},{7,3},{0,4},{1,5},{2,6},{3,7},{12,8},{13,9},{14,... | collective-permute-start | bytes 196616 | tf_op jit(solution)/shard_map/ppermute | solution.py:348
  6.3 5.8 %collective-permute-start = (bf16[256,128]{1,0:T(8,128)(2,1)S(1)}, bf16[256,128]{1,0:T(8,128)(2,1)S(1)}, u32[]{:S(2)}, u32[]{:S(2)}) collective-permute-start(bf16[256,128]{1,0:T(8,128)(2,1)S(1)} %get-tuple-element.27.refs_0_), channel_id=1, source_target_pairs={{8,0},{13,1},{10,2},{15,3},{12,4},{9,5},{14,6},{11,7},{0,8},{5,9},... | collective-permute-start | bytes 196616 | tf_op jit(solution)/shard_map/ppermute | solution.py:348
  7.0 7.3 %collective-permute-start.2 = (bf16[256,128]{1,0:T(8,128)(2,1)S(1)}, bf16[256,128]{1,0:T(8,128)(2,1)S(1)}, u32[]{:S(2)}, u32[]{:S(2)}) collective-permute-start(bf16[256,128]{1,0:T(8,128)(2,1)S(1)} %get-tuple-element.27.refs_0_), channel_id=1, source_target_pairs={{2,0},{3,1},{0,2},{1,3},{6,4},{7,5},{4,6},{5,7},{10,8},{11,9},{8,1... | collective-permute-start | bytes 196616 | tf_op jit(solution)/shard_map/ppermute | solution.py:348
  9.2 5.1 %collective-permute-start.4 = (bf16[256,128]{1,0:T(8,128)(2,1)S(1)}, bf16[256,128]{1,0:T(8,128)(2,1)S(1)}, u32[]{:S(2)}, u32[]{:S(2)}) collective-permute-start(bf16[256,128]{1,0:T(8,128)(2,1)S(1)} %collective-permute-done.3.refs_3_), channel_id=1, source_target_pairs={{2,0},{3,1},{0,2},{1,3},{6,4},{7,5},{4,6},{5,7},{10,8},{11,9},{8,1... | collective-permute-start | bytes 196616 | tf_op jit(solution)/shard_map/ppermute | solution.py:348
  10.7 4.4 %collective-permute-start.6 = (bf16[256,128]{1,0:T(8,128)(2,1)S(1)}, bf16[256,128]{1,0:T(8,128)(2,1)S(1)}, u32[]{:S(2)}, u32[]{:S(2)}) collective-permute-start(bf16[256,128]{1,0:T(8,128)(2,1)S(1)} %collective-permute-done.5.refs_1_), channel_id=1, source_target_pairs={{2,0},{3,1},{0,2},{1,3},{6,4},{7,5},{4,6},{5,7},{10,8},{11,9},{8,1... | collective-permute-start | bytes 196616 | tf_op jit(solution)/shard_map/ppermute | solution.py:348
  12.1 4.3 %collective-permute-start.1 = (bf16[256,128]{1,0:T(8,128)(2,1)S(1)}, bf16[256,128]{1,0:T(8,128)(2,1)S(1)}, u32[]{:S(2)}, u32[]{:S(2)}) collective-permute-start(bf16[256,128]{1,0:T(8,128)(2,1)S(1)} %collective-permute-done.refs_2_), channel_id=1, source_target_pairs={{2,0},{3,1},{0,2},{1,3},{6,4},{7,5},{4,6},{5,7},{10,8},{11,9},{8,1... | collective-permute-start | bytes 196616 | tf_op jit(solution)/shard_map/ppermute | solution.py:348
  14.1 2.5 %collective-permute-start.8 = (bf16[4,256,128]{2,1,0:T(8,128)(2,1)S(1)}, bf16[4,256,128]{2,1,0:T(8,128)(2,1)S(1)}, u32[]{:S(2)}, u32[]{:S(2)}) collective-permute-start(bf16[4,256,128]{2,1,0:T(8,128)(2,1)S(1)} %get-tuple-element.35), channel_id=1, source_target_pairs={{1,0},{0,1},{3,2},{2,3},{5,4},{4,5},{7,6},{6,7},{9,8},{8,9},{11,10... | collective-permute-start | bytes 786440 | tf_op jit(solution)/shard_map/ppermute | solution.py:348
  16.6 1.6 %collective-permute-start.7 = (bf16[4,256,128]{2,1,0:T(8,128)(2,1)S(1)}, bf16[4,256,128]{2,1,0:T(8,128)(2,1)S(1)}, u32[]{:S(2)}, u32[]{:S(2)}) collective-permute-start(bf16[4,256,128]{2,1,0:T(8,128)(2,1)S(1)} %outgoing_last.1.last_ref), channel_id=1, source_target_pairs={{1,0},{0,1},{3,2},{2,3},{5,4},{4,5},{7,6},{6,7},{9,8},{8,9},{11,10... | collective-permute-start | bytes 786440 | tf_op jit(solution)/shard_map/ppermute | solution.py:348
  18.9 6.6 %collective-permute-start.10 = (bf16[256,128]{1,0:T(8,128)(2,1)S(1)}, bf16[256,128]{1,0:T(8,128)(2,1)S(1)}, u32[]{:S(2)}, u32[]{:S(2)}) collective-permute-start(bf16[256,128]{1,0:T(8,128)(2,1)S(1)} %get-tuple-element.42.refs_0_), channel_id=1, source_target_pairs={{12,0},{9,1},{14,2},{11,3},{8,4},{13,5},{10,6},{15,7},{4,8},{1,9},... | collective-permute-start | bytes 196616 | tf_op jit(solution)/shard_map/ppermute | solution.py:348
  22.1 4.9 %collective-permute-start.12 = (bf16[256,128]{1,0:T(8,128)(2,1)S(1)}, bf16[256,128]{1,0:T(8,128)(2,1)S(1)}, u32[]{:S(2)}, u32[]{:S(2)}) collective-permute-start(bf16[256,128]{1,0:T(8,128)(2,1)S(1)} %get-tuple-element.42.refs_0_), channel_id=1, source_target_pairs={{4,0},{5,1},{6,2},{7,3},{0,4},{1,5},{2,6},{3,7},{12,8},{13,9},{14,... | collective-permute-start | bytes 196616 | tf_op jit(solution)/shard_map/ppermute | solution.py:348
  22.1 5.9 %collective-permute-start.14 = (bf16[256,128]{1,0:T(8,128)(2,1)S(1)}, bf16[256,128]{1,0:T(8,128)(2,1)S(1)}, u32[]{:S(2)}, u32[]{:S(2)}) collective-permute-start(bf16[256,128]{1,0:T(8,128)(2,1)S(1)} %get-tuple-element.42.refs_0_), channel_id=1, source_target_pairs={{8,0},{13,1},{10,2},{15,3},{12,4},{9,5},{14,6},{11,7},{0,8},{5,9},... | collective-permute-start | bytes 196616 | tf_op jit(solution)/shard_map/ppermute | solution.py:348
  23.3 6.7 %collective-permute-start.9 = (bf16[256,128]{1,0:T(8,128)(2,1)S(1)}, bf16[256,128]{1,0:T(8,128)(2,1)S(1)}, u32[]{:S(2)}, u32[]{:S(2)}) collective-permute-start(bf16[256,128]{1,0:T(8,128)(2,1)S(1)} %get-tuple-element.42.refs_0_), channel_id=1, source_target_pairs={{2,0},{3,1},{0,2},{1,3},{6,4},{7,5},{4,6},{5,7},{10,8},{11,9},{8,1... | collective-permute-start | bytes 196616 | tf_op jit(solution)/shard_map/ppermute | solution.py:348
  25.5 4.5 %collective-permute-start.11 = (bf16[256,128]{1,0:T(8,128)(2,1)S(1)}, bf16[256,128]{1,0:T(8,128)(2,1)S(1)}, u32[]{:S(2)}, u32[]{:S(2)}) collective-permute-start(bf16[256,128]{1,0:T(8,128)(2,1)S(1)} %collective-permute-done.10.refs_3_), channel_id=1, source_target_pairs={{2,0},{3,1},{0,2},{1,3},{6,4},{7,5},{4,6},{5,7},{10,8},{11,9},{8,1... | collective-permute-start | bytes 196616 | tf_op jit(solution)/shard_map/ppermute | solution.py:348
  27.0 4.3 %collective-permute-start.13 = (bf16[256,128]{1,0:T(8,128)(2,1)S(1)}, bf16[256,128]{1,0:T(8,128)(2,1)S(1)}, u32[]{:S(2)}, u32[]{:S(2)}) collective-permute-start(bf16[256,128]{1,0:T(8,128)(2,1)S(1)} %collective-permute-done.12.refs_1_), channel_id=1, source_target_pairs={{2,0},{3,1},{0,2},{1,3},{6,4},{7,5},{4,6},{5,7},{10,8},{11,9},{8,1... | collective-permute-start | bytes 196616 | tf_op jit(solution)/shard_map/ppermute | solution.py:348
  28.0 4.3 %collective-permute-start.16 = (bf16[256,128]{1,0:T(8,128)(2,1)S(1)}, bf16[256,128]{1,0:T(8,128)(2,1)S(1)}, u32[]{:S(2)}, u32[]{:S(2)}) collective-permute-start(bf16[256,128]{1,0:T(8,128)(2,1)S(1)} %collective-permute-done.14.refs_2_), channel_id=1, source_target_pairs={{2,0},{3,1},{0,2},{1,3},{6,4},{7,5},{4,6},{5,7},{10,8},{11,9},{8,1... | collective-permute-start | bytes 196616 | tf_op jit(solution)/shard_map/ppermute | solution.py:348
  30.0 2.5 %collective-permute-start.15 = (bf16[4,288,128]{2,1,0:T(8,128)(2,1)S(1)}, bf16[4,288,128]{2,1,0:T(8,128)(2,1)S(1)}, u32[]{:S(2)}, u32[]{:S(2)}) collective-permute-start(bf16[4,288,128]{2,1,0:T(8,128)(2,1)S(1)} %get-tuple-element.45), channel_id=1, source_target_pairs={{1,0},{0,1},{3,2},{2,3},{5,4},{4,5},{7,6},{6,7},{9,8},{8,9},{11,10... | collective-permute-start | bytes 884744 | tf_op jit(solution)/shard_map/ppermute | solution.py:348
  32.4 1.6 %collective-permute-start.17 = (bf16[4,288,128]{2,1,0:T(8,128)(2,1)S(1)}, bf16[4,288,128]{2,1,0:T(8,128)(2,1)S(1)}, u32[]{:S(2)}, u32[]{:S(2)}) collective-permute-start(bf16[4,288,128]{2,1,0:T(8,128)(2,1)S(1)} %incoming_last.1.last_ref), channel_id=1, source_target_pairs={{1,0},{0,1},{3,2},{2,3},{5,4},{4,5},{7,6},{6,7},{9,8},{8,9},{11,10... | collective-permute-start | bytes 884744 | tf_op jit(solution)/shard_map/ppermute | solution.py:348

commit v7 on v5

v7 whole, which is shorter than its diff:
```python
import functools

import jax
import jax.numpy as jnp
from jax import lax
from jax.experimental import pallas as pl
from jax.experimental.pallas import tpu as pltpu
from jax.sharding import PartitionSpec as P

F32 = jnp.float32
BF16 = jnp.bfloat16
VMEM = pl.BlockSpec(memory_space=pltpu.VMEM)
SMEM = pl.BlockSpec(memory_space=pltpu.SMEM)
CHUNK = 64
BLOCK = 512
PARAMS = pltpu.CompilerParams(vmem_limit_bytes=48 * 1024 * 1024)


def normalize(values, gain, shift):
    mean = jnp.mean(values, axis=-1, keepdims=True)
    centered = values - mean
    spread = jnp.mean(centered * centered, axis=-1, keepdims=True)
    return centered * lax.rsqrt(spread + 1e-05) * gain + shift


def sigmoid(values):
    return 0.5 * jnp.tanh(0.5 * values) + 0.5


def gated(normed, edge_w_ref, edge_bias_ref, layer, index, hidden):
    span = slice(index * hidden, (index + 2) * hidden)
    both = jnp.dot(normed, edge_w_ref[layer, :, span], preferred_element_type=F32)
    both = both + edge_bias_ref[layer : layer + 1, span]
    return sigmoid(both[:, :hidden]) * both[:, hidden:]


def masked(values, row, column, mask_ref):
    valid = jnp.sum(mask_ref[...].astype(F32), axis=1, keepdims=True)
    return jnp.where(jnp.maximum(row, column).astype(F32) < valid, values, 0.0)


def edges(normed_ref, out_ref, first_row, side, mask_ref, edge_w_ref, edge_bias_ref, layer, index):
    count, hidden = normed_ref.shape[0], out_ref.shape[1]
    size = min(count, BLOCK)

    def block(at):
        values = gated(
            normed_ref[pl.ds(at, size), :], edge_w_ref, edge_bias_ref, layer, index, hidden
        )
        position = at + lax.broadcasted_iota(jnp.int32, values.shape, 0)
        values = masked(values, first_row + position // side, position % side, mask_ref)
        out_ref[pl.ds(at, size), :] = values.astype(BF16).astype(out_ref.dtype)

    if count == size:
        block(0)
    else:
        pl.loop(0, count // size)(lambda n: block(pl.multiple_of(n * size, size)))


def gate_of(normed, gate_ref, edge_w_ref, edge_bias_ref, layer):
    width = gate_ref.shape[1]
    low = edge_bias_ref.shape[1] - width
    value = jnp.dot(normed, edge_w_ref[layer, :, low:], preferred_element_type=F32)
    gate_ref[...] = sigmoid(value + edge_bias_ref[layer : layer + 1, low:])


def finish(block, contracted, gate, gain_ref, shift_ref, out_w_ref, out_bias_ref, layer):
    normed = normalize(contracted, gain_ref[layer, 1:2, :], shift_ref[layer, 1:2, :]).astype(BF16)
    result = jnp.dot(normed, out_w_ref[layer], preferred_element_type=F32)
    return block + gate * (result + out_bias_ref[layer : layer + 1, :])


def chip_of(me, distances, own):
    core = me & 1 if own else 1 - (me & 1)
    near, far = distances
    return me >> 1 ^ near + (far - near) * core


def load_kernel(*refs):
    count = len(refs) // 2
    given, kept, sems = refs[:count], refs[count : 2 * count], refs[2 * count]
    copies = [
        pltpu.make_async_copy(source, target, sems.at[n])
        for n, (source, target) in enumerate(zip(given, kept))
    ]
    for copy in copies:
        copy.start()
    for copy in copies:
        copy.wait()


def norm_kernel(at_ref, pair_ref, other_ref, gain_ref, shift_ref, both_ref, normed_ref):
    rows = pair_ref.shape[0]
    core = at_ref[0] & 1
    both_ref[pl.ds(core * rows, rows)] = pair_ref[...]
    both_ref[pl.ds((1 - core) * rows, rows)] = other_ref[...]
    block = both_ref[...].reshape(normed_ref.shape)
    normed_ref[...] = normalize(block, gain_ref[0, 0:1, :], shift_ref[0, 0:1, :]).astype(BF16)


def merge(low, a, b, shift):
    return jnp.where(low, a, b) + pltpu.roll(jnp.where(low, b, a), shift, 0)


def fold(parts, sub):
    for shift in (1, 2, 4):
        low = (sub & shift) == 0
        parts = [merge(low, a, b, shift) for a, b in zip(parts[0::2], parts[1::2])]
    return parts[0]


def row_sums(left_ref, piece_ref, a, first, some, side):
    hidden = left_ref.shape[1]

    def chunk(at, totals):
        right = piece_ref[pl.ds(a * side + at, CHUNK), :].astype(F32)
        sums = []
        for i in range(first, first + some):
            product = left_ref[pl.ds(i * side + at, CHUNK), :] * right
            sums.append(jnp.sum(product.reshape(CHUNK // 8, 8, hidden), axis=0))
        return [t + s for t, s in zip(totals, sums)] if totals else sums

    totals = chunk(0, None)
    if side > CHUNK:
        totals = lax.fori_loop(
            1, side // CHUNK, lambda n, t: chunk(pl.multiple_of(n * CHUNK, CHUNK), t), totals
        )
    return totals


def products(left_ref, piece_ref, part_ref, side):
    rows, height, hidden = part_ref.shape
    sub = lax.broadcasted_iota(jnp.int32, (height, hidden), 0)
    some = 4
    for first in range(0, rows, some):
        totals = [row_sums(left_ref, piece_ref, a, first, some, side) for a in range(height)]
        for i in range(some):
            part_ref[first + i] = fold([total[i] for total in totals], sub)


def outgoing_edges_kernel(held, side, at_ref, *refs):
    normed, refs = refs[: len(held)], refs[len(held) :]
    mask_ref, edge_w_ref, edge_bias_ref, *refs = refs
    if len(refs) == 5:
        own_ref, right_ref, part_ref, left_ref, gate_ref = refs
    else:
        left_ref, right_ref, part_ref = refs
    me = at_ref[0]
    height = left_ref.shape[0] // side
    shared = (side, mask_ref, edge_w_ref, edge_bias_ref, 0)
    if len(refs) == 5:
        edges(own_ref, left_ref, (me >> 1) * height, *shared, 0)
        gate_of(own_ref[...], gate_ref, edge_w_ref, edge_bias_ref, 0)
    for n, distances in enumerate(held):
        first = chip_of(me, distances, True) * height
        edges(normed[n], right_ref.at[n], first, *shared, 2)
        products(left_ref, right_ref.at[n], part_ref.at[n], side)


def outgoing_last_kernel(
    last, side, at_ref, normed_ref, mask_ref, edge_w_ref, edge_bias_ref, before_ref, right_ref
):
    count = before_ref.shape[0]
    height = normed_ref.shape[0] // side
    right_ref[:count] = before_ref[...]
    edges(
        normed_ref, right_ref.at[count], chip_of(at_ref[0], last, True) * height, side,
        mask_ref, edge_w_ref, edge_bias_ref, 0, 2,
    )


def outgoing_kernel(left_ref, piece_ref, last_ref, part_ref):
    side = left_ref.shape[0] // part_ref.shape[1]
    count = piece_ref.shape[0]
    pieces = [piece_ref.at[n] for n in range(count)] + [last_ref.at[last_ref.shape[0] - 1]]
    for n, piece in enumerate(pieces):
        products(left_ref, piece, part_ref.at[n], side)


def outgoing_finish_kernel(held, given, at_ref, piece_ref, *refs):
    parts, refs = refs[: len(given)], refs[len(given) :]
    (
        left_ref, gate_ref, both_ref, gain_ref, shift_ref, out_w_ref, out_bias_ref,
        first_ref, normed_ref, x_scr, part_scr,
    ) = refs
    height, side, width = both_ref.shape
    hidden = left_ref.shape[1]
    me = at_ref[0]

    def put(part, distances, own):
        at = pl.multiple_of(chip_of(me, distances, own) * height, height)
        for i in range(height):
            x_scr[i, pl.ds(at, height), :] = part[i]

    for part, slots in zip(parts, given):
        for n, (distances, own) in enumerate(slots):
            put(part.at[n], distances, own)
    for n, distances in enumerate(held):
        products(left_ref, piece_ref.at[n], part_scr.at[n], side)
        put(part_scr.at[n], distances, False)

    block = both_ref[...].reshape(height * side, width)
    contracted = x_scr[...].reshape(height * side, hidden)
    first = finish(
        block, contracted, gate_ref[...], gain_ref, shift_ref, out_w_ref, out_bias_ref, 0
    )
    first_ref[...] = first.reshape(first_ref.shape)
    normed_ref[...] = normalize(first, gain_ref[1, 0:1, :], shift_ref[1, 0:1, :]).astype(BF16)


def add_pieces(pieces, left_scr, x_ref, start):
    rows, side, hidden = x_ref.shape
    height = 2 * rows
    for n, (piece, came) in enumerate(pieces):
        left_scr[n] = piece[height * side :, :].astype(F32)

    def columns(at):
        totals = [start(i, at) for i in range(rows)]
        for n, (piece, came) in enumerate(pieces):
            for a in range(height):
                right = piece[pl.ds(a * side + at, CHUNK), :].astype(F32)
                for i in range(rows):
                    row = a * height + came * rows + i
                    totals[i] = totals[i] + left_scr[n, row : row + 1, :] * right
        for i in range(rows):
            x_ref[i, pl.ds(at, CHUNK), :] = totals[i]

    if side == CHUNK:
        columns(0)
    else:
        pl.loop(0, side // CHUNK)(lambda n: columns(pl.multiple_of(n * CHUNK, CHUNK)))


def form_incoming(held, me, normed, out_refs, mask_ref, edge_w_ref, edge_bias_ref, side):
    chip = me >> 1
    height = normed[0].shape[0] // side
    hidden = out_refs[0].shape[1]
    columns, places = [], []
    for distances, normed_ref, out_ref in zip(held, normed, out_refs):
        first = chip_of(me, distances, True) * height
        edges(
            normed_ref, out_ref.at[pl.ds(0, height * side)], first, side,
            mask_ref, edge_w_ref, edge_bias_ref, 1, 2,
        )
        for a in range(height):
            both = normed_ref[pl.ds(pl.multiple_of(a * side + (chip >> 1) * 16, 16), 16), :]
            both = both.astype(F32)
            columns.append(jnp.where(chip & 1 == 0, both[:8], both[8:]))
            places.append(jnp.full((8, hidden), first + a, jnp.int32))
    left = gated(
        jnp.concatenate(columns, 0).astype(BF16), edge_w_ref, edge_bias_ref, 1, 0, hidden
    )
    column = chip * 8 + lax.broadcasted_iota(jnp.int32, left.shape, 0) % 8
    left = masked(left, jnp.concatenate(places, 0), column, mask_ref)
    left = left.reshape(len(held) * height, 8, hidden)
    left = jnp.where(me & 1 == 0, left, pltpu.roll(left, 4, 1))
    left = left.reshape(len(held), height * 8, hidden).astype(BF16)
    for n, out_ref in enumerate(out_refs):
        out_ref[height * side :, :] = left[n]


def incoming_edges_kernel(held, side, at_ref, *refs):
    normed, refs = refs[: len(held)], refs[len(held) :]
    mask_ref, edge_w_ref, edge_bias_ref, extra_ref, out_ref, x_ref, *refs = refs
    rows, _, hidden = x_ref.shape
    me = at_ref[0]
    if len(refs) == 2:
        gate_ref, left_scr = refs
        count = rows * side
        own = extra_ref[pl.ds(pl.multiple_of((me & 1) * count, count), count), :]
        gate_of(own, gate_ref, edge_w_ref, edge_bias_ref, 1)
        start = lambda i, at: jnp.zeros((CHUNK, hidden), F32)
    else:
        (left_scr,) = refs
        start = lambda i, at: extra_ref[i, pl.ds(at, CHUNK), :]
    outs = [out_ref.at[n] for n in range(len(held))]
    form_incoming(held, me, normed, outs, mask_ref, edge_w_ref, edge_bias_ref, side)
    add_pieces([(out, 0) for out in outs], left_scr, x_ref, start)


def incoming_last_kernel(
    last, side, at_ref, normed_ref, mask_ref, edge_w_ref, edge_bias_ref, before_ref, out_ref
):
    count = before_ref.shape[0]
    out_ref[:count] = before_ref[...]
    form_incoming(
        [last], at_ref[0], [normed_ref], [out_ref.at[count]],
        mask_ref, edge_w_ref, edge_bias_ref, side,
    )


def incoming_kernel(before_ref, piece_ref, last_ref, x_ref, left_scr):
    pieces = [(piece_ref.at[n], 1) for n in range(piece_ref.shape[0])]
    pieces.append((last_ref.at[last_ref.shape[0] - 1], 0))
    add_pieces(pieces, left_scr, x_ref, lambda i, at: before_ref[i, pl.ds(at, CHUNK), :])


def incoming_finish_kernel(
    at_ref, before_ref, piece_ref, first_ref, gate_ref, gain_ref, shift_ref, out_w_ref,
    out_bias_ref, out_ref, left_scr, x_scr,
):
    rows, side, width = out_ref.shape
    hidden = gate_ref.shape[1]
    pieces = [(piece_ref.at[n], 1) for n in range(piece_ref.shape[0])]
    add_pieces(pieces, left_scr, x_scr, lambda i, at: before_ref[i, pl.ds(at, CHUNK), :])
    first = first_ref[pl.ds((at_ref[0] & 1) * rows, rows)].reshape(rows * side, width)
    out_ref[...] = finish(
        first, x_scr[...].reshape(rows * side, hidden), gate_ref[...],
        gain_ref, shift_ref, out_w_ref, out_bias_ref, 1,
    ).reshape(rows, side, width)


def call(kernel, name, outs, *operands, scalar=None, scratch=()):
    given = operands if scalar is None else (scalar, *operands)
    return pl.pallas_call(
        kernel,
        in_specs=[SMEM] * (scalar is not None) + [VMEM] * len(operands),
        out_specs=[VMEM] * len(outs),
        out_shape=[jax.ShapeDtypeStruct(*out) for out in outs],
        scratch_shapes=[pltpu.VMEM(*one) for one in scratch],
        compiler_params=PARAMS,
        name=name,
    )(*given)


def body(pair, residue_mask, norm_gain, norm_bias, edge_w, edge_bias, out_w, out_bias):
    rows, side, width = pair.shape
    hidden = out_w.shape[1]
    dap = lax.axis_size("dap")
    chips = dap // 2
    me = lax.axis_index("dap").reshape(1)
    mask = residue_mask.reshape(1, side)
    height = 2 * rows
    count = height * side
    span = count + height * height
    half = chips // 2
    quarter = half // 2

    near = [n for n in range(half) if n % 4 in (1, 2)]
    far = [half + n for n in range(half - 2, -1, -2)]
    slots = list(zip(near, far))
    slots += [(a ^ 2, b ^ 1) for a, b in slots]
    groups = (list(range(quarter)), list(range(half - 1, quarter, -1)))
    last = quarter

    def swap(piece, distances):
        pairs = [(device, device ^ 2 * distances[device & 1]) for device in range(dap)]
        return lax.ppermute(piece, "dap", pairs)

    def flip(value):
        return lax.ppermute(value, "dap", [(device, device ^ 1) for device in range(dap)])

    def gather(own):
        pieces = [swap(own, distances) for distances in slots[:quarter]]
        return pieces + [swap(piece, (2, 1)) for piece in pieces]

    arguments = (pair, norm_gain, norm_bias, mask, edge_w, edge_bias, out_w, out_bias)
    kept = pl.pallas_call(
        load_kernel,
        in_specs=[pl.BlockSpec(memory_space=pltpu.HBM)] * len(arguments),
        out_specs=[VMEM] * len(arguments),
        out_shape=[jax.ShapeDtypeStruct(value.shape, value.dtype) for value in arguments],
        scratch_shapes=[pltpu.SemaphoreType.DMA((len(arguments),))],
        compiler_params=PARAMS,
        name="load",
    )(*[pltpu.with_memory_space_constraint(value, pltpu.HBM) for value in arguments])
    other = flip(pair)
    pair, norm_gain, norm_bias, mask, edge_w, edge_bias, out_w, out_bias = kept
    norms = (norm_gain, norm_bias)
    weights = (mask, edge_w, edge_bias)
    part_shape = (height, height, hidden)
    x_shape = (rows, side, hidden)

    both, normed = call(
        norm_kernel, "norm", [((height, side, width), F32), ((count, width), BF16)],
        pair, other, *norms, scalar=me,
    )
    pieces = gather(normed)
    others, parts = [], []
    for group in groups:
        held = [slots[n] for n in group]
        outs = [((len(held), count, hidden), BF16), ((len(held), *part_shape), F32)]
        if not parts:
            outs += [((count, hidden), F32), ((count, width), F32)]
        right, part, *rest = call(
            functools.partial(outgoing_edges_kernel, held, side), "outgoing_edges", outs,
            *[pieces[n] for n in group], *weights, left if parts else normed, scalar=me,
        )
        if rest:
            left, gate = rest
            others.append(flip(right))
        parts.append(part)
    (right,) = call(
        functools.partial(outgoing_last_kernel, slots[last], side), "outgoing_last",
        [((quarter, count, hidden), BF16)], pieces[last], *weights, right, scalar=me,
    )
    others.append(flip(right))
    (part,) = call(
        outgoing_kernel, "outgoing", [((quarter + 1, *part_shape), F32)], left, others[0], right
    )
    known = [[(slots[n], True) for n in group] for group in groups]
    known.append([(slots[n], False) for n in groups[0]] + [(slots[last], True)])
    came = [slots[n] for n in [*groups[1], last]]
    first, normed = call(
        functools.partial(outgoing_finish_kernel, came, known), "outgoing_finish",
        [((height, side, width), F32), ((count, width), BF16)],
        others[1], *parts, part, left, gate, both, *norms, out_w, out_bias,
        scalar=me, scratch=[((height, side, hidden), F32), ((len(came), *part_shape), F32)],
    )

    pieces = gather(normed)
    others, x = [], []
    for group in groups:
        held = [slots[n] for n in group]
        outs = [((len(held), span, hidden), BF16), (x_shape, F32)]
        if not x:
            outs += [((rows * side, width), F32)]
        edge, *made = call(
            functools.partial(incoming_edges_kernel, held, side), "incoming_edges", outs,
            *[pieces[n] for n in group], *weights, *(x or [normed]),
            scalar=me, scratch=[((len(held), height * height, hidden), F32)],
        )
        if not x:
            gate = made.pop()
            others.append(flip(edge))
        x = made
    (edge,) = call(
        functools.partial(incoming_last_kernel, slots[last], side), "incoming_last",
        [((quarter, span, hidden), BF16)], pieces[last], *weights, edge, scalar=me,
    )
    others.append(flip(edge))
    x = call(
        incoming_kernel, "incoming", [(x_shape, F32)], *x, others[0], edge,
        scratch=[((quarter + 1, height * height, hidden), F32)],
    )
    (out,) = call(
        incoming_finish_kernel, "incoming_finish", [((rows, side, width), F32)],
        *x, others[1], first, gate, *norms, out_w, out_bias, scalar=me,
        scratch=[((quarter, height * height, hidden), F32), (x_shape, F32)],
    )
    return out


def solution(mesh):
    in_specs = (P(("groups", "dap"), None, None), P("groups"), P(), P(), P(), P(), P(), P())
    out_specs = P(("groups", "dap"), None, None)
    return jax.shard_map(body, mesh=mesh, in_specs=in_specs, out_specs=out_specs, check_vma=False)
```

time: 36.4 us -> 34.6 us (0.951)
  starting transfers between devices: 20.1 us -> 16.6 us
  Pallas kernels: 5.98 us -> 7.03 us
  waiting for transfers between devices: 10 us -> 10.8 us
    ppermute x18 -> x13, starting transfers between devices: 20.1 us -> 16.6 us  [the longest x8 11.7 us: swap(): return lax.ppermute(piece, 'dap', pairs)]
    pallas_call x10 -> x11, Pallas kernels: 4.8 us -> 5.86 us  [call(): pl.pallas_call(kernel, in_specs=[SMEM] * (scalar is not None) + [VMEM] *...]
    ppermute x18 -> x13, waiting for transfers between devices: 10 us -> 10.8 us  [the longest x8 8.67 us: swap(): return lax.ppermute(piece, 'dap', pairs)]
  transfers between devices with their start and end apart: 18 -> 13, of which waited for: 10 -> 7; matrix products, arithmetic and copies ran while one was open for 0% -> 0% of each run, Pallas kernels for 8% -> 14%
where the time goes in v7:
time: 34.6 us; the launch traced here: 34.5 us
  starting transfers between devices  16.6 us (48%)
  waiting for transfers between devices  10.8 us (31%)
  Pallas kernels  7.03 us (20%)
    ppermute x8, starting transfers between devices, swap(): return lax.ppermute(piece, 'dap', pairs)  11.7 us
    ppermute x8, waiting for transfers between devices, swap(): return lax.ppermute(piece, 'dap', pairs)  8.67 us
    pallas_call x11, Pallas kernels, call(): pl.pallas_call(kernel, in_specs=[SMEM] * (scalar is not None) + [VMEM] *...  5.86 us
    ppermute x5, starting transfers between devices, flip(): lax.ppermute(value, 'dap', [(device, device ^ 1) for device in range(dap)])  4.91 us
    ppermute x5, waiting for transfers between devices, flip(): lax.ppermute(value, 'dap', [(device, device ^ 1) for device in range(dap)])  2.13 us
    pallas_call x1, Pallas kernels, body(): pl.pallas_call(load_kernel, in_specs=[pl.BlockSpec(memory_space=pltpu.HBM...  1.17 us
  transfers between devices with their start and end apart: 13, of which 7 were waited for; matrix products, arithmetic and copies ran while one was open for 0% of the time, Pallas kernels for 14%

profile of v7, /device:TPU:0, one launch (start us, length us, event | category | flops | bytes accessed | tf_op | source)
XLA Modules:
  0.0 34.5 jit_solution(4635035094340670344)
XLA Ops:
  0.0 0.5 %collective-permute-start = (f32[4,64,128]{2,1,0:T(8,128)}, f32[4,64,128]{2,1,0:T(8,128)S(1)}, u32[]{:S(2)}, u32[]{:S(2)}) collective-permute-start(f32[4,64,128]{2,1,0:T(8,128)} %refs_0_.1), channel_id=1, source_target_pairs={{0,1},{1,0},{2,3},{3,2},{4,5},{5,4},{6,7},{7,6},{8,9},{9,8},{10,11... | collective-permute-start | bytes 393224 | tf_op jit(solution)/shard_map/ppermute | solution.py:351
  0.5 1.2 %load.1 = (f32[4,64,128]{2,1,0:T(8,128)S(1)}, f32[2,2,128]{2,1,0:T(2,128)S(1)}, f32[2,2,128]{2,1,0:T(2,128)S(1)}, s32[1,64]{1,0:T(1,128)S(1)}, bf16[2,128,640]{2...) custom-call(f32[4,64,128]{2,1,0:T(8,128)} %refs_0_.1, ...), custom_call_target="tpu_custom_call" | custom-call | tf_op jit(solution)/shard_map/load/pallas_call | solution.py:358
  1.9 3.0 %collective-permute-start.3 = (bf16[512,128]{1,0:T(8,128)(2,1)S(1)}, bf16[512,128]{1,0:T(8,128)(2,1)S(1)}, u32[]{:S(2)}, u32[]{:S(2)}) collective-permute-start(bf16[512,128]{1,0:T(8,128)(2,1)S(1)} %get-tuple-element.31.refs_5_), channel_id=1, source_target_pairs={{0,4},{1,9},{2,6},{3,11},{4,0},{5,13},{6,2},{7,15},{8,12},{9,1},{1... | collective-permute-start | bytes 393224 | tf_op jit(solution)/shard_map/ppermute | solution.py:348
  4.9 1.5 %collective-permute-start.1 = (bf16[512,128]{1,0:T(8,128)(2,1)S(1)}, bf16[512,128]{1,0:T(8,128)(2,1)S(1)}, u32[]{:S(2)}, u32[]{:S(2)}) collective-permute-start(bf16[512,128]{1,0:T(8,128)(2,1)S(1)} %get-tuple-element.31.refs_5_), channel_id=1, source_target_pairs={{0,2},{1,13},{2,0},{3,15},{4,6},{5,9},{6,4},{7,11},{8,10},{9,5},{1... | collective-permute-start | bytes 393224 | tf_op jit(solution)/shard_map/ppermute | solution.py:348
  6.4 2.5 %collective-permute-done.3.refs_1_ = bf16[512,128]{1,0:T(8,128)(2,1)S(1)} collective-permute-done((bf16[512,128]{1,0:T(8,128)(2,1)S(1)}, bf16[512,128]{1,0:T(8,128)(2,1)S(1)}, u32[]{:S(2)}, u32[]{:S(2)}) %collective-permute-start.3) | collective-permute-done | bytes 131104 | tf_op jit(solution)/shard_map/ppermute | solution.py:348
  9.0 2.1 %collective-permute-start.4 = (bf16[512,128]{1,0:T(8,128)(2,1)S(1)}, bf16[512,128]{1,0:T(8,128)(2,1)S(1)}, u32[]{:S(2)}, u32[]{:S(2)}) collective-permute-start(bf16[512,128]{1,0:T(8,128)(2,1)S(1)} %collective-permute-done.3.refs_1_), channel_id=1, source_target_pairs={{0,4},{1,3},{2,6},{3,1},{4,0},{5,7},{6,2},{7,5},{8,12},{9,11},{10,... | collective-permute-start | bytes 393224 | tf_op jit(solution)/shard_map/ppermute | solution.py:348
  11.1 0.9 %outgoing_edges.2 = (bf16[2,512,128]{2,1,0:T(8,128)(2,1)S(1)}, f32[2,8,8,128]{3,2,1,0:T(8,128)S(1)}, f32[512,128]{1,0:T(8,128)S(1)}, f32[512,128]{1,0:T(8,128)S(1)}) custom-call(s32[1]{0:T(128)} %bitcast.at_ref, bf16[512,128]{1,0:T(8,128)(2,1)S(1)} %collective-permute-done.1.refs_0_, bf16[512,128]{1,0:T(8,128)(2,1)S(1)} %collective-permute-done.3.refs_1_, ...), custom_call_target="tpu_custom_call" | custom-call | tf_op jit(solution)/shard_map/outgoing_edges/pallas_call | solution.py:315
  12.0 2.3 %collective-permute-start.6 = (bf16[2,512,128]{2,1,0:T(8,128)(2,1)S(1)}, bf16[2,512,128]{2,1,0:T(8,128)(2,1)S(1)}, u32[]{:S(2)}, u32[]{:S(2)}) collective-permute-start(bf16[2,512,128]{2,1,0:T(8,128)(2,1)S(1)} %get-tuple-element.39), channel_id=1, source_target_pairs={{0,1},{1,0},{2,3},{3,2},{4,5},{5,4},{6,7},{7,6},{8,9},{9,8},{10,11... | collective-permute-start | bytes 786440 | tf_op jit(solution)/shard_map/ppermute | solution.py:351
  14.3 0.4 %outgoing_edges.3 = (bf16[1,512,128]{2,1,0:T(8,128)(2,1)S(1)}, f32[1,8,8,128]{3,2,1,0:T(8,128)S(1)}) custom-call(s32[1]{0:T(128)} %bitcast.at_ref, bf16[512,128]{1,0:T(8,128)(2,1)S(1)} %collective-permute-done.4.refs_0_, s32[1,64]{1,0:T(1,128)S(1)} %get-tuple-element.32.refs_2_.refs_1_.mask_ref, ...), custom_call_target="tpu_custom_call" | custom-call | tf_op jit(solution)/shard_map/outgoing_edges/pallas_call | solution.py:315
  14.8 1.3 %collective-permute-done.2.normed_ref = bf16[512,128]{1,0:T(8,128)(2,1)S(1)} collective-permute-done((bf16[512,128]{1,0:T(8,128)(2,1)S(1)}, bf16[512,128]{1,0:T(8,128)(2,1)S(1)}, u32[]{:S(2)}, u32[]{:S(2)}) %collective-permute-start.2) | collective-permute-done | bytes 131104 | tf_op jit(solution)/shard_map/ppermute | solution.py:348
  16.5 0.5 %outgoing.1.refs_2_ = f32[3,8,8,128]{3,2,1,0:T(8,128)S(1)} custom-call(f32[512,128]{1,0:T(8,128)S(1)} %get-tuple-element.35.refs_4_.left_ref.refs_3_, bf16[2,512,128]{2,1,0:T(8,128)(2,1)S(1)} %collective-permute-done.6.piece_ref, bf16[2,512,128]{2,1,0:T(8,128)(2,1)S(1)} %outgoing_last.1.last_ref), custom_call_target="tpu_custom_call" | custom-call | tf_op jit(solution)/shard_map/outgoing/pallas_call | solution.py:315
  17.0 0.9 %collective-permute-done.5.piece_ref = bf16[2,512,128]{2,1,0:T(8,128)(2,1)S(1)} collective-permute-done((bf16[2,512,128]{2,1,0:T(8,128)(2,1)S(1)}, bf16[2,512,128]{2,1,0:T(8,128)(2,1)S(1)}, u32[]{:S(2)}, u32[]{:S(2)}) %collective-permute-start.5) | collective-permute-done | bytes 262176 | tf_op jit(solution)/shard_map/ppermute | solution.py:351
  17.9 0.9 %outgoing_finish.1 = (f32[8,64,128]{2,1,0:T(8,128)S(1)}, bf16[512,128]{1,0:T(8,128)(2,1)S(1)}) custom-call(s32[1]{0:T(128)} %bitcast.at_ref, bf16[2,512,128]{2,1,0:T(8,128)(2,1)S(1)} %collective-permute-done.5.piece_ref, f32[2,8,8,128]{3,2,1,0:T(8,128)S(1)} %get-tuple-element.37.refs_0_, f32[1,8,8,128]{3,2,1,0:T(8,128)S(1)} %get-tuple-element.38.refs_1_, ...), custom_call_target="tpu_custom_call" | custom-call | tf_op jit(solution)/shard_map/outgoing_finish/pallas_call | solution.py:315
  18.8 1.5 %collective-permute-start.7 = (bf16[512,128]{1,0:T(8,128)(2,1)S(1)}, bf16[512,128]{1,0:T(8,128)(2,1)S(1)}, u32[]{:S(2)}, u32[]{:S(2)}) collective-permute-start(bf16[512,128]{1,0:T(8,128)(2,1)S(1)} %get-tuple-element.44.refs_5_), channel_id=1, source_target_pairs={{0,4},{1,9},{2,6},{3,11},{4,0},{5,13},{6,2},{7,15},{8,12},{9,1},{1... | collective-permute-start | bytes 393224 | tf_op jit(solution)/shard_map/ppermute | solution.py:348
  20.3 1.5 %collective-permute-start.9 = (bf16[512,128]{1,0:T(8,128)(2,1)S(1)}, bf16[512,128]{1,0:T(8,128)(2,1)S(1)}, u32[]{:S(2)}, u32[]{:S(2)}) collective-permute-start(bf16[512,128]{1,0:T(8,128)(2,1)S(1)} %get-tuple-element.44.refs_5_), channel_id=1, source_target_pairs={{0,2},{1,13},{2,0},{3,15},{4,6},{5,9},{6,4},{7,11},{8,10},{9,5},{1... | collective-permute-start | bytes 393224 | tf_op jit(solution)/shard_map/ppermute | solution.py:348
  21.8 3.3 %collective-permute-done.7.refs_1_ = bf16[512,128]{1,0:T(8,128)(2,1)S(1)} collective-permute-done((bf16[512,128]{1,0:T(8,128)(2,1)S(1)}, bf16[512,128]{1,0:T(8,128)(2,1)S(1)}, u32[]{:S(2)}, u32[]{:S(2)}) %collective-permute-start.7) | collective-permute-done | bytes 131104 | tf_op jit(solution)/shard_map/ppermute | solution.py:348
  25.1 1.2 %collective-permute-start.8 = (bf16[512,128]{1,0:T(8,128)(2,1)S(1)}, bf16[512,128]{1,0:T(8,128)(2,1)S(1)}, u32[]{:S(2)}, u32[]{:S(2)}) collective-permute-start(bf16[512,128]{1,0:T(8,128)(2,1)S(1)} %collective-permute-done.7.refs_1_), channel_id=1, source_target_pairs={{0,4},{1,3},{2,6},{3,1},{4,0},{5,7},{6,2},{7,5},{8,12},{9,11},{10,... | collective-permute-start | bytes 393224 | tf_op jit(solution)/shard_map/ppermute | solution.py:348
  26.3 0.8 %collective-permute-start.11 = (bf16[512,128]{1,0:T(8,128)(2,1)S(1)}, bf16[512,128]{1,0:T(8,128)(2,1)S(1)}, u32[]{:S(2)}, u32[]{:S(2)}) collective-permute-start(bf16[512,128]{1,0:T(8,128)(2,1)S(1)} %collective-permute-done.9.refs_0_), channel_id=1, source_target_pairs={{0,4},{1,3},{2,6},{3,1},{4,0},{5,7},{6,2},{7,5},{8,12},{9,11},{10,... | collective-permute-start | bytes 393224 | tf_op jit(solution)/shard_map/ppermute | solution.py:348
  27.1 0.6 %incoming_edges.2 = (bf16[2,576,128]{2,1,0:T(8,128)(2,1)S(1)}, f32[4,64,128]{2,1,0:T(8,128)S(1)}, f32[256,128]{1,0:T(8,128)S(1)}) custom-call(s32[1]{0:T(128)} %bitcast.at_ref, bf16[512,128]{1,0:T(8,128)(2,1)S(1)} %collective-permute-done.9.refs_0_, bf16[512,128]{1,0:T(8,128)(2,1)S(1)} %collective-permute-done.7.refs_1_, ...), custom_call_target="tpu_custom_call" | custom-call | tf_op jit(solution)/shard_map/incoming_edges/pallas_call | solution.py:315
  27.7 1.8 %collective-permute-start.10 = (bf16[2,576,128]{2,1,0:T(8,128)(2,1)S(1)}, bf16[2,576,128]{2,1,0:T(8,128)(2,1)S(1)}, u32[]{:S(2)}, u32[]{:S(2)}) collective-permute-start(bf16[2,576,128]{2,1,0:T(8,128)(2,1)S(1)} %get-tuple-element.47), channel_id=1, source_target_pairs={{0,1},{1,0},{2,3},{3,2},{4,5},{5,4},{6,7},{7,6},{8,9},{9,8},{10,11... | collective-permute-start | bytes 884744 | tf_op jit(solution)/shard_map/ppermute | solution.py:351
  29.6 0.5 %collective-permute-done.8.refs_0_ = bf16[512,128]{1,0:T(8,128)(2,1)S(1)} collective-permute-done((bf16[512,128]{1,0:T(8,128)(2,1)S(1)}, bf16[512,128]{1,0:T(8,128)(2,1)S(1)}, u32[]{:S(2)}, u32[]{:S(2)}) %collective-permute-start.8) | collective-permute-done | bytes 131104 | tf_op jit(solution)/shard_map/ppermute | solution.py:348
  30.4 1.0 %collective-permute-done.11.normed_ref = bf16[512,128]{1,0:T(8,128)(2,1)S(1)} collective-permute-done((bf16[512,128]{1,0:T(8,128)(2,1)S(1)}, bf16[512,128]{1,0:T(8,128)(2,1)S(1)}, u32[]{:S(2)}, u32[]{:S(2)}) %collective-permute-start.11) | collective-permute-done | bytes 131104 | tf_op jit(solution)/shard_map/ppermute | solution.py:348
  32.2 1.2 %collective-permute-done.12.piece_ref = bf16[2,576,128]{2,1,0:T(8,128)(2,1)S(1)} collective-permute-done((bf16[2,576,128]{2,1,0:T(8,128)(2,1)S(1)}, bf16[2,576,128]{2,1,0:T(8,128)(2,1)S(1)}, u32[]{:S(2)}, u32[]{:S(2)}) %collective-permute-start.12) | collective-permute-done | bytes 294944 | tf_op jit(solution)/shard_map/ppermute | solution.py:351
  33.4 1.1 %incoming_finish.1 = f32[4,64,128]{2,1,0:T(8,128)} custom-call(s32[1]{0:T(128)} %bitcast.at_ref, f32[4,64,128]{2,1,0:T(8,128)S(1)} %incoming.1.before_ref, bf16[2,576,128]{2,1,0:T(8,128)(2,1)S(1)} %collective-permute-done.12.piece_ref, f32[8,64,128]{2,1,0:T(8,128)S(1)} %get-tuple-element.49.first_ref, f32[256,128]{1,0:T(8,128)S(1)} %get-tuple-element.50.gate_ref, ...), custom_call_target="tpu_custom_call" | custom-call | tf_op jit(solution)/shard_map/incoming_finish/pallas_call | solution.py:315
  (14 shorter events, 1.8 us)
Async XLA Ops:
  0.0 1.6 %collective-permute-start = (f32[4,64,128]{2,1,0:T(8,128)}, f32[4,64,128]{2,1,0:T(8,128)S(1)}, u32[]{:S(2)}, u32[]{:S(2)}) collective-permute-start(f32[4,64,128]{2,1,0:T(8,128)} %refs_0_.1), channel_id=1, source_target_pairs={{0,1},{1,0},{2,3},{3,2},{4,5},{5,4},{6,7},{7,6},{8,9},{9,8},{10,11... | collective-permute-start | bytes 393224 | tf_op jit(solution)/shard_map/ppermute | solution.py:351
  1.9 7.1 %collective-permute-start.3 = (bf16[512,128]{1,0:T(8,128)(2,1)S(1)}, bf16[512,128]{1,0:T(8,128)(2,1)S(1)}, u32[]{:S(2)}, u32[]{:S(2)}) collective-permute-start(bf16[512,128]{1,0:T(8,128)(2,1)S(1)} %get-tuple-element.31.refs_5_), channel_id=1, source_target_pairs={{0,4},{1,9},{2,6},{3,11},{4,0},{5,13},{6,2},{7,15},{8,12},{9,1},{1... | collective-permute-start | bytes 393224 | tf_op jit(solution)/shard_map/ppermute | solution.py:348
  4.9 6.2 %collective-permute-start.1 = (bf16[512,128]{1,0:T(8,128)(2,1)S(1)}, bf16[512,128]{1,0:T(8,128)(2,1)S(1)}, u32[]{:S(2)}, u32[]{:S(2)}) collective-permute-start(bf16[512,128]{1,0:T(8,128)(2,1)S(1)} %get-tuple-element.31.refs_5_), channel_id=1, source_target_pairs={{0,2},{1,13},{2,0},{3,15},{4,6},{5,9},{6,4},{7,11},{8,10},{9,5},{1... | collective-permute-start | bytes 393224 | tf_op jit(solution)/shard_map/ppermute | solution.py:348
  9.0 5.3 %collective-permute-start.4 = (bf16[512,128]{1,0:T(8,128)(2,1)S(1)}, bf16[512,128]{1,0:T(8,128)(2,1)S(1)}, u32[]{:S(2)}, u32[]{:S(2)}) collective-permute-start(bf16[512,128]{1,0:T(8,128)(2,1)S(1)} %collective-permute-done.3.refs_1_), channel_id=1, source_target_pairs={{0,4},{1,3},{2,6},{3,1},{4,0},{5,7},{6,2},{7,5},{8,12},{9,11},{10,... | collective-permute-start | bytes 393224 | tf_op jit(solution)/shard_map/ppermute | solution.py:348
  11.1 5.0 %collective-permute-start.2 = (bf16[512,128]{1,0:T(8,128)(2,1)S(1)}, bf16[512,128]{1,0:T(8,128)(2,1)S(1)}, u32[]{:S(2)}, u32[]{:S(2)}) collective-permute-start(bf16[512,128]{1,0:T(8,128)(2,1)S(1)} %collective-permute-done.1.refs_0_), channel_id=1, source_target_pairs={{0,4},{1,3},{2,6},{3,1},{4,0},{5,7},{6,2},{7,5},{8,12},{9,11},{10,... | collective-permute-start | bytes 393224 | tf_op jit(solution)/shard_map/ppermute | solution.py:348
  12.0 4.5 %collective-permute-start.6 = (bf16[2,512,128]{2,1,0:T(8,128)(2,1)S(1)}, bf16[2,512,128]{2,1,0:T(8,128)(2,1)S(1)}, u32[]{:S(2)}, u32[]{:S(2)}) collective-permute-start(bf16[2,512,128]{2,1,0:T(8,128)(2,1)S(1)} %get-tuple-element.39), channel_id=1, source_target_pairs={{0,1},{1,0},{2,3},{3,2},{4,5},{5,4},{6,7},{7,6},{8,9},{9,8},{10,11... | collective-permute-start | bytes 786440 | tf_op jit(solution)/shard_map/ppermute | solution.py:351
  16.3 1.6 %collective-permute-start.5 = (bf16[2,512,128]{2,1,0:T(8,128)(2,1)S(1)}, bf16[2,512,128]{2,1,0:T(8,128)(2,1)S(1)}, u32[]{:S(2)}, u32[]{:S(2)}) collective-permute-start(bf16[2,512,128]{2,1,0:T(8,128)(2,1)S(1)} %outgoing_last.1.last_ref), channel_id=1, source_target_pairs={{0,1},{1,0},{2,3},{3,2},{4,5},{5,4},{6,7},{7,6},{8,9},{9,8},{10,11... | collective-permute-start | bytes 786440 | tf_op jit(solution)/shard_map/ppermute | solution.py:351
  18.8 6.3 %collective-permute-start.7 = (bf16[512,128]{1,0:T(8,128)(2,1)S(1)}, bf16[512,128]{1,0:T(8,128)(2,1)S(1)}, u32[]{:S(2)}, u32[]{:S(2)}) collective-permute-start(bf16[512,128]{1,0:T(8,128)(2,1)S(1)} %get-tuple-element.44.refs_5_), channel_id=1, source_target_pairs={{0,4},{1,9},{2,6},{3,11},{4,0},{5,13},{6,2},{7,15},{8,12},{9,1},{1... | collective-permute-start | bytes 393224 | tf_op jit(solution)/shard_map/ppermute | solution.py:348
  20.3 6.0 %collective-permute-start.9 = (bf16[512,128]{1,0:T(8,128)(2,1)S(1)}, bf16[512,128]{1,0:T(8,128)(2,1)S(1)}, u32[]{:S(2)}, u32[]{:S(2)}) collective-permute-start(bf16[512,128]{1,0:T(8,128)(2,1)S(1)} %get-tuple-element.44.refs_5_), channel_id=1, source_target_pairs={{0,2},{1,13},{2,0},{3,15},{4,6},{5,9},{6,4},{7,11},{8,10},{9,5},{1... | collective-permute-start | bytes 393224 | tf_op jit(solution)/shard_map/ppermute | solution.py:348
  25.1 5.0 %collective-permute-start.8 = (bf16[512,128]{1,0:T(8,128)(2,1)S(1)}, bf16[512,128]{1,0:T(8,128)(2,1)S(1)}, u32[]{:S(2)}, u32[]{:S(2)}) collective-permute-start(bf16[512,128]{1,0:T(8,128)(2,1)S(1)} %collective-permute-done.7.refs_1_), channel_id=1, source_target_pairs={{0,4},{1,3},{2,6},{3,1},{4,0},{5,7},{6,2},{7,5},{8,12},{9,11},{10,... | collective-permute-start | bytes 393224 | tf_op jit(solution)/shard_map/ppermute | solution.py:348
  26.3 5.2 %collective-permute-start.11 = (bf16[512,128]{1,0:T(8,128)(2,1)S(1)}, bf16[512,128]{1,0:T(8,128)(2,1)S(1)}, u32[]{:S(2)}, u32[]{:S(2)}) collective-permute-start(bf16[512,128]{1,0:T(8,128)(2,1)S(1)} %collective-permute-done.9.refs_0_), channel_id=1, source_target_pairs={{0,4},{1,3},{2,6},{3,1},{4,0},{5,7},{6,2},{7,5},{8,12},{9,11},{10,... | collective-permute-start | bytes 393224 | tf_op jit(solution)/shard_map/ppermute | solution.py:348
  27.7 4.2 %collective-permute-start.10 = (bf16[2,576,128]{2,1,0:T(8,128)(2,1)S(1)}, bf16[2,576,128]{2,1,0:T(8,128)(2,1)S(1)}, u32[]{:S(2)}, u32[]{:S(2)}) collective-permute-start(bf16[2,576,128]{2,1,0:T(8,128)(2,1)S(1)} %get-tuple-element.47), channel_id=1, source_target_pairs={{0,1},{1,0},{2,3},{3,2},{4,5},{5,4},{6,7},{7,6},{8,9},{9,8},{10,11... | collective-permute-start | bytes 884744 | tf_op jit(solution)/shard_map/ppermute | solution.py:351
  31.7 1.6 %collective-permute-start.12 = (bf16[2,576,128]{2,1,0:T(8,128)(2,1)S(1)}, bf16[2,576,128]{2,1,0:T(8,128)(2,1)S(1)}, u32[]{:S(2)}, u32[]{:S(2)}) collective-permute-start(bf16[2,576,128]{2,1,0:T(8,128)(2,1)S(1)} %incoming_last.1.last_ref), channel_id=1, source_target_pairs={{0,1},{1,0},{2,3},{3,2},{4,5},{5,4},{6,7},{7,6},{8,9},{9,8},{10,11... | collective-permute-start | bytes 884744 | tf_op jit(solution)/shard_map/ppermute | solution.py:351

commit v8 on v7

--- a/solution.py
+++ b/solution.py
@@ -158,21 +158,19 @@
 
 
 def outgoing_last_kernel(
-    last, side, at_ref, normed_ref, mask_ref, edge_w_ref, edge_bias_ref, before_ref, right_ref
+    last, side, at_ref, normed_ref, mask_ref, edge_w_ref, edge_bias_ref, right_ref
 ):
-    count = before_ref.shape[0]
     height = normed_ref.shape[0] // side
-    right_ref[:count] = before_ref[...]
     edges(
-        normed_ref, right_ref.at[count], chip_of(at_ref[0], last, True) * height, side,
+        normed_ref, right_ref.at[0], chip_of(at_ref[0], last, True) * height, side,
         mask_ref, edge_w_ref, edge_bias_ref, 0, 2,
     )
 
 
-def outgoing_kernel(left_ref, piece_ref, last_ref, part_ref):
+def outgoing_kernel(left_ref, *refs):
+    piece_refs, part_ref = refs[:-1], refs[-1]
     side = left_ref.shape[0] // part_ref.shape[1]
-    count = piece_ref.shape[0]
-    pieces = [piece_ref.at[n] for n in range(count)] + [last_ref.at[last_ref.shape[0] - 1]]
+    pieces = [ref.at[n] for ref in piece_refs for n in range(ref.shape[0])]
     for n, piece in enumerate(pieces):
         products(left_ref, piece, part_ref.at[n], side)
 
@@ -279,19 +277,18 @@
 
 
 def incoming_last_kernel(
-    last, side, at_ref, normed_ref, mask_ref, edge_w_ref, edge_bias_ref, before_ref, out_ref
+    last, side, at_ref, normed_ref, mask_ref, edge_w_ref, edge_bias_ref, out_ref
 ):
-    count = before_ref.shape[0]
-    out_ref[:count] = before_ref[...]
     form_incoming(
-        [last], at_ref[0], [normed_ref], [out_ref.at[count]],
+        [last], at_ref[0], [normed_ref], [out_ref.at[0]],
         mask_ref, edge_w_ref, edge_bias_ref, side,
     )
 
 
-def incoming_kernel(before_ref, piece_ref, last_ref, x_ref, left_scr):
-    pieces = [(piece_ref.at[n], 1) for n in range(piece_ref.shape[0])]
-    pieces.append((last_ref.at[last_ref.shape[0] - 1], 0))
+def incoming_kernel(before_ref, *refs):
+    *came, last_ref, x_ref, left_scr = refs
+    pieces = [(ref.at[n], 1) for ref in came for n in range(ref.shape[0])]
+    pieces.append((last_ref.at[0], 0))
     add_pieces(pieces, left_scr, x_ref, lambda i, at: before_ref[i, pl.ds(at, CHUNK), :])
 
 
@@ -310,7 +307,7 @@
     ).reshape(rows, side, width)
 
 
-def call(kernel, name, outs, *operands, scalar=None, scratch=()):
+def call(kernel, name, outs, *operands, scalar=None, scratch=(), work=0):
     given = operands if scalar is None else (scalar, *operands)
     return pl.pallas_call(
         kernel,
@@ -319,6 +316,7 @@
         out_shape=[jax.ShapeDtypeStruct(*out) for out in outs],
         scratch_shapes=[pltpu.VMEM(*one) for one in scratch],
         compiler_params=PARAMS,
+        cost_estimate=pl.CostEstimate(flops=work, bytes_accessed=work // 100, transcendentals=0),
         name=name,
     )(*given)
 
@@ -388,23 +386,23 @@
         )
         if rest:
             left, gate = rest
-            others.append(flip(right))
+        others.append(flip(right))
         parts.append(part)
     (right,) = call(
         functools.partial(outgoing_last_kernel, slots[last], side), "outgoing_last",
-        [((quarter, count, hidden), BF16)], pieces[last], *weights, right, scalar=me,
+        [((1, count, hidden), BF16)], pieces[last], *weights, scalar=me, work=10**10,
     )
     others.append(flip(right))
     (part,) = call(
-        outgoing_kernel, "outgoing", [((quarter + 1, *part_shape), F32)], left, others[0], right
+        outgoing_kernel, "outgoing", [((half, *part_shape), F32)], left, *others[:2], right
     )
     known = [[(slots[n], True) for n in group] for group in groups]
-    known.append([(slots[n], False) for n in groups[0]] + [(slots[last], True)])
-    came = [slots[n] for n in [*groups[1], last]]
+    known.append([(slots[n], False) for n in groups[0] + groups[1]] + [(slots[last], True)])
+    came = [slots[last]]
     first, normed = call(
         functools.partial(outgoing_finish_kernel, came, known), "outgoing_finish",
         [((height, side, width), F32), ((count, width), BF16)],
-        others[1], *parts, part, left, gate, both, *norms, out_w, out_bias,
+        others[2], *parts, part, left, gate, both, *norms, out_w, out_bias,
         scalar=me, scratch=[((height, side, hidden), F32), ((len(came), *part_shape), F32)],
     )
 
@@ -422,21 +420,21 @@
         )
         if not x:
             gate = made.pop()
-            others.append(flip(edge))
+        others.append(flip(edge))
         x = made
     (edge,) = call(
         functools.partial(incoming_last_kernel, slots[last], side), "incoming_last",
-        [((quarter, span, hidden), BF16)], pieces[last], *weights, edge, scalar=me,
+        [((1, span, hidden), BF16)], pieces[last], *weights, scalar=me, work=10**10,
     )
     others.append(flip(edge))
     x = call(
-        incoming_kernel, "incoming", [(x_shape, F32)], *x, others[0], edge,
-        scratch=[((quarter + 1, height * height, hidden), F32)],
+        incoming_kernel, "incoming", [(x_shape, F32)], *x, *others[:2], edge,
+        scratch=[((half, height * height, hidden), F32)],
     )
     (out,) = call(
         incoming_finish_kernel, "incoming_finish", [((rows, side, width), F32)],
-        *x, others[1], first, gate, *norms, out_w, out_bias, scalar=me,
-        scratch=[((quarter, height * height, hidden), F32), (x_shape, F32)],
+        *x, others[2], first, gate, *norms, out_w, out_bias, scalar=me,
+        scratch=[((1, height * height, hidden), F32), (x_shape, F32)],
     )
     return out
 

time: 34.6 us -> 34 us (0.983)
  waiting for transfers between devices: 10.8 us -> 9.98 us
    ppermute x5 -> x7, waiting for transfers between devices: 2.13 us -> 1.49 us  [flip(): lax.ppermute(value, 'dap', [(device, device ^ 1) for device in range(dap)])]
    ppermute x5 -> x7, starting transfers between devices: 4.91 us -> 5.09 us  [flip(): lax.ppermute(value, 'dap', [(device, device ^ 1) for device in range(dap)])]
  transfers between devices with their start and end apart: 13 -> 15, of which waited for: 7 -> 7; matrix products, arithmetic and copies ran while one was open for 0% -> 0% of each run, Pallas kernels for 14% -> 15%
where the time goes in v8:
time: 34 us; the launch traced here: 33.8 us
  starting transfers between devices  16.8 us (49%)
  waiting for transfers between devices  9.98 us (29%)
  Pallas kernels  7 us (21%)
    ppermute x8, starting transfers between devices, swap(): return lax.ppermute(piece, 'dap', pairs)  11.7 us
    ppermute x8, waiting for transfers between devices, swap(): return lax.ppermute(piece, 'dap', pairs)  8.49 us
    pallas_call x11, Pallas kernels, call(): pl.pallas_call(kernel, in_specs=[SMEM] * (scalar is not None) + [VMEM] *...  5.84 us
    ppermute x7, starting transfers between devices, flip(): lax.ppermute(value, 'dap', [(device, device ^ 1) for device in range(dap)])  5.09 us
    ppermute x7, waiting for transfers between devices, flip(): lax.ppermute(value, 'dap', [(device, device ^ 1) for device in range(dap)])  1.49 us
    pallas_call x1, Pallas kernels, body(): pl.pallas_call(load_kernel, in_specs=[pl.BlockSpec(memory_space=pltpu.HBM...  1.17 us
  transfers between devices with their start and end apart: 15, of which 7 were waited for; matrix products, arithmetic and copies ran while one was open for 0% of the time, Pallas kernels for 15%

profile of v8, /device:TPU:0, one launch (start us, length us, event | category | flops | bytes accessed | tf_op | source)
XLA Modules:
  0.0 33.8 jit_solution(4241591204849487065)
XLA Ops:
  0.0 0.5 %collective-permute-start = (f32[4,64,128]{2,1,0:T(8,128)}, f32[4,64,128]{2,1,0:T(8,128)S(1)}, u32[]{:S(2)}, u32[]{:S(2)}) collective-permute-start(f32[4,64,128]{2,1,0:T(8,128)} %refs_0_.1), channel_id=1, source_target_pairs={{0,1},{1,0},{2,3},{3,2},{4,5},{5,4},{6,7},{7,6},{8,9},{9,8},{10,11... | collective-permute-start | bytes 393224 | tf_op jit(solution)/shard_map/ppermute | solution.py:349
  0.5 1.2 %load.1 = (f32[4,64,128]{2,1,0:T(8,128)S(1)}, f32[2,2,128]{2,1,0:T(2,128)S(1)}, f32[2,2,128]{2,1,0:T(2,128)S(1)}, s32[1,64]{1,0:T(1,128)S(1)}, bf16[2,128,640]{2...) custom-call(f32[4,64,128]{2,1,0:T(8,128)} %refs_0_.1, ...), custom_call_target="tpu_custom_call" | custom-call | tf_op jit(solution)/shard_map/load/pallas_call | solution.py:356
  1.9 3.0 %collective-permute-start.4 = (bf16[512,128]{1,0:T(8,128)(2,1)S(1)}, bf16[512,128]{1,0:T(8,128)(2,1)S(1)}, u32[]{:S(2)}, u32[]{:S(2)}) collective-permute-start(bf16[512,128]{1,0:T(8,128)(2,1)S(1)} %get-tuple-element.31.refs_5_), channel_id=1, source_target_pairs={{0,4},{1,9},{2,6},{3,11},{4,0},{5,13},{6,2},{7,15},{8,12},{9,1},{1... | collective-permute-start | bytes 393224 | tf_op jit(solution)/shard_map/ppermute | solution.py:346
  4.9 1.5 %collective-permute-start.1 = (bf16[512,128]{1,0:T(8,128)(2,1)S(1)}, bf16[512,128]{1,0:T(8,128)(2,1)S(1)}, u32[]{:S(2)}, u32[]{:S(2)}) collective-permute-start(bf16[512,128]{1,0:T(8,128)(2,1)S(1)} %get-tuple-element.31.refs_5_), channel_id=1, source_target_pairs={{0,2},{1,13},{2,0},{3,15},{4,6},{5,9},{6,4},{7,11},{8,10},{9,5},{1... | collective-permute-start | bytes 393224 | tf_op jit(solution)/shard_map/ppermute | solution.py:346
  6.4 2.5 %collective-permute-done.4.refs_1_ = bf16[512,128]{1,0:T(8,128)(2,1)S(1)} collective-permute-done((bf16[512,128]{1,0:T(8,128)(2,1)S(1)}, bf16[512,128]{1,0:T(8,128)(2,1)S(1)}, u32[]{:S(2)}, u32[]{:S(2)}) %collective-permute-start.4) | collective-permute-done | bytes 131104 | tf_op jit(solution)/shard_map/ppermute | solution.py:346
  9.0 2.1 %collective-permute-start.5 = (bf16[512,128]{1,0:T(8,128)(2,1)S(1)}, bf16[512,128]{1,0:T(8,128)(2,1)S(1)}, u32[]{:S(2)}, u32[]{:S(2)}) collective-permute-start(bf16[512,128]{1,0:T(8,128)(2,1)S(1)} %collective-permute-done.4.refs_1_), channel_id=1, source_target_pairs={{0,4},{1,3},{2,6},{3,1},{4,0},{5,7},{6,2},{7,5},{8,12},{9,11},{10,... | collective-permute-start | bytes 393224 | tf_op jit(solution)/shard_map/ppermute | solution.py:346
  11.1 0.9 %outgoing_edges.2 = (bf16[2,512,128]{2,1,0:T(8,128)(2,1)S(1)}, f32[2,8,8,128]{3,2,1,0:T(8,128)S(1)}, f32[512,128]{1,0:T(8,128)S(1)}, f32[512,128]{1,0:T(8,128)S(1)}) custom-call(s32[1]{0:T(128)} %bitcast.at_ref, bf16[512,128]{1,0:T(8,128)(2,1)S(1)} %collective-permute-done.1.refs_0_, bf16[512,128]{1,0:T(8,128)(2,1)S(1)} %collective-permute-done.4.refs_1_, ...), custom_call_target="tpu_custom_call" | custom-call | tf_op jit(solution)/shard_map/outgoing_edges/pallas_call | solution.py:312
  12.0 2.3 %collective-permute-start.6 = (bf16[2,512,128]{2,1,0:T(8,128)(2,1)S(1)}, bf16[2,512,128]{2,1,0:T(8,128)(2,1)S(1)}, u32[]{:S(2)}, u32[]{:S(2)}) collective-permute-start(bf16[2,512,128]{2,1,0:T(8,128)(2,1)S(1)} %get-tuple-element.38), channel_id=1, source_target_pairs={{0,1},{1,0},{2,3},{3,2},{4,5},{5,4},{6,7},{7,6},{8,9},{9,8},{10,11... | collective-permute-start | bytes 786440 | tf_op jit(solution)/shard_map/ppermute | solution.py:349
  14.3 0.4 %outgoing_edges.3 = (bf16[1,512,128]{2,1,0:T(8,128)(2,1)S(1)}, f32[1,8,8,128]{3,2,1,0:T(8,128)S(1)}) custom-call(s32[1]{0:T(128)} %bitcast.at_ref, bf16[512,128]{1,0:T(8,128)(2,1)S(1)} %collective-permute-done.5.refs_0_, s32[1,64]{1,0:T(1,128)S(1)} %get-tuple-element.32.mask_ref.refs_2_.refs_1_, ...), custom_call_target="tpu_custom_call" | custom-call | tf_op jit(solution)/shard_map/outgoing_edges/pallas_call | solution.py:312
  14.9 1.2 %collective-permute-done.2.normed_ref = bf16[512,128]{1,0:T(8,128)(2,1)S(1)} collective-permute-done((bf16[512,128]{1,0:T(8,128)(2,1)S(1)}, bf16[512,128]{1,0:T(8,128)(2,1)S(1)}, u32[]{:S(2)}, u32[]{:S(2)}) %collective-permute-start.2) | collective-permute-done | bytes 131104 | tf_op jit(solution)/shard_map/ppermute | solution.py:346
  16.5 0.7 %outgoing.1.refs_2_ = f32[4,8,8,128]{3,2,1,0:T(8,128)S(1)} custom-call(f32[512,128]{1,0:T(8,128)S(1)} %get-tuple-element.36.refs_4_.left_ref.refs_3_, bf16[2,512,128]{2,1,0:T(8,128)(2,1)S(1)} %collective-permute-done.6.refs_0_, bf16[1,512,128]{2,1,0:T(8,128)(2,1)S(1)} %collective-permute-done.7.refs_1_, bf16[1,512,128]{2,1,0:T(8,128)(2,1)S(1)} %outgoing_last.1.refs_2_), custom_call_target="tpu_custom_call" | custom-call | tf_op jit(solution)/shard_map/outgoing/pallas_call | solution.py:312
  17.2 0.5 %collective-permute-done.3.piece_ref = bf16[1,512,128]{2,1,0:T(8,128)(2,1)S(1)} collective-permute-done((bf16[1,512,128]{2,1,0:T(8,128)(2,1)S(1)}, bf16[1,512,128]{2,1,0:T(8,128)(2,1)S(1)}, u32[]{:S(2)}, u32[]{:S(2)}) %collective-permute-start.3) | collective-permute-done | bytes 131104 | tf_op jit(solution)/shard_map/ppermute | solution.py:349
  17.7 0.7 %outgoing_finish.1 = (f32[8,64,128]{2,1,0:T(8,128)S(1)}, bf16[512,128]{1,0:T(8,128)(2,1)S(1)}) custom-call(s32[1]{0:T(128)} %bitcast.at_ref, bf16[1,512,128]{2,1,0:T(8,128)(2,1)S(1)} %collective-permute-done.3.piece_ref, f32[2,8,8,128]{3,2,1,0:T(8,128)S(1)} %get-tuple-element.35.refs_0_, f32[1,8,8,128]{3,2,1,0:T(8,128)S(1)} %get-tuple-element.37.refs_1_, ...), custom_call_target="tpu_custom_call" | custom-call | tf_op jit(solution)/shard_map/outgoing_finish/pallas_call | solution.py:312
  18.5 1.5 %collective-permute-start.8 = (bf16[512,128]{1,0:T(8,128)(2,1)S(1)}, bf16[512,128]{1,0:T(8,128)(2,1)S(1)}, u32[]{:S(2)}, u32[]{:S(2)}) collective-permute-start(bf16[512,128]{1,0:T(8,128)(2,1)S(1)} %get-tuple-element.44.refs_5_), channel_id=1, source_target_pairs={{0,4},{1,9},{2,6},{3,11},{4,0},{5,13},{6,2},{7,15},{8,12},{9,1},{1... | collective-permute-start | bytes 393224 | tf_op jit(solution)/shard_map/ppermute | solution.py:346
  19.9 1.5 %collective-permute-start.10 = (bf16[512,128]{1,0:T(8,128)(2,1)S(1)}, bf16[512,128]{1,0:T(8,128)(2,1)S(1)}, u32[]{:S(2)}, u32[]{:S(2)}) collective-permute-start(bf16[512,128]{1,0:T(8,128)(2,1)S(1)} %get-tuple-element.44.refs_5_), channel_id=1, source_target_pairs={{0,2},{1,13},{2,0},{3,15},{4,6},{5,9},{6,4},{7,11},{8,10},{9,5},{1... | collective-permute-start | bytes 393224 | tf_op jit(solution)/shard_map/ppermute | solution.py:346
  21.4 3.3 %collective-permute-done.8.refs_1_ = bf16[512,128]{1,0:T(8,128)(2,1)S(1)} collective-permute-done((bf16[512,128]{1,0:T(8,128)(2,1)S(1)}, bf16[512,128]{1,0:T(8,128)(2,1)S(1)}, u32[]{:S(2)}, u32[]{:S(2)}) %collective-permute-start.8) | collective-permute-done | bytes 131104 | tf_op jit(solution)/shard_map/ppermute | solution.py:346
  24.7 1.2 %collective-permute-start.9 = (bf16[512,128]{1,0:T(8,128)(2,1)S(1)}, bf16[512,128]{1,0:T(8,128)(2,1)S(1)}, u32[]{:S(2)}, u32[]{:S(2)}) collective-permute-start(bf16[512,128]{1,0:T(8,128)(2,1)S(1)} %collective-permute-done.8.refs_1_), channel_id=1, source_target_pairs={{0,4},{1,3},{2,6},{3,1},{4,0},{5,7},{6,2},{7,5},{8,12},{9,11},{10,... | collective-permute-start | bytes 393224 | tf_op jit(solution)/shard_map/ppermute | solution.py:346
  25.9 0.8 %collective-permute-start.13 = (bf16[512,128]{1,0:T(8,128)(2,1)S(1)}, bf16[512,128]{1,0:T(8,128)(2,1)S(1)}, u32[]{:S(2)}, u32[]{:S(2)}) collective-permute-start(bf16[512,128]{1,0:T(8,128)(2,1)S(1)} %collective-permute-done.10.refs_0_), channel_id=1, source_target_pairs={{0,4},{1,3},{2,6},{3,1},{4,0},{5,7},{6,2},{7,5},{8,12},{9,11},{10,... | collective-permute-start | bytes 393224 | tf_op jit(solution)/shard_map/ppermute | solution.py:346
  26.8 0.6 %incoming_edges.2 = (bf16[2,576,128]{2,1,0:T(8,128)(2,1)S(1)}, f32[4,64,128]{2,1,0:T(8,128)S(1)}, f32[256,128]{1,0:T(8,128)S(1)}) custom-call(s32[1]{0:T(128)} %bitcast.at_ref, bf16[512,128]{1,0:T(8,128)(2,1)S(1)} %collective-permute-done.10.refs_0_, bf16[512,128]{1,0:T(8,128)(2,1)S(1)} %collective-permute-done.8.refs_1_, ...), custom_call_target="tpu_custom_call" | custom-call | tf_op jit(solution)/shard_map/incoming_edges/pallas_call | solution.py:312
  27.4 1.8 %collective-permute-start.11 = (bf16[2,576,128]{2,1,0:T(8,128)(2,1)S(1)}, bf16[2,576,128]{2,1,0:T(8,128)(2,1)S(1)}, u32[]{:S(2)}, u32[]{:S(2)}) collective-permute-start(bf16[2,576,128]{2,1,0:T(8,128)(2,1)S(1)} %get-tuple-element.47), channel_id=1, source_target_pairs={{0,1},{1,0},{2,3},{3,2},{4,5},{5,4},{6,7},{7,6},{8,9},{9,8},{10,11... | collective-permute-start | bytes 884744 | tf_op jit(solution)/shard_map/ppermute | solution.py:349
  29.2 0.5 %collective-permute-done.9.refs_0_ = bf16[512,128]{1,0:T(8,128)(2,1)S(1)} collective-permute-done((bf16[512,128]{1,0:T(8,128)(2,1)S(1)}, bf16[512,128]{1,0:T(8,128)(2,1)S(1)}, u32[]{:S(2)}, u32[]{:S(2)}) %collective-permute-start.9) | collective-permute-done | bytes 131104 | tf_op jit(solution)/shard_map/ppermute | solution.py:346
  30.1 1.0 %collective-permute-done.13.normed_ref = bf16[512,128]{1,0:T(8,128)(2,1)S(1)} collective-permute-done((bf16[512,128]{1,0:T(8,128)(2,1)S(1)}, bf16[512,128]{1,0:T(8,128)(2,1)S(1)}, u32[]{:S(2)}, u32[]{:S(2)}) %collective-permute-start.13) | collective-permute-done | bytes 131104 | tf_op jit(solution)/shard_map/ppermute | solution.py:346
  31.9 0.9 %collective-permute-done.14.piece_ref = bf16[1,576,128]{2,1,0:T(8,128)(2,1)S(1)} collective-permute-done((bf16[1,576,128]{2,1,0:T(8,128)(2,1)S(1)}, bf16[1,576,128]{2,1,0:T(8,128)(2,1)S(1)}, u32[]{:S(2)}, u32[]{:S(2)}) %collective-permute-start.14) | collective-permute-done | bytes 147488 | tf_op jit(solution)/shard_map/ppermute | solution.py:349
  32.8 1.0 %incoming_finish.1 = f32[4,64,128]{2,1,0:T(8,128)} custom-call(s32[1]{0:T(128)} %bitcast.at_ref, f32[4,64,128]{2,1,0:T(8,128)S(1)} %incoming.1.before_ref, bf16[1,576,128]{2,1,0:T(8,128)(2,1)S(1)} %collective-permute-done.14.piece_ref, f32[8,64,128]{2,1,0:T(8,128)S(1)} %get-tuple-element.49.first_ref, f32[256,128]{1,0:T(8,128)S(1)} %get-tuple-element.50.gate_ref, ...), custom_call_target="tpu_custom_call" | custom-call | tf_op jit(solution)/shard_map/incoming_finish/pallas_call | solution.py:312
  (18 shorter events, 2.0 us)
Async XLA Ops:
  0.0 1.6 %collective-permute-start = (f32[4,64,128]{2,1,0:T(8,128)}, f32[4,64,128]{2,1,0:T(8,128)S(1)}, u32[]{:S(2)}, u32[]{:S(2)}) collective-permute-start(f32[4,64,128]{2,1,0:T(8,128)} %refs_0_.1), channel_id=1, source_target_pairs={{0,1},{1,0},{2,3},{3,2},{4,5},{5,4},{6,7},{7,6},{8,9},{9,8},{10,11... | collective-permute-start | bytes 393224 | tf_op jit(solution)/shard_map/ppermute | solution.py:349
  1.9 7.1 %collective-permute-start.4 = (bf16[512,128]{1,0:T(8,128)(2,1)S(1)}, bf16[512,128]{1,0:T(8,128)(2,1)S(1)}, u32[]{:S(2)}, u32[]{:S(2)}) collective-permute-start(bf16[512,128]{1,0:T(8,128)(2,1)S(1)} %get-tuple-element.31.refs_5_), channel_id=1, source_target_pairs={{0,4},{1,9},{2,6},{3,11},{4,0},{5,13},{6,2},{7,15},{8,12},{9,1},{1... | collective-permute-start | bytes 393224 | tf_op jit(solution)/shard_map/ppermute | solution.py:346
  4.9 6.2 %collective-permute-start.1 = (bf16[512,128]{1,0:T(8,128)(2,1)S(1)}, bf16[512,128]{1,0:T(8,128)(2,1)S(1)}, u32[]{:S(2)}, u32[]{:S(2)}) collective-permute-start(bf16[512,128]{1,0:T(8,128)(2,1)S(1)} %get-tuple-element.31.refs_5_), channel_id=1, source_target_pairs={{0,2},{1,13},{2,0},{3,15},{4,6},{5,9},{6,4},{7,11},{8,10},{9,5},{1... | collective-permute-start | bytes 393224 | tf_op jit(solution)/shard_map/ppermute | solution.py:346
  9.0 5.3 %collective-permute-start.5 = (bf16[512,128]{1,0:T(8,128)(2,1)S(1)}, bf16[512,128]{1,0:T(8,128)(2,1)S(1)}, u32[]{:S(2)}, u32[]{:S(2)}) collective-permute-start(bf16[512,128]{1,0:T(8,128)(2,1)S(1)} %collective-permute-done.4.refs_1_), channel_id=1, source_target_pairs={{0,4},{1,3},{2,6},{3,1},{4,0},{5,7},{6,2},{7,5},{8,12},{9,11},{10,... | collective-permute-start | bytes 393224 | tf_op jit(solution)/shard_map/ppermute | solution.py:346
  11.1 5.0 %collective-permute-start.2 = (bf16[512,128]{1,0:T(8,128)(2,1)S(1)}, bf16[512,128]{1,0:T(8,128)(2,1)S(1)}, u32[]{:S(2)}, u32[]{:S(2)}) collective-permute-start(bf16[512,128]{1,0:T(8,128)(2,1)S(1)} %collective-permute-done.1.refs_0_), channel_id=1, source_target_pairs={{0,4},{1,3},{2,6},{3,1},{4,0},{5,7},{6,2},{7,5},{8,12},{9,11},{10,... | collective-permute-start | bytes 393224 | tf_op jit(solution)/shard_map/ppermute | solution.py:346
  12.0 4.5 %collective-permute-start.6 = (bf16[2,512,128]{2,1,0:T(8,128)(2,1)S(1)}, bf16[2,512,128]{2,1,0:T(8,128)(2,1)S(1)}, u32[]{:S(2)}, u32[]{:S(2)}) collective-permute-start(bf16[2,512,128]{2,1,0:T(8,128)(2,1)S(1)} %get-tuple-element.38), channel_id=1, source_target_pairs={{0,1},{1,0},{2,3},{3,2},{4,5},{5,4},{6,7},{7,6},{8,9},{9,8},{10,11... | collective-permute-start | bytes 786440 | tf_op jit(solution)/shard_map/ppermute | solution.py:349
  14.8 1.7 %collective-permute-start.7 = (bf16[1,512,128]{2,1,0:T(8,128)(2,1)S(1)}, bf16[1,512,128]{2,1,0:T(8,128)(2,1)S(1)}, u32[]{:S(2)}, u32[]{:S(2)}) collective-permute-start(bf16[1,512,128]{2,1,0:T(8,128)(2,1)S(1)} %get-tuple-element.39), channel_id=1, source_target_pairs={{0,1},{1,0},{2,3},{3,2},{4,5},{5,4},{6,7},{7,6},{8,9},{9,8},{10,11... | collective-permute-start | bytes 393224 | tf_op jit(solution)/shard_map/ppermute | solution.py:349
  16.3 1.4 %collective-permute-start.3 = (bf16[1,512,128]{2,1,0:T(8,128)(2,1)S(1)}, bf16[1,512,128]{2,1,0:T(8,128)(2,1)S(1)}, u32[]{:S(2)}, u32[]{:S(2)}) collective-permute-start(bf16[1,512,128]{2,1,0:T(8,128)(2,1)S(1)} %outgoing_last.1.refs_2_), channel_id=1, source_target_pairs={{0,1},{1,0},{2,3},{3,2},{4,5},{5,4},{6,7},{7,6},{8,9},{9,8},{10,11... | collective-permute-start | bytes 393224 | tf_op jit(solution)/shard_map/ppermute | solution.py:349
  18.5 6.3 %collective-permute-start.8 = (bf16[512,128]{1,0:T(8,128)(2,1)S(1)}, bf16[512,128]{1,0:T(8,128)(2,1)S(1)}, u32[]{:S(2)}, u32[]{:S(2)}) collective-permute-start(bf16[512,128]{1,0:T(8,128)(2,1)S(1)} %get-tuple-element.44.refs_5_), channel_id=1, source_target_pairs={{0,4},{1,9},{2,6},{3,11},{4,0},{5,13},{6,2},{7,15},{8,12},{9,1},{1... | collective-permute-start | bytes 393224 | tf_op jit(solution)/shard_map/ppermute | solution.py:346
  19.9 6.0 %collective-permute-start.10 = (bf16[512,128]{1,0:T(8,128)(2,1)S(1)}, bf16[512,128]{1,0:T(8,128)(2,1)S(1)}, u32[]{:S(2)}, u32[]{:S(2)}) collective-permute-start(bf16[512,128]{1,0:T(8,128)(2,1)S(1)} %get-tuple-element.44.refs_5_), channel_id=1, source_target_pairs={{0,2},{1,13},{2,0},{3,15},{4,6},{5,9},{6,4},{7,11},{8,10},{9,5},{1... | collective-permute-start | bytes 393224 | tf_op jit(solution)/shard_map/ppermute | solution.py:346
  24.7 5.0 %collective-permute-start.9 = (bf16[512,128]{1,0:T(8,128)(2,1)S(1)}, bf16[512,128]{1,0:T(8,128)(2,1)S(1)}, u32[]{:S(2)}, u32[]{:S(2)}) collective-permute-start(bf16[512,128]{1,0:T(8,128)(2,1)S(1)} %collective-permute-done.8.refs_1_), channel_id=1, source_target_pairs={{0,4},{1,3},{2,6},{3,1},{4,0},{5,7},{6,2},{7,5},{8,12},{9,11},{10,... | collective-permute-start | bytes 393224 | tf_op jit(solution)/shard_map/ppermute | solution.py:346
  25.9 5.2 %collective-permute-start.13 = (bf16[512,128]{1,0:T(8,128)(2,1)S(1)}, bf16[512,128]{1,0:T(8,128)(2,1)S(1)}, u32[]{:S(2)}, u32[]{:S(2)}) collective-permute-start(bf16[512,128]{1,0:T(8,128)(2,1)S(1)} %collective-permute-done.10.refs_0_), channel_id=1, source_target_pairs={{0,4},{1,3},{2,6},{3,1},{4,0},{5,7},{6,2},{7,5},{8,12},{9,11},{10,... | collective-permute-start | bytes 393224 | tf_op jit(solution)/shard_map/ppermute | solution.py:346
  27.4 4.2 %collective-permute-start.11 = (bf16[2,576,128]{2,1,0:T(8,128)(2,1)S(1)}, bf16[2,576,128]{2,1,0:T(8,128)(2,1)S(1)}, u32[]{:S(2)}, u32[]{:S(2)}) collective-permute-start(bf16[2,576,128]{2,1,0:T(8,128)(2,1)S(1)} %get-tuple-element.47), channel_id=1, source_target_pairs={{0,1},{1,0},{2,3},{3,2},{4,5},{5,4},{6,7},{7,6},{8,9},{9,8},{10,11... | collective-permute-start | bytes 884744 | tf_op jit(solution)/shard_map/ppermute | solution.py:349
  30.1 1.5 %collective-permute-start.12 = (bf16[1,576,128]{2,1,0:T(8,128)(2,1)S(1)}, bf16[1,576,128]{2,1,0:T(8,128)(2,1)S(1)}, u32[]{:S(2)}, u32[]{:S(2)}) collective-permute-start(bf16[1,576,128]{2,1,0:T(8,128)(2,1)S(1)} %get-tuple-element.48), channel_id=1, source_target_pairs={{0,1},{1,0},{2,3},{3,2},{4,5},{5,4},{6,7},{7,6},{8,9},{9,8},{10,11... | collective-permute-start | bytes 442376 | tf_op jit(solution)/shard_map/ppermute | solution.py:349
  31.4 1.4 %collective-permute-start.14 = (bf16[1,576,128]{2,1,0:T(8,128)(2,1)S(1)}, bf16[1,576,128]{2,1,0:T(8,128)(2,1)S(1)}, u32[]{:S(2)}, u32[]{:S(2)}) collective-permute-start(bf16[1,576,128]{2,1,0:T(8,128)(2,1)S(1)} %incoming_last.1.refs_2_), channel_id=1, source_target_pairs={{0,1},{1,0},{2,3},{3,2},{4,5},{5,4},{6,7},{7,6},{8,9},{9,8},{10,11... | collective-permute-start | bytes 442376 | tf_op jit(solution)/shard_map/ppermute | solution.py:349

commit v9 on v8

--- a/solution.py
+++ b/solution.py
@@ -17,9 +17,10 @@
 
 
 def normalize(values, gain, shift):
-    mean = jnp.mean(values, axis=-1, keepdims=True)
+    scale = 1.0 / values.shape[-1]
+    mean = jnp.sum(values, axis=-1, keepdims=True) * scale
     centered = values - mean
-    spread = jnp.mean(centered * centered, axis=-1, keepdims=True)
+    spread = jnp.sum(centered * centered, axis=-1, keepdims=True) * scale
     return centered * lax.rsqrt(spread + 1e-05) * gain + shift
 
 
@@ -41,14 +42,16 @@
 
 def edges(normed_ref, out_ref, first_row, side, mask_ref, edge_w_ref, edge_bias_ref, layer, index):
     count, hidden = normed_ref.shape[0], out_ref.shape[1]
-    size = min(count, BLOCK)
+    size = min(count, max(BLOCK, side))
 
     def block(at):
         values = gated(
             normed_ref[pl.ds(at, size), :], edge_w_ref, edge_bias_ref, layer, index, hidden
         )
-        position = at + lax.broadcasted_iota(jnp.int32, values.shape, 0)
-        values = masked(values, first_row + position // side, position % side, mask_ref)
+        grid = (size // side, side, hidden)
+        row = lax.broadcasted_iota(jnp.int32, grid, 0).reshape(values.shape)
+        column = lax.broadcasted_iota(jnp.int32, grid, 1).reshape(values.shape)
+        values = masked(values, first_row + at // side + row, column, mask_ref)
         out_ref[pl.ds(at, size), :] = values.astype(BF16).astype(out_ref.dtype)
 
     if count == size:
@@ -77,25 +80,37 @@
 
 
 def load_kernel(*refs):
-    count = len(refs) // 2
-    given, kept, sems = refs[:count], refs[count : 2 * count], refs[2 * count]
+    count = len(refs) // 2 - 1
+    given, kept, (normed_ref, sems) = refs[:count], refs[count : 2 * count], refs[2 * count :]
     copies = [
         pltpu.make_async_copy(source, target, sems.at[n])
         for n, (source, target) in enumerate(zip(given, kept))
     ]
     for copy in copies:
         copy.start()
-    for copy in copies:
+    for copy in copies[:3]:
         copy.wait()
-
-
-def norm_kernel(at_ref, pair_ref, other_ref, gain_ref, shift_ref, both_ref, normed_ref):
-    rows = pair_ref.shape[0]
+    first_normed(*kept[:3], normed_ref)
+    for copy in copies[3:]:
+        copy.wait()
+
+
+def first_normed(pair_ref, gain_ref, shift_ref, normed_ref):
+    block = pair_ref[...].reshape(normed_ref.shape)
+    normed_ref[...] = normalize(block, gain_ref[0, 0:1, :], shift_ref[0, 0:1, :]).astype(BF16)
+
+
+def norm_kernel(
+    at_ref, pair_ref, own_ref, other_ref, gain_ref, shift_ref, both_ref, normed_ref
+):
+    rows, side, _ = pair_ref.shape
+    count = rows * side
     core = at_ref[0] & 1
     both_ref[pl.ds(core * rows, rows)] = pair_ref[...]
     both_ref[pl.ds((1 - core) * rows, rows)] = other_ref[...]
-    block = both_ref[...].reshape(normed_ref.shape)
-    normed_ref[...] = normalize(block, gain_ref[0, 0:1, :], shift_ref[0, 0:1, :]).astype(BF16)
+    normed_ref[pl.ds(pl.multiple_of(core * count, count), count), :] = own_ref[...]
+    part = normed_ref.at[pl.ds(pl.multiple_of((1 - core) * count, count), count)]
+    first_normed(other_ref, gain_ref, shift_ref, part)
 
 
 def merge(low, a, b, shift):
@@ -353,11 +368,12 @@
         return pieces + [swap(piece, (2, 1)) for piece in pieces]
 
     arguments = (pair, norm_gain, norm_bias, mask, edge_w, edge_bias, out_w, out_bias)
-    kept = pl.pallas_call(
+    *kept, normed = pl.pallas_call(
         load_kernel,
         in_specs=[pl.BlockSpec(memory_space=pltpu.HBM)] * len(arguments),
-        out_specs=[VMEM] * len(arguments),
-        out_shape=[jax.ShapeDtypeStruct(value.shape, value.dtype) for value in arguments],
+        out_specs=[VMEM] * (len(arguments) + 1),
+        out_shape=[jax.ShapeDtypeStruct(value.shape, value.dtype) for value in arguments]
+        + [jax.ShapeDtypeStruct((rows * side, width), BF16)],
         scratch_shapes=[pltpu.SemaphoreType.DMA((len(arguments),))],
         compiler_params=PARAMS,
         name="load",
@@ -371,7 +387,7 @@
 
     both, normed = call(
         norm_kernel, "norm", [((height, side, width), F32), ((count, width), BF16)],
-        pair, other, *norms, scalar=me,
+        pair, normed, other, *norms, scalar=me,
     )
     pieces = gather(normed)
     others, parts = [], []

time: 34 us -> 33.9 us (level)
  no operation moved by 1% of the time
where the time goes in v9:
time: 33.9 us; the launch traced here: 33.8 us
  starting transfers between devices  16.8 us (50%)
  waiting for transfers between devices  9.88 us (29%)
  Pallas kernels  7 us (21%)
    ppermute x8, starting transfers between devices, swap(): return lax.ppermute(piece, 'dap', pairs)  11.7 us
    ppermute x8, waiting for transfers between devices, swap(): return lax.ppermute(piece, 'dap', pairs)  8.42 us
    pallas_call x11, Pallas kernels, call(): pl.pallas_call(kernel, in_specs=[SMEM] * (scalar is not None) + [VMEM] *...  5.81 us
    ppermute x7, starting transfers between devices, flip(): lax.ppermute(value, 'dap', [(device, device ^ 1) for device in range(dap)])  5.12 us
    ppermute x7, waiting for transfers between devices, flip(): lax.ppermute(value, 'dap', [(device, device ^ 1) for device in range(dap)])  1.47 us
    pallas_call x1, Pallas kernels, body(): pl.pallas_call(load_kernel, in_specs=[pl.BlockSpec(memory_space=pltpu.HBM...  1.18 us
  transfers between devices with their start and end apart: 15, of which 7 were waited for; matrix products, arithmetic and copies ran while one was open for 0% of the time, Pallas kernels for 15%

profile of v9, /device:TPU:0, one launch (start us, length us, event | category | flops | bytes accessed | tf_op | source)
XLA Modules:
  0.0 33.8 jit_solution(8075039220947283522)
XLA Ops:
  0.0 0.5 %collective-permute-start = (f32[4,64,128]{2,1,0:T(8,128)}, f32[4,64,128]{2,1,0:T(8,128)S(1)}, u32[]{:S(2)}, u32[]{:S(2)}) collective-permute-start(f32[4,64,128]{2,1,0:T(8,128)} %refs_0_.1), channel_id=1, source_target_pairs={{0,1},{1,0},{2,3},{3,2},{4,5},{5,4},{6,7},{7,6},{8,9},{9,8},{10,11... | collective-permute-start | bytes 393224 | tf_op jit(solution)/shard_map/ppermute | solution.py:364
  0.5 1.2 %load.1 = (f32[4,64,128]{2,1,0:T(8,128)S(1)}, f32[2,2,128]{2,1,0:T(2,128)S(1)}, f32[2,2,128]{2,1,0:T(2,128)S(1)}, s32[1,64]{1,0:T(1,128)S(1)}, bf16[2,128,640]{2...) custom-call(f32[4,64,128]{2,1,0:T(8,128)} %refs_0_.1, ...), custom_call_target="tpu_custom_call" | custom-call | tf_op jit(solution)/shard_map/load/pallas_call | solution.py:371
  1.9 3.0 %collective-permute-start.4 = (bf16[512,128]{1,0:T(8,128)(2,1)S(1)}, bf16[512,128]{1,0:T(8,128)(2,1)S(1)}, u32[]{:S(2)}, u32[]{:S(2)}) collective-permute-start(bf16[512,128]{1,0:T(8,128)(2,1)S(1)} %get-tuple-element.33.refs_5_), channel_id=1, source_target_pairs={{0,4},{1,9},{2,6},{3,11},{4,0},{5,13},{6,2},{7,15},{8,12},{9,1},{1... | collective-permute-start | bytes 393224 | tf_op jit(solution)/shard_map/ppermute | solution.py:361
  4.9 1.5 %collective-permute-start.1 = (bf16[512,128]{1,0:T(8,128)(2,1)S(1)}, bf16[512,128]{1,0:T(8,128)(2,1)S(1)}, u32[]{:S(2)}, u32[]{:S(2)}) collective-permute-start(bf16[512,128]{1,0:T(8,128)(2,1)S(1)} %get-tuple-element.33.refs_5_), channel_id=1, source_target_pairs={{0,2},{1,13},{2,0},{3,15},{4,6},{5,9},{6,4},{7,11},{8,10},{9,5},{1... | collective-permute-start | bytes 393224 | tf_op jit(solution)/shard_map/ppermute | solution.py:361
  6.4 2.5 %collective-permute-done.4.refs_1_ = bf16[512,128]{1,0:T(8,128)(2,1)S(1)} collective-permute-done((bf16[512,128]{1,0:T(8,128)(2,1)S(1)}, bf16[512,128]{1,0:T(8,128)(2,1)S(1)}, u32[]{:S(2)}, u32[]{:S(2)}) %collective-permute-start.4) | collective-permute-done | bytes 131104 | tf_op jit(solution)/shard_map/ppermute | solution.py:361
  8.9 2.1 %collective-permute-start.5 = (bf16[512,128]{1,0:T(8,128)(2,1)S(1)}, bf16[512,128]{1,0:T(8,128)(2,1)S(1)}, u32[]{:S(2)}, u32[]{:S(2)}) collective-permute-start(bf16[512,128]{1,0:T(8,128)(2,1)S(1)} %collective-permute-done.4.refs_1_), channel_id=1, source_target_pairs={{0,4},{1,3},{2,6},{3,1},{4,0},{5,7},{6,2},{7,5},{8,12},{9,11},{10,... | collective-permute-start | bytes 393224 | tf_op jit(solution)/shard_map/ppermute | solution.py:361
  11.1 0.9 %outgoing_edges.2 = (bf16[2,512,128]{2,1,0:T(8,128)(2,1)S(1)}, f32[2,8,8,128]{3,2,1,0:T(8,128)S(1)}, f32[512,128]{1,0:T(8,128)S(1)}, f32[512,128]{1,0:T(8,128)S(1)}) custom-call(s32[1]{0:T(128)} %bitcast.at_ref, bf16[512,128]{1,0:T(8,128)(2,1)S(1)} %collective-permute-done.1.refs_0_, bf16[512,128]{1,0:T(8,128)(2,1)S(1)} %collective-permute-done.4.refs_1_, ...), custom_call_target="tpu_custom_call" | custom-call | tf_op jit(solution)/shard_map/outgoing_edges/pallas_call | solution.py:327
  12.0 2.3 %collective-permute-start.6 = (bf16[2,512,128]{2,1,0:T(8,128)(2,1)S(1)}, bf16[2,512,128]{2,1,0:T(8,128)(2,1)S(1)}, u32[]{:S(2)}, u32[]{:S(2)}) collective-permute-start(bf16[2,512,128]{2,1,0:T(8,128)(2,1)S(1)} %get-tuple-element.40), channel_id=1, source_target_pairs={{0,1},{1,0},{2,3},{3,2},{4,5},{5,4},{6,7},{7,6},{8,9},{9,8},{10,11... | collective-permute-start | bytes 786440 | tf_op jit(solution)/shard_map/ppermute | solution.py:364
  14.3 0.4 %outgoing_edges.3 = (bf16[1,512,128]{2,1,0:T(8,128)(2,1)S(1)}, f32[1,8,8,128]{3,2,1,0:T(8,128)S(1)}) custom-call(s32[1]{0:T(128)} %bitcast.at_ref, bf16[512,128]{1,0:T(8,128)(2,1)S(1)} %collective-permute-done.5.refs_0_, s32[1,64]{1,0:T(1,128)S(1)} %get-tuple-element.34.mask_ref.refs_2_.refs_1_, ...), custom_call_target="tpu_custom_call" | custom-call | tf_op jit(solution)/shard_map/outgoing_edges/pallas_call | solution.py:327
  14.8 1.2 %collective-permute-done.2.normed_ref = bf16[512,128]{1,0:T(8,128)(2,1)S(1)} collective-permute-done((bf16[512,128]{1,0:T(8,128)(2,1)S(1)}, bf16[512,128]{1,0:T(8,128)(2,1)S(1)}, u32[]{:S(2)}, u32[]{:S(2)}) %collective-permute-start.2) | collective-permute-done | bytes 131104 | tf_op jit(solution)/shard_map/ppermute | solution.py:361
  16.4 0.7 %outgoing.1.refs_2_ = f32[4,8,8,128]{3,2,1,0:T(8,128)S(1)} custom-call(f32[512,128]{1,0:T(8,128)S(1)} %get-tuple-element.38.refs_4_.left_ref.refs_3_, bf16[2,512,128]{2,1,0:T(8,128)(2,1)S(1)} %collective-permute-done.6.refs_0_, bf16[1,512,128]{2,1,0:T(8,128)(2,1)S(1)} %collective-permute-done.7.refs_1_, bf16[1,512,128]{2,1,0:T(8,128)(2,1)S(1)} %outgoing_last.1.refs_2_), custom_call_target="tpu_custom_call" | custom-call | tf_op jit(solution)/shard_map/outgoing/pallas_call | solution.py:327
  17.1 0.5 %collective-permute-done.3.piece_ref = bf16[1,512,128]{2,1,0:T(8,128)(2,1)S(1)} collective-permute-done((bf16[1,512,128]{2,1,0:T(8,128)(2,1)S(1)}, bf16[1,512,128]{2,1,0:T(8,128)(2,1)S(1)}, u32[]{:S(2)}, u32[]{:S(2)}) %collective-permute-start.3) | collective-permute-done | bytes 131104 | tf_op jit(solution)/shard_map/ppermute | solution.py:364
  17.7 0.7 %outgoing_finish.1 = (f32[8,64,128]{2,1,0:T(8,128)S(1)}, bf16[512,128]{1,0:T(8,128)(2,1)S(1)}) custom-call(s32[1]{0:T(128)} %bitcast.at_ref, bf16[1,512,128]{2,1,0:T(8,128)(2,1)S(1)} %collective-permute-done.3.piece_ref, f32[2,8,8,128]{3,2,1,0:T(8,128)S(1)} %get-tuple-element.37.refs_0_, f32[1,8,8,128]{3,2,1,0:T(8,128)S(1)} %get-tuple-element.39.refs_1_, ...), custom_call_target="tpu_custom_call" | custom-call | tf_op jit(solution)/shard_map/outgoing_finish/pallas_call | solution.py:327
  18.4 1.5 %collective-permute-start.8 = (bf16[512,128]{1,0:T(8,128)(2,1)S(1)}, bf16[512,128]{1,0:T(8,128)(2,1)S(1)}, u32[]{:S(2)}, u32[]{:S(2)}) collective-permute-start(bf16[512,128]{1,0:T(8,128)(2,1)S(1)} %get-tuple-element.46.refs_5_), channel_id=1, source_target_pairs={{0,4},{1,9},{2,6},{3,11},{4,0},{5,13},{6,2},{7,15},{8,12},{9,1},{1... | collective-permute-start | bytes 393224 | tf_op jit(solution)/shard_map/ppermute | solution.py:361
  19.9 1.5 %collective-permute-start.10 = (bf16[512,128]{1,0:T(8,128)(2,1)S(1)}, bf16[512,128]{1,0:T(8,128)(2,1)S(1)}, u32[]{:S(2)}, u32[]{:S(2)}) collective-permute-start(bf16[512,128]{1,0:T(8,128)(2,1)S(1)} %get-tuple-element.46.refs_5_), channel_id=1, source_target_pairs={{0,2},{1,13},{2,0},{3,15},{4,6},{5,9},{6,4},{7,11},{8,10},{9,5},{1... | collective-permute-start | bytes 393224 | tf_op jit(solution)/shard_map/ppermute | solution.py:361
  21.4 3.3 %collective-permute-done.8.refs_1_ = bf16[512,128]{1,0:T(8,128)(2,1)S(1)} collective-permute-done((bf16[512,128]{1,0:T(8,128)(2,1)S(1)}, bf16[512,128]{1,0:T(8,128)(2,1)S(1)}, u32[]{:S(2)}, u32[]{:S(2)}) %collective-permute-start.8) | collective-permute-done | bytes 131104 | tf_op jit(solution)/shard_map/ppermute | solution.py:361
  24.6 1.2 %collective-permute-start.9 = (bf16[512,128]{1,0:T(8,128)(2,1)S(1)}, bf16[512,128]{1,0:T(8,128)(2,1)S(1)}, u32[]{:S(2)}, u32[]{:S(2)}) collective-permute-start(bf16[512,128]{1,0:T(8,128)(2,1)S(1)} %collective-permute-done.8.refs_1_), channel_id=1, source_target_pairs={{0,4},{1,3},{2,6},{3,1},{4,0},{5,7},{6,2},{7,5},{8,12},{9,11},{10,... | collective-permute-start | bytes 393224 | tf_op jit(solution)/shard_map/ppermute | solution.py:361
  25.9 0.8 %collective-permute-start.13 = (bf16[512,128]{1,0:T(8,128)(2,1)S(1)}, bf16[512,128]{1,0:T(8,128)(2,1)S(1)}, u32[]{:S(2)}, u32[]{:S(2)}) collective-permute-start(bf16[512,128]{1,0:T(8,128)(2,1)S(1)} %collective-permute-done.10.refs_0_), channel_id=1, source_target_pairs={{0,4},{1,3},{2,6},{3,1},{4,0},{5,7},{6,2},{7,5},{8,12},{9,11},{10,... | collective-permute-start | bytes 393224 | tf_op jit(solution)/shard_map/ppermute | solution.py:361
  26.7 0.6 %incoming_edges.2 = (bf16[2,576,128]{2,1,0:T(8,128)(2,1)S(1)}, f32[4,64,128]{2,1,0:T(8,128)S(1)}, f32[256,128]{1,0:T(8,128)S(1)}) custom-call(s32[1]{0:T(128)} %bitcast.at_ref, bf16[512,128]{1,0:T(8,128)(2,1)S(1)} %collective-permute-done.10.refs_0_, bf16[512,128]{1,0:T(8,128)(2,1)S(1)} %collective-permute-done.8.refs_1_, ...), custom_call_target="tpu_custom_call" | custom-call | tf_op jit(solution)/shard_map/incoming_edges/pallas_call | solution.py:327
  27.3 1.9 %collective-permute-start.11 = (bf16[2,576,128]{2,1,0:T(8,128)(2,1)S(1)}, bf16[2,576,128]{2,1,0:T(8,128)(2,1)S(1)}, u32[]{:S(2)}, u32[]{:S(2)}) collective-permute-start(bf16[2,576,128]{2,1,0:T(8,128)(2,1)S(1)} %get-tuple-element.49), channel_id=1, source_target_pairs={{0,1},{1,0},{2,3},{3,2},{4,5},{5,4},{6,7},{7,6},{8,9},{9,8},{10,11... | collective-permute-start | bytes 884744 | tf_op jit(solution)/shard_map/ppermute | solution.py:364
  29.2 0.4 %collective-permute-done.9.refs_0_ = bf16[512,128]{1,0:T(8,128)(2,1)S(1)} collective-permute-done((bf16[512,128]{1,0:T(8,128)(2,1)S(1)}, bf16[512,128]{1,0:T(8,128)(2,1)S(1)}, u32[]{:S(2)}, u32[]{:S(2)}) %collective-permute-start.9) | collective-permute-done | bytes 131104 | tf_op jit(solution)/shard_map/ppermute | solution.py:361
  30.0 1.0 %collective-permute-done.13.normed_ref = bf16[512,128]{1,0:T(8,128)(2,1)S(1)} collective-permute-done((bf16[512,128]{1,0:T(8,128)(2,1)S(1)}, bf16[512,128]{1,0:T(8,128)(2,1)S(1)}, u32[]{:S(2)}, u32[]{:S(2)}) %collective-permute-start.13) | collective-permute-done | bytes 131104 | tf_op jit(solution)/shard_map/ppermute | solution.py:361
  31.8 0.9 %collective-permute-done.14.piece_ref = bf16[1,576,128]{2,1,0:T(8,128)(2,1)S(1)} collective-permute-done((bf16[1,576,128]{2,1,0:T(8,128)(2,1)S(1)}, bf16[1,576,128]{2,1,0:T(8,128)(2,1)S(1)}, u32[]{:S(2)}, u32[]{:S(2)}) %collective-permute-start.14) | collective-permute-done | bytes 147488 | tf_op jit(solution)/shard_map/ppermute | solution.py:364
  32.7 1.0 %incoming_finish.1 = f32[4,64,128]{2,1,0:T(8,128)} custom-call(s32[1]{0:T(128)} %bitcast.at_ref, f32[4,64,128]{2,1,0:T(8,128)S(1)} %incoming.1.before_ref, bf16[1,576,128]{2,1,0:T(8,128)(2,1)S(1)} %collective-permute-done.14.piece_ref, f32[8,64,128]{2,1,0:T(8,128)S(1)} %get-tuple-element.51.first_ref, f32[256,128]{1,0:T(8,128)S(1)} %get-tuple-element.52.gate_ref, ...), custom_call_target="tpu_custom_call" | custom-call | tf_op jit(solution)/shard_map/incoming_finish/pallas_call | solution.py:327
  (18 shorter events, 2.0 us)
Async XLA Ops:
  0.0 1.6 %collective-permute-start = (f32[4,64,128]{2,1,0:T(8,128)}, f32[4,64,128]{2,1,0:T(8,128)S(1)}, u32[]{:S(2)}, u32[]{:S(2)}) collective-permute-start(f32[4,64,128]{2,1,0:T(8,128)} %refs_0_.1), channel_id=1, source_target_pairs={{0,1},{1,0},{2,3},{3,2},{4,5},{5,4},{6,7},{7,6},{8,9},{9,8},{10,11... | collective-permute-start | bytes 393224 | tf_op jit(solution)/shard_map/ppermute | solution.py:364
  1.9 7.1 %collective-permute-start.4 = (bf16[512,128]{1,0:T(8,128)(2,1)S(1)}, bf16[512,128]{1,0:T(8,128)(2,1)S(1)}, u32[]{:S(2)}, u32[]{:S(2)}) collective-permute-start(bf16[512,128]{1,0:T(8,128)(2,1)S(1)} %get-tuple-element.33.refs_5_), channel_id=1, source_target_pairs={{0,4},{1,9},{2,6},{3,11},{4,0},{5,13},{6,2},{7,15},{8,12},{9,1},{1... | collective-permute-start | bytes 393224 | tf_op jit(solution)/shard_map/ppermute | solution.py:361
  4.9 6.2 %collective-permute-start.1 = (bf16[512,128]{1,0:T(8,128)(2,1)S(1)}, bf16[512,128]{1,0:T(8,128)(2,1)S(1)}, u32[]{:S(2)}, u32[]{:S(2)}) collective-permute-start(bf16[512,128]{1,0:T(8,128)(2,1)S(1)} %get-tuple-element.33.refs_5_), channel_id=1, source_target_pairs={{0,2},{1,13},{2,0},{3,15},{4,6},{5,9},{6,4},{7,11},{8,10},{9,5},{1... | collective-permute-start | bytes 393224 | tf_op jit(solution)/shard_map/ppermute | solution.py:361
  8.9 5.3 %collective-permute-start.5 = (bf16[512,128]{1,0:T(8,128)(2,1)S(1)}, bf16[512,128]{1,0:T(8,128)(2,1)S(1)}, u32[]{:S(2)}, u32[]{:S(2)}) collective-permute-start(bf16[512,128]{1,0:T(8,128)(2,1)S(1)} %collective-permute-done.4.refs_1_), channel_id=1, source_target_pairs={{0,4},{1,3},{2,6},{3,1},{4,0},{5,7},{6,2},{7,5},{8,12},{9,11},{10,... | collective-permute-start | bytes 393224 | tf_op jit(solution)/shard_map/ppermute | solution.py:361
  11.0 5.0 %collective-permute-start.2 = (bf16[512,128]{1,0:T(8,128)(2,1)S(1)}, bf16[512,128]{1,0:T(8,128)(2,1)S(1)}, u32[]{:S(2)}, u32[]{:S(2)}) collective-permute-start(bf16[512,128]{1,0:T(8,128)(2,1)S(1)} %collective-permute-done.1.refs_0_), channel_id=1, source_target_pairs={{0,4},{1,3},{2,6},{3,1},{4,0},{5,7},{6,2},{7,5},{8,12},{9,11},{10,... | collective-permute-start | bytes 393224 | tf_op jit(solution)/shard_map/ppermute | solution.py:361
  12.0 4.4 %collective-permute-start.6 = (bf16[2,512,128]{2,1,0:T(8,128)(2,1)S(1)}, bf16[2,512,128]{2,1,0:T(8,128)(2,1)S(1)}, u32[]{:S(2)}, u32[]{:S(2)}) collective-permute-start(bf16[2,512,128]{2,1,0:T(8,128)(2,1)S(1)} %get-tuple-element.40), channel_id=1, source_target_pairs={{0,1},{1,0},{2,3},{3,2},{4,5},{5,4},{6,7},{7,6},{8,9},{9,8},{10,11... | collective-permute-start | bytes 786440 | tf_op jit(solution)/shard_map/ppermute | solution.py:364
  14.7 1.7 %collective-permute-start.7 = (bf16[1,512,128]{2,1,0:T(8,128)(2,1)S(1)}, bf16[1,512,128]{2,1,0:T(8,128)(2,1)S(1)}, u32[]{:S(2)}, u32[]{:S(2)}) collective-permute-start(bf16[1,512,128]{2,1,0:T(8,128)(2,1)S(1)} %get-tuple-element.41), channel_id=1, source_target_pairs={{0,1},{1,0},{2,3},{3,2},{4,5},{5,4},{6,7},{7,6},{8,9},{9,8},{10,11... | collective-permute-start | bytes 393224 | tf_op jit(solution)/shard_map/ppermute | solution.py:364
  16.2 1.4 %collective-permute-start.3 = (bf16[1,512,128]{2,1,0:T(8,128)(2,1)S(1)}, bf16[1,512,128]{2,1,0:T(8,128)(2,1)S(1)}, u32[]{:S(2)}, u32[]{:S(2)}) collective-permute-start(bf16[1,512,128]{2,1,0:T(8,128)(2,1)S(1)} %outgoing_last.1.refs_2_), channel_id=1, source_target_pairs={{0,1},{1,0},{2,3},{3,2},{4,5},{5,4},{6,7},{7,6},{8,9},{9,8},{10,11... | collective-permute-start | bytes 393224 | tf_op jit(solution)/shard_map/ppermute | solution.py:364
  18.4 6.3 %collective-permute-start.8 = (bf16[512,128]{1,0:T(8,128)(2,1)S(1)}, bf16[512,128]{1,0:T(8,128)(2,1)S(1)}, u32[]{:S(2)}, u32[]{:S(2)}) collective-permute-start(bf16[512,128]{1,0:T(8,128)(2,1)S(1)} %get-tuple-element.46.refs_5_), channel_id=1, source_target_pairs={{0,4},{1,9},{2,6},{3,11},{4,0},{5,13},{6,2},{7,15},{8,12},{9,1},{1... | collective-permute-start | bytes 393224 | tf_op jit(solution)/shard_map/ppermute | solution.py:361
  19.9 6.0 %collective-permute-start.10 = (bf16[512,128]{1,0:T(8,128)(2,1)S(1)}, bf16[512,128]{1,0:T(8,128)(2,1)S(1)}, u32[]{:S(2)}, u32[]{:S(2)}) collective-permute-start(bf16[512,128]{1,0:T(8,128)(2,1)S(1)} %get-tuple-element.46.refs_5_), channel_id=1, source_target_pairs={{0,2},{1,13},{2,0},{3,15},{4,6},{5,9},{6,4},{7,11},{8,10},{9,5},{1... | collective-permute-start | bytes 393224 | tf_op jit(solution)/shard_map/ppermute | solution.py:361
  24.6 5.0 %collective-permute-start.9 = (bf16[512,128]{1,0:T(8,128)(2,1)S(1)}, bf16[512,128]{1,0:T(8,128)(2,1)S(1)}, u32[]{:S(2)}, u32[]{:S(2)}) collective-permute-start(bf16[512,128]{1,0:T(8,128)(2,1)S(1)} %collective-permute-done.8.refs_1_), channel_id=1, source_target_pairs={{0,4},{1,3},{2,6},{3,1},{4,0},{5,7},{6,2},{7,5},{8,12},{9,11},{10,... | collective-permute-start | bytes 393224 | tf_op jit(solution)/shard_map/ppermute | solution.py:361
  25.9 5.2 %collective-permute-start.13 = (bf16[512,128]{1,0:T(8,128)(2,1)S(1)}, bf16[512,128]{1,0:T(8,128)(2,1)S(1)}, u32[]{:S(2)}, u32[]{:S(2)}) collective-permute-start(bf16[512,128]{1,0:T(8,128)(2,1)S(1)} %collective-permute-done.10.refs_0_), channel_id=1, source_target_pairs={{0,4},{1,3},{2,6},{3,1},{4,0},{5,7},{6,2},{7,5},{8,12},{9,11},{10,... | collective-permute-start | bytes 393224 | tf_op jit(solution)/shard_map/ppermute | solution.py:361
  27.3 4.2 %collective-permute-start.11 = (bf16[2,576,128]{2,1,0:T(8,128)(2,1)S(1)}, bf16[2,576,128]{2,1,0:T(8,128)(2,1)S(1)}, u32[]{:S(2)}, u32[]{:S(2)}) collective-permute-start(bf16[2,576,128]{2,1,0:T(8,128)(2,1)S(1)} %get-tuple-element.49), channel_id=1, source_target_pairs={{0,1},{1,0},{2,3},{3,2},{4,5},{5,4},{6,7},{7,6},{8,9},{9,8},{10,11... | collective-permute-start | bytes 884744 | tf_op jit(solution)/shard_map/ppermute | solution.py:364
  30.0 1.5 %collective-permute-start.12 = (bf16[1,576,128]{2,1,0:T(8,128)(2,1)S(1)}, bf16[1,576,128]{2,1,0:T(8,128)(2,1)S(1)}, u32[]{:S(2)}, u32[]{:S(2)}) collective-permute-start(bf16[1,576,128]{2,1,0:T(8,128)(2,1)S(1)} %get-tuple-element.50), channel_id=1, source_target_pairs={{0,1},{1,0},{2,3},{3,2},{4,5},{5,4},{6,7},{7,6},{8,9},{9,8},{10,11... | collective-permute-start | bytes 442376 | tf_op jit(solution)/shard_map/ppermute | solution.py:364
  31.3 1.4 %collective-permute-start.14 = (bf16[1,576,128]{2,1,0:T(8,128)(2,1)S(1)}, bf16[1,576,128]{2,1,0:T(8,128)(2,1)S(1)}, u32[]{:S(2)}, u32[]{:S(2)}) collective-permute-start(bf16[1,576,128]{2,1,0:T(8,128)(2,1)S(1)} %incoming_last.1.refs_2_), channel_id=1, source_target_pairs={{0,1},{1,0},{2,3},{3,2},{4,5},{5,4},{6,7},{7,6},{8,9},{9,8},{10,11... | collective-permute-start | bytes 442376 | tf_op jit(solution)/shard_map/ppermute | solution.py:364

commit v10 on v9

--- a/solution.py
+++ b/solution.py
@@ -146,7 +146,7 @@
 def products(left_ref, piece_ref, part_ref, side):
     rows, height, hidden = part_ref.shape
     sub = lax.broadcasted_iota(jnp.int32, (height, hidden), 0)
-    some = 4
+    some = 8
     for first in range(0, rows, some):
         totals = [row_sums(left_ref, piece_ref, a, first, some, side) for a in range(height)]
         for i in range(some):

time: 33.9 us -> 33.9 us (level)
  no operation moved by 1% of the time
where the time goes in v10:
time: 33.9 us; the launch traced here: 33.8 us
  starting transfers between devices  16.8 us (50%)
  waiting for transfers between devices  9.91 us (29%)
  Pallas kernels  6.97 us (21%)
    ppermute x8, starting transfers between devices, swap(): return lax.ppermute(piece, 'dap', pairs)  11.7 us
    ppermute x8, waiting for transfers between devices, swap(): return lax.ppermute(piece, 'dap', pairs)  8.41 us
    pallas_call x11, Pallas kernels, call(): pl.pallas_call(kernel, in_specs=[SMEM] * (scalar is not None) + [VMEM] *...  5.78 us
    ppermute x7, starting transfers between devices, flip(): lax.ppermute(value, 'dap', [(device, device ^ 1) for device in range(dap)])  5.12 us
    ppermute x7, waiting for transfers between devices, flip(): lax.ppermute(value, 'dap', [(device, device ^ 1) for device in range(dap)])  1.5 us
    pallas_call x1, Pallas kernels, body(): pl.pallas_call(load_kernel, in_specs=[pl.BlockSpec(memory_space=pltpu.HBM...  1.18 us
  transfers between devices with their start and end apart: 15, of which 7 were waited for; matrix products, arithmetic and copies ran while one was open for 0% of the time, Pallas kernels for 15%

profile of v10, /device:TPU:0, one launch (start us, length us, event | category | flops | bytes accessed | tf_op | source)
XLA Modules:
  0.0 33.8 jit_solution(3313408783270647326)
XLA Ops:
  0.0 0.5 %collective-permute-start = (f32[4,64,128]{2,1,0:T(8,128)}, f32[4,64,128]{2,1,0:T(8,128)S(1)}, u32[]{:S(2)}, u32[]{:S(2)}) collective-permute-start(f32[4,64,128]{2,1,0:T(8,128)} %refs_0_.1), channel_id=1, source_target_pairs={{0,1},{1,0},{2,3},{3,2},{4,5},{5,4},{6,7},{7,6},{8,9},{9,8},{10,11... | collective-permute-start | bytes 393224 | tf_op jit(solution)/shard_map/ppermute | solution.py:364
  0.5 1.2 %load.1 = (f32[4,64,128]{2,1,0:T(8,128)S(1)}, f32[2,2,128]{2,1,0:T(2,128)S(1)}, f32[2,2,128]{2,1,0:T(2,128)S(1)}, s32[1,64]{1,0:T(1,128)S(1)}, bf16[2,128,640]{2...) custom-call(f32[4,64,128]{2,1,0:T(8,128)} %refs_0_.1, ...), custom_call_target="tpu_custom_call" | custom-call | tf_op jit(solution)/shard_map/load/pallas_call | solution.py:371
  1.9 3.0 %collective-permute-start.4 = (bf16[512,128]{1,0:T(8,128)(2,1)S(1)}, bf16[512,128]{1,0:T(8,128)(2,1)S(1)}, u32[]{:S(2)}, u32[]{:S(2)}) collective-permute-start(bf16[512,128]{1,0:T(8,128)(2,1)S(1)} %get-tuple-element.33.refs_5_), channel_id=1, source_target_pairs={{0,4},{1,9},{2,6},{3,11},{4,0},{5,13},{6,2},{7,15},{8,12},{9,1},{1... | collective-permute-start | bytes 393224 | tf_op jit(solution)/shard_map/ppermute | solution.py:361
  4.9 1.5 %collective-permute-start.1 = (bf16[512,128]{1,0:T(8,128)(2,1)S(1)}, bf16[512,128]{1,0:T(8,128)(2,1)S(1)}, u32[]{:S(2)}, u32[]{:S(2)}) collective-permute-start(bf16[512,128]{1,0:T(8,128)(2,1)S(1)} %get-tuple-element.33.refs_5_), channel_id=1, source_target_pairs={{0,2},{1,13},{2,0},{3,15},{4,6},{5,9},{6,4},{7,11},{8,10},{9,5},{1... | collective-permute-start | bytes 393224 | tf_op jit(solution)/shard_map/ppermute | solution.py:361
  6.4 2.5 %collective-permute-done.4.refs_1_ = bf16[512,128]{1,0:T(8,128)(2,1)S(1)} collective-permute-done((bf16[512,128]{1,0:T(8,128)(2,1)S(1)}, bf16[512,128]{1,0:T(8,128)(2,1)S(1)}, u32[]{:S(2)}, u32[]{:S(2)}) %collective-permute-start.4) | collective-permute-done | bytes 131104 | tf_op jit(solution)/shard_map/ppermute | solution.py:361
  8.9 2.1 %collective-permute-start.5 = (bf16[512,128]{1,0:T(8,128)(2,1)S(1)}, bf16[512,128]{1,0:T(8,128)(2,1)S(1)}, u32[]{:S(2)}, u32[]{:S(2)}) collective-permute-start(bf16[512,128]{1,0:T(8,128)(2,1)S(1)} %collective-permute-done.4.refs_1_), channel_id=1, source_target_pairs={{0,4},{1,3},{2,6},{3,1},{4,0},{5,7},{6,2},{7,5},{8,12},{9,11},{10,... | collective-permute-start | bytes 393224 | tf_op jit(solution)/shard_map/ppermute | solution.py:361
  11.1 0.9 %outgoing_edges.2 = (bf16[2,512,128]{2,1,0:T(8,128)(2,1)S(1)}, f32[2,8,8,128]{3,2,1,0:T(8,128)S(1)}, f32[512,128]{1,0:T(8,128)S(1)}, f32[512,128]{1,0:T(8,128)S(1)}) custom-call(s32[1]{0:T(128)} %bitcast.at_ref, bf16[512,128]{1,0:T(8,128)(2,1)S(1)} %collective-permute-done.1.refs_0_, bf16[512,128]{1,0:T(8,128)(2,1)S(1)} %collective-permute-done.4.refs_1_, ...), custom_call_target="tpu_custom_call" | custom-call | tf_op jit(solution)/shard_map/outgoing_edges/pallas_call | solution.py:327
  12.0 2.3 %collective-permute-start.6 = (bf16[2,512,128]{2,1,0:T(8,128)(2,1)S(1)}, bf16[2,512,128]{2,1,0:T(8,128)(2,1)S(1)}, u32[]{:S(2)}, u32[]{:S(2)}) collective-permute-start(bf16[2,512,128]{2,1,0:T(8,128)(2,1)S(1)} %get-tuple-element.40), channel_id=1, source_target_pairs={{0,1},{1,0},{2,3},{3,2},{4,5},{5,4},{6,7},{7,6},{8,9},{9,8},{10,11... | collective-permute-start | bytes 786440 | tf_op jit(solution)/shard_map/ppermute | solution.py:364
  14.3 0.4 %outgoing_edges.3 = (bf16[1,512,128]{2,1,0:T(8,128)(2,1)S(1)}, f32[1,8,8,128]{3,2,1,0:T(8,128)S(1)}) custom-call(s32[1]{0:T(128)} %bitcast.at_ref, bf16[512,128]{1,0:T(8,128)(2,1)S(1)} %collective-permute-done.5.refs_0_, s32[1,64]{1,0:T(1,128)S(1)} %get-tuple-element.34.mask_ref.refs_2_.refs_1_, ...), custom_call_target="tpu_custom_call" | custom-call | tf_op jit(solution)/shard_map/outgoing_edges/pallas_call | solution.py:327
  14.8 1.2 %collective-permute-done.2.normed_ref = bf16[512,128]{1,0:T(8,128)(2,1)S(1)} collective-permute-done((bf16[512,128]{1,0:T(8,128)(2,1)S(1)}, bf16[512,128]{1,0:T(8,128)(2,1)S(1)}, u32[]{:S(2)}, u32[]{:S(2)}) %collective-permute-start.2) | collective-permute-done | bytes 131104 | tf_op jit(solution)/shard_map/ppermute | solution.py:361
  16.4 0.7 %outgoing.1.refs_2_ = f32[4,8,8,128]{3,2,1,0:T(8,128)S(1)} custom-call(f32[512,128]{1,0:T(8,128)S(1)} %get-tuple-element.38.refs_4_.left_ref.refs_3_, bf16[2,512,128]{2,1,0:T(8,128)(2,1)S(1)} %collective-permute-done.6.refs_0_, bf16[1,512,128]{2,1,0:T(8,128)(2,1)S(1)} %collective-permute-done.7.refs_1_, bf16[1,512,128]{2,1,0:T(8,128)(2,1)S(1)} %outgoing_last.1.refs_2_), custom_call_target="tpu_custom_call" | custom-call | tf_op jit(solution)/shard_map/outgoing/pallas_call | solution.py:327
  17.1 0.6 %collective-permute-done.3.piece_ref = bf16[1,512,128]{2,1,0:T(8,128)(2,1)S(1)} collective-permute-done((bf16[1,512,128]{2,1,0:T(8,128)(2,1)S(1)}, bf16[1,512,128]{2,1,0:T(8,128)(2,1)S(1)}, u32[]{:S(2)}, u32[]{:S(2)}) %collective-permute-start.3) | collective-permute-done | bytes 131104 | tf_op jit(solution)/shard_map/ppermute | solution.py:364
  17.7 0.7 %outgoing_finish.1 = (f32[8,64,128]{2,1,0:T(8,128)S(1)}, bf16[512,128]{1,0:T(8,128)(2,1)S(1)}) custom-call(s32[1]{0:T(128)} %bitcast.at_ref, bf16[1,512,128]{2,1,0:T(8,128)(2,1)S(1)} %collective-permute-done.3.piece_ref, f32[2,8,8,128]{3,2,1,0:T(8,128)S(1)} %get-tuple-element.37.refs_0_, f32[1,8,8,128]{3,2,1,0:T(8,128)S(1)} %get-tuple-element.39.refs_1_, ...), custom_call_target="tpu_custom_call" | custom-call | tf_op jit(solution)/shard_map/outgoing_finish/pallas_call | solution.py:327
  18.4 1.5 %collective-permute-start.8 = (bf16[512,128]{1,0:T(8,128)(2,1)S(1)}, bf16[512,128]{1,0:T(8,128)(2,1)S(1)}, u32[]{:S(2)}, u32[]{:S(2)}) collective-permute-start(bf16[512,128]{1,0:T(8,128)(2,1)S(1)} %get-tuple-element.46.refs_5_), channel_id=1, source_target_pairs={{0,4},{1,9},{2,6},{3,11},{4,0},{5,13},{6,2},{7,15},{8,12},{9,1},{1... | collective-permute-start | bytes 393224 | tf_op jit(solution)/shard_map/ppermute | solution.py:361
  19.9 1.5 %collective-permute-start.10 = (bf16[512,128]{1,0:T(8,128)(2,1)S(1)}, bf16[512,128]{1,0:T(8,128)(2,1)S(1)}, u32[]{:S(2)}, u32[]{:S(2)}) collective-permute-start(bf16[512,128]{1,0:T(8,128)(2,1)S(1)} %get-tuple-element.46.refs_5_), channel_id=1, source_target_pairs={{0,2},{1,13},{2,0},{3,15},{4,6},{5,9},{6,4},{7,11},{8,10},{9,5},{1... | collective-permute-start | bytes 393224 | tf_op jit(solution)/shard_map/ppermute | solution.py:361
  21.4 3.3 %collective-permute-done.8.refs_1_ = bf16[512,128]{1,0:T(8,128)(2,1)S(1)} collective-permute-done((bf16[512,128]{1,0:T(8,128)(2,1)S(1)}, bf16[512,128]{1,0:T(8,128)(2,1)S(1)}, u32[]{:S(2)}, u32[]{:S(2)}) %collective-permute-start.8) | collective-permute-done | bytes 131104 | tf_op jit(solution)/shard_map/ppermute | solution.py:361
  24.6 1.2 %collective-permute-start.9 = (bf16[512,128]{1,0:T(8,128)(2,1)S(1)}, bf16[512,128]{1,0:T(8,128)(2,1)S(1)}, u32[]{:S(2)}, u32[]{:S(2)}) collective-permute-start(bf16[512,128]{1,0:T(8,128)(2,1)S(1)} %collective-permute-done.8.refs_1_), channel_id=1, source_target_pairs={{0,4},{1,3},{2,6},{3,1},{4,0},{5,7},{6,2},{7,5},{8,12},{9,11},{10,... | collective-permute-start | bytes 393224 | tf_op jit(solution)/shard_map/ppermute | solution.py:361
  25.8 0.8 %collective-permute-start.13 = (bf16[512,128]{1,0:T(8,128)(2,1)S(1)}, bf16[512,128]{1,0:T(8,128)(2,1)S(1)}, u32[]{:S(2)}, u32[]{:S(2)}) collective-permute-start(bf16[512,128]{1,0:T(8,128)(2,1)S(1)} %collective-permute-done.10.refs_0_), channel_id=1, source_target_pairs={{0,4},{1,3},{2,6},{3,1},{4,0},{5,7},{6,2},{7,5},{8,12},{9,11},{10,... | collective-permute-start | bytes 393224 | tf_op jit(solution)/shard_map/ppermute | solution.py:361
  26.7 0.6 %incoming_edges.2 = (bf16[2,576,128]{2,1,0:T(8,128)(2,1)S(1)}, f32[4,64,128]{2,1,0:T(8,128)S(1)}, f32[256,128]{1,0:T(8,128)S(1)}) custom-call(s32[1]{0:T(128)} %bitcast.at_ref, bf16[512,128]{1,0:T(8,128)(2,1)S(1)} %collective-permute-done.10.refs_0_, bf16[512,128]{1,0:T(8,128)(2,1)S(1)} %collective-permute-done.8.refs_1_, ...), custom_call_target="tpu_custom_call" | custom-call | tf_op jit(solution)/shard_map/incoming_edges/pallas_call | solution.py:327
  27.3 1.9 %collective-permute-start.11 = (bf16[2,576,128]{2,1,0:T(8,128)(2,1)S(1)}, bf16[2,576,128]{2,1,0:T(8,128)(2,1)S(1)}, u32[]{:S(2)}, u32[]{:S(2)}) collective-permute-start(bf16[2,576,128]{2,1,0:T(8,128)(2,1)S(1)} %get-tuple-element.49), channel_id=1, source_target_pairs={{0,1},{1,0},{2,3},{3,2},{4,5},{5,4},{6,7},{7,6},{8,9},{9,8},{10,11... | collective-permute-start | bytes 884744 | tf_op jit(solution)/shard_map/ppermute | solution.py:364
  29.2 0.4 %collective-permute-done.9.refs_0_ = bf16[512,128]{1,0:T(8,128)(2,1)S(1)} collective-permute-done((bf16[512,128]{1,0:T(8,128)(2,1)S(1)}, bf16[512,128]{1,0:T(8,128)(2,1)S(1)}, u32[]{:S(2)}, u32[]{:S(2)}) %collective-permute-start.9) | collective-permute-done | bytes 131104 | tf_op jit(solution)/shard_map/ppermute | solution.py:361
  30.0 1.0 %collective-permute-done.13.normed_ref = bf16[512,128]{1,0:T(8,128)(2,1)S(1)} collective-permute-done((bf16[512,128]{1,0:T(8,128)(2,1)S(1)}, bf16[512,128]{1,0:T(8,128)(2,1)S(1)}, u32[]{:S(2)}, u32[]{:S(2)}) %collective-permute-start.13) | collective-permute-done | bytes 131104 | tf_op jit(solution)/shard_map/ppermute | solution.py:361
  31.8 0.9 %collective-permute-done.14.piece_ref = bf16[1,576,128]{2,1,0:T(8,128)(2,1)S(1)} collective-permute-done((bf16[1,576,128]{2,1,0:T(8,128)(2,1)S(1)}, bf16[1,576,128]{2,1,0:T(8,128)(2,1)S(1)}, u32[]{:S(2)}, u32[]{:S(2)}) %collective-permute-start.14) | collective-permute-done | bytes 147488 | tf_op jit(solution)/shard_map/ppermute | solution.py:364
  32.7 1.0 %incoming_finish.1 = f32[4,64,128]{2,1,0:T(8,128)} custom-call(s32[1]{0:T(128)} %bitcast.at_ref, f32[4,64,128]{2,1,0:T(8,128)S(1)} %incoming.1.before_ref, bf16[1,576,128]{2,1,0:T(8,128)(2,1)S(1)} %collective-permute-done.14.piece_ref, f32[8,64,128]{2,1,0:T(8,128)S(1)} %get-tuple-element.51.first_ref, f32[256,128]{1,0:T(8,128)S(1)} %get-tuple-element.52.gate_ref, ...), custom_call_target="tpu_custom_call" | custom-call | tf_op jit(solution)/shard_map/incoming_finish/pallas_call | solution.py:327
  (18 shorter events, 2.0 us)
Async XLA Ops:
  0.0 1.6 %collective-permute-start = (f32[4,64,128]{2,1,0:T(8,128)}, f32[4,64,128]{2,1,0:T(8,128)S(1)}, u32[]{:S(2)}, u32[]{:S(2)}) collective-permute-start(f32[4,64,128]{2,1,0:T(8,128)} %refs_0_.1), channel_id=1, source_target_pairs={{0,1},{1,0},{2,3},{3,2},{4,5},{5,4},{6,7},{7,6},{8,9},{9,8},{10,11... | collective-permute-start | bytes 393224 | tf_op jit(solution)/shard_map/ppermute | solution.py:364
  1.9 7.1 %collective-permute-start.4 = (bf16[512,128]{1,0:T(8,128)(2,1)S(1)}, bf16[512,128]{1,0:T(8,128)(2,1)S(1)}, u32[]{:S(2)}, u32[]{:S(2)}) collective-permute-start(bf16[512,128]{1,0:T(8,128)(2,1)S(1)} %get-tuple-element.33.refs_5_), channel_id=1, source_target_pairs={{0,4},{1,9},{2,6},{3,11},{4,0},{5,13},{6,2},{7,15},{8,12},{9,1},{1... | collective-permute-start | bytes 393224 | tf_op jit(solution)/shard_map/ppermute | solution.py:361
  4.9 6.2 %collective-permute-start.1 = (bf16[512,128]{1,0:T(8,128)(2,1)S(1)}, bf16[512,128]{1,0:T(8,128)(2,1)S(1)}, u32[]{:S(2)}, u32[]{:S(2)}) collective-permute-start(bf16[512,128]{1,0:T(8,128)(2,1)S(1)} %get-tuple-element.33.refs_5_), channel_id=1, source_target_pairs={{0,2},{1,13},{2,0},{3,15},{4,6},{5,9},{6,4},{7,11},{8,10},{9,5},{1... | collective-permute-start | bytes 393224 | tf_op jit(solution)/shard_map/ppermute | solution.py:361
  8.9 5.3 %collective-permute-start.5 = (bf16[512,128]{1,0:T(8,128)(2,1)S(1)}, bf16[512,128]{1,0:T(8,128)(2,1)S(1)}, u32[]{:S(2)}, u32[]{:S(2)}) collective-permute-start(bf16[512,128]{1,0:T(8,128)(2,1)S(1)} %collective-permute-done.4.refs_1_), channel_id=1, source_target_pairs={{0,4},{1,3},{2,6},{3,1},{4,0},{5,7},{6,2},{7,5},{8,12},{9,11},{10,... | collective-permute-start | bytes 393224 | tf_op jit(solution)/shard_map/ppermute | solution.py:361
  11.0 5.0 %collective-permute-start.2 = (bf16[512,128]{1,0:T(8,128)(2,1)S(1)}, bf16[512,128]{1,0:T(8,128)(2,1)S(1)}, u32[]{:S(2)}, u32[]{:S(2)}) collective-permute-start(bf16[512,128]{1,0:T(8,128)(2,1)S(1)} %collective-permute-done.1.refs_0_), channel_id=1, source_target_pairs={{0,4},{1,3},{2,6},{3,1},{4,0},{5,7},{6,2},{7,5},{8,12},{9,11},{10,... | collective-permute-start | bytes 393224 | tf_op jit(solution)/shard_map/ppermute | solution.py:361
  12.0 4.4 %collective-permute-start.6 = (bf16[2,512,128]{2,1,0:T(8,128)(2,1)S(1)}, bf16[2,512,128]{2,1,0:T(8,128)(2,1)S(1)}, u32[]{:S(2)}, u32[]{:S(2)}) collective-permute-start(bf16[2,512,128]{2,1,0:T(8,128)(2,1)S(1)} %get-tuple-element.40), channel_id=1, source_target_pairs={{0,1},{1,0},{2,3},{3,2},{4,5},{5,4},{6,7},{7,6},{8,9},{9,8},{10,11... | collective-permute-start | bytes 786440 | tf_op jit(solution)/shard_map/ppermute | solution.py:364
  14.7 1.7 %collective-permute-start.7 = (bf16[1,512,128]{2,1,0:T(8,128)(2,1)S(1)}, bf16[1,512,128]{2,1,0:T(8,128)(2,1)S(1)}, u32[]{:S(2)}, u32[]{:S(2)}) collective-permute-start(bf16[1,512,128]{2,1,0:T(8,128)(2,1)S(1)} %get-tuple-element.41), channel_id=1, source_target_pairs={{0,1},{1,0},{2,3},{3,2},{4,5},{5,4},{6,7},{7,6},{8,9},{9,8},{10,11... | collective-permute-start | bytes 393224 | tf_op jit(solution)/shard_map/ppermute | solution.py:364
  16.2 1.4 %collective-permute-start.3 = (bf16[1,512,128]{2,1,0:T(8,128)(2,1)S(1)}, bf16[1,512,128]{2,1,0:T(8,128)(2,1)S(1)}, u32[]{:S(2)}, u32[]{:S(2)}) collective-permute-start(bf16[1,512,128]{2,1,0:T(8,128)(2,1)S(1)} %outgoing_last.1.refs_2_), channel_id=1, source_target_pairs={{0,1},{1,0},{2,3},{3,2},{4,5},{5,4},{6,7},{7,6},{8,9},{9,8},{10,11... | collective-permute-start | bytes 393224 | tf_op jit(solution)/shard_map/ppermute | solution.py:364
  18.4 6.3 %collective-permute-start.8 = (bf16[512,128]{1,0:T(8,128)(2,1)S(1)}, bf16[512,128]{1,0:T(8,128)(2,1)S(1)}, u32[]{:S(2)}, u32[]{:S(2)}) collective-permute-start(bf16[512,128]{1,0:T(8,128)(2,1)S(1)} %get-tuple-element.46.refs_5_), channel_id=1, source_target_pairs={{0,4},{1,9},{2,6},{3,11},{4,0},{5,13},{6,2},{7,15},{8,12},{9,1},{1... | collective-permute-start | bytes 393224 | tf_op jit(solution)/shard_map/ppermute | solution.py:361
  19.9 6.0 %collective-permute-start.10 = (bf16[512,128]{1,0:T(8,128)(2,1)S(1)}, bf16[512,128]{1,0:T(8,128)(2,1)S(1)}, u32[]{:S(2)}, u32[]{:S(2)}) collective-permute-start(bf16[512,128]{1,0:T(8,128)(2,1)S(1)} %get-tuple-element.46.refs_5_), channel_id=1, source_target_pairs={{0,2},{1,13},{2,0},{3,15},{4,6},{5,9},{6,4},{7,11},{8,10},{9,5},{1... | collective-permute-start | bytes 393224 | tf_op jit(solution)/shard_map/ppermute | solution.py:361
  24.6 5.0 %collective-permute-start.9 = (bf16[512,128]{1,0:T(8,128)(2,1)S(1)}, bf16[512,128]{1,0:T(8,128)(2,1)S(1)}, u32[]{:S(2)}, u32[]{:S(2)}) collective-permute-start(bf16[512,128]{1,0:T(8,128)(2,1)S(1)} %collective-permute-done.8.refs_1_), channel_id=1, source_target_pairs={{0,4},{1,3},{2,6},{3,1},{4,0},{5,7},{6,2},{7,5},{8,12},{9,11},{10,... | collective-permute-start | bytes 393224 | tf_op jit(solution)/shard_map/ppermute | solution.py:361
  25.8 5.2 %collective-permute-start.13 = (bf16[512,128]{1,0:T(8,128)(2,1)S(1)}, bf16[512,128]{1,0:T(8,128)(2,1)S(1)}, u32[]{:S(2)}, u32[]{:S(2)}) collective-permute-start(bf16[512,128]{1,0:T(8,128)(2,1)S(1)} %collective-permute-done.10.refs_0_), channel_id=1, source_target_pairs={{0,4},{1,3},{2,6},{3,1},{4,0},{5,7},{6,2},{7,5},{8,12},{9,11},{10,... | collective-permute-start | bytes 393224 | tf_op jit(solution)/shard_map/ppermute | solution.py:361
  27.3 4.2 %collective-permute-start.11 = (bf16[2,576,128]{2,1,0:T(8,128)(2,1)S(1)}, bf16[2,576,128]{2,1,0:T(8,128)(2,1)S(1)}, u32[]{:S(2)}, u32[]{:S(2)}) collective-permute-start(bf16[2,576,128]{2,1,0:T(8,128)(2,1)S(1)} %get-tuple-element.49), channel_id=1, source_target_pairs={{0,1},{1,0},{2,3},{3,2},{4,5},{5,4},{6,7},{7,6},{8,9},{9,8},{10,11... | collective-permute-start | bytes 884744 | tf_op jit(solution)/shard_map/ppermute | solution.py:364
  30.0 1.5 %collective-permute-start.12 = (bf16[1,576,128]{2,1,0:T(8,128)(2,1)S(1)}, bf16[1,576,128]{2,1,0:T(8,128)(2,1)S(1)}, u32[]{:S(2)}, u32[]{:S(2)}) collective-permute-start(bf16[1,576,128]{2,1,0:T(8,128)(2,1)S(1)} %get-tuple-element.50), channel_id=1, source_target_pairs={{0,1},{1,0},{2,3},{3,2},{4,5},{5,4},{6,7},{7,6},{8,9},{9,8},{10,11... | collective-permute-start | bytes 442376 | tf_op jit(solution)/shard_map/ppermute | solution.py:364
  31.3 1.4 %collective-permute-start.14 = (bf16[1,576,128]{2,1,0:T(8,128)(2,1)S(1)}, bf16[1,576,128]{2,1,0:T(8,128)(2,1)S(1)}, u32[]{:S(2)}, u32[]{:S(2)}) collective-permute-start(bf16[1,576,128]{2,1,0:T(8,128)(2,1)S(1)} %incoming_last.1.refs_2_), channel_id=1, source_target_pairs={{0,1},{1,0},{2,3},{3,2},{4,5},{5,4},{6,7},{7,6},{8,9},{9,8},{10,11... | collective-permute-start | bytes 442376 | tf_op jit(solution)/shard_map/ppermute | solution.py:364
